TPU v7x, 32 devices: a whole 2x2x4 slice. The times are simulated.
32 devices in a mesh: batch: 4 (over x, core), seq: 8 (over z, y).
Axes of the slice: x: 2, y: 2, z: 4, core: 2. Of those that a mesh axis runs over, the one named last changes fastest.
Arguments:
- tokens: bfloat16 [4, 1024, 1600], P('batch', 'seq'), may hold values from -6 to 6
- ln1_gain: bfloat16 [1600], P('seq'), may hold values from 0.25 to 1.75
- ln1_bias: bfloat16 [1600], P('seq'), may hold values from -3 to 3
- qkv_weight: bfloat16 [1600, 4800], P('seq'), may hold values from -0.15625 to 0.15625
- qv_bias: bfloat16 [3200], P('seq'), may hold values from -3 to 3
- proj_weight: bfloat16 [1600, 1600], P('seq'), may hold values from -0.625 to 0.625
- proj_bias: bfloat16 [1600], P('seq'), may hold values from -3 to 3
- ln2_gain: bfloat16 [1600], P('seq'), may hold values from 0.25 to 1.75
- ln2_bias: bfloat16 [1600], P('seq'), may hold values from -3 to 3
- fc_weight: bfloat16 [1600, 6400], P('seq'), may hold values from -0.15625 to 0.15625
- fc_bias: bfloat16 [6400], P('seq'), may hold values from -3 to 3
- out_weight: bfloat16 [6400, 1600], P('seq'), may hold values from -0.078125 to 0.078125
- out_bias: bfloat16 [1600], P('seq'), may hold values from -3 to 3
- cotangent: bfloat16 [4, 1024, 1600], P('batch', 'seq'), may hold values from -6 to 6
Outputs:
- out: bfloat16 [4, 1024, 1600], P('batch', 'seq')
- input_grad: bfloat16 [4, 1024, 1600], P('batch', 'seq')
- ln1_gain_grad: float32 [1600], P('seq')
- ln1_bias_grad: float32 [1600], P('seq')
- qkv_weight_grad: float32 [1600, 4800], P('seq', 'batch')
- qv_bias_grad: float32 [3200], P('seq')
- proj_weight_grad: float32 [1600, 1600], P('seq', 'batch')
- proj_bias_grad: float32 [1600], P('seq')
- ln2_gain_grad: float32 [1600], P('seq')
- ln2_bias_grad: float32 [1600], P('seq')
- fc_weight_grad: float32 [1600, 6400], P('seq', 'batch')
- fc_bias_grad: float32 [6400], P('seq')
- out_weight_grad: float32 [6400, 1600], P('seq', 'batch')
- out_bias_grad: float32 [1600], P('seq')
All inputs are finite; a program needn't handle non-finite values.
Results may differ from a plain program's by a relative error of at most 0.017.
Values may be sent and summed in bfloat16 or wider, within the bound.
No kernel may reach another device: no remote copies, remote signals or barrier semaphores. Data moves between devices by JAX's collectives and lax.ppermute only.
A program may use at most 384 MiB of HBM per device.

v0:
```python
import jax
import jax.numpy as jnp
from jax import lax
from jax.sharding import PartitionSpec as P

HEAD_DIM = 64


EPSILON = 1e-05
FLOOR_SCORE = -1e30


def norm_rows(inputs, gain_full, shift_full):
    mean_rows = jnp.mean(inputs, axis=-1, keepdims=True)
    centred = inputs - mean_rows
    variance = jnp.mean(centred * centred, axis=-1, keepdims=True)
    return centred * lax.rsqrt(variance + EPSILON) * gain_full + shift_full


def gelu_tanh(inputs):
    return jax.nn.gelu(inputs, approximate=True)


def fetch_attention(gain_one, shift_one, qkv_rows, bias_rows, proj_rows, proj_shift):
    return (
        lax.all_gather(gain_one, "seq", axis=0, tiled=True),
        lax.all_gather(shift_one, "seq", axis=0, tiled=True),
        lax.all_gather(qkv_rows, "seq", axis=0, tiled=True),
        lax.all_gather(bias_rows, "seq", axis=0, tiled=True),
        lax.all_gather(proj_rows, "seq", axis=0, tiled=True),
        lax.all_gather(proj_shift, "seq", axis=0, tiled=True),
    )


def fetch_mlp(gain_two, shift_two, fc_rows, fc_shift, out_rows, out_shift):
    return (
        lax.all_gather(gain_two, "seq", axis=0, tiled=True),
        lax.all_gather(shift_two, "seq", axis=0, tiled=True),
        lax.all_gather(fc_rows, "seq", axis=0, tiled=True),
        lax.all_gather(fc_shift, "seq", axis=0, tiled=True),
        lax.all_gather(out_rows, "seq", axis=0, tiled=True),
        lax.all_gather(out_shift, "seq", axis=0, tiled=True),
    )


def inner_left(left_side, right_side):
    return lax.dot_general(
        left_side, right_side, (((0,), (0,)), ((), ())), preferred_element_type=jnp.float32
    )


def inner_right(left_side, right_side):
    return lax.dot_general(
        left_side, right_side, (((1,), (1,)), ((), ())), preferred_element_type=jnp.float32
    )


def weight_grad(left_side, right_side):
    return lax.psum_scatter(
        inner_left(left_side, right_side).astype(jnp.bfloat16),
        "seq",
        scatter_dimension=0,
        tiled=True,
    ).astype(jnp.float32)


def take_block(piece_arr, block_index, span_len):
    return lax.dynamic_slice_in_dim(piece_arr, block_index * span_len, span_len, 1)


def keep_state(state_old):
    return state_old


def block_scores(query_block, key_block, query_first, key_first, score_scale):
    raw_scores = (
        jnp.einsum("sqhd,skhd->shqk", query_block, key_block, preferred_element_type=jnp.float32)
        * score_scale
    )
    shape_two = (query_block.shape[1], key_block.shape[1])
    query_pos = query_first + lax.broadcasted_iota(jnp.int32, shape_two, 0)
    key_pos = key_first + lax.broadcasted_iota(jnp.int32, shape_two, 1)
    return (raw_scores, key_pos <= query_pos)


def block_probs(raw_scores, allowed, log_block):
    return jnp.where(allowed, jnp.exp(raw_scores - log_block[..., None]), 0.0)


def per_device(
    tokens,
    ln1_gain,
    ln1_bias,
    qkv_weight,
    qv_bias,
    proj_weight,
    proj_bias,
    ln2_gain,
    ln2_bias,
    fc_weight,
    fc_bias,
    out_weight,
    out_bias,
    cotangent,
):
    seq_count, span_len, model_width = tokens.shape
    head_count = model_width // HEAD_DIM
    row_count = seq_count * span_len
    score_scale = HEAD_DIM ** (-0.5)
    my_first = lax.axis_index("seq") * span_len
    head_shape = (seq_count, span_len, head_count, HEAD_DIM)
    stat_shape = (seq_count, head_count, span_len)
    gathered_attn = fetch_attention(ln1_gain, ln1_bias, qkv_weight, qv_bias, proj_weight, proj_bias)
    gathered_mlp = fetch_mlp(ln2_gain, ln2_bias, fc_weight, fc_bias, out_weight, out_bias)
    gain_one, shift_one, w_qkv, bias_qv, w_proj, b_proj = gathered_attn
    gain_two, shift_two, w_fc, b_fc, w_out, b_out = gathered_mlp
    inputs = tokens.reshape(row_count, model_width).astype(jnp.float32)
    normed_one, norm_pull_one = jax.vjp(
        norm_rows, inputs, gain_one.astype(jnp.float32), shift_one.astype(jnp.float32)
    )
    normed_one = normed_one.astype(jnp.bfloat16)
    bias_full = jnp.concatenate(
        [bias_qv[:model_width], jnp.zeros((model_width,), jnp.bfloat16), bias_qv[model_width:]]
    ).astype(jnp.float32)
    projected = (jnp.dot(normed_one, w_qkv, preferred_element_type=jnp.float32) + bias_full).astype(
        jnp.bfloat16
    )
    query_rows = projected[:, :model_width].reshape(seq_count, span_len, model_width)
    key_rows = projected[:, model_width : 2 * model_width].reshape(seq_count, span_len, model_width)
    value_rows = projected[:, 2 * model_width :].reshape(seq_count, span_len, model_width)
    query_heads = query_rows.reshape(head_shape)
    key_heads = key_rows.reshape(head_shape)
    value_heads = value_rows.reshape(head_shape)
    start_stats = (
        jnp.full(stat_shape, FLOOR_SCORE, jnp.float32),
        jnp.zeros(stat_shape, jnp.float32),
    )
    key_piece = lax.all_gather(key_rows, "seq", axis=1, tiled=True)

    def stat_one_block(block_index, state_in):
        key_first = block_index * span_len

        def stat_add_block(state_old):
            row_top, row_total = state_old
            key_block = take_block(key_piece, block_index, span_len).reshape(head_shape)
            raw_scores, allowed = block_scores(
                query_heads, key_block, my_first, key_first, score_scale
            )
            masked = jnp.where(allowed, raw_scores, FLOOR_SCORE)
            new_top = jnp.maximum(row_top, jnp.max(masked, axis=-1))
            row_total = row_total * jnp.exp(row_top - new_top) + jnp.sum(
                jnp.exp(masked - new_top[..., None]), axis=-1
            )
            return (new_top, row_total)

        return lax.cond(key_first <= my_first, stat_add_block, keep_state, state_in)

    row_top, row_total = lax.fori_loop(
        0, key_piece.shape[1] // span_len, stat_one_block, start_stats
    )
    log_total = row_top + jnp.log(row_total)
    out_key_piece = lax.all_gather(key_rows, "seq", axis=1, tiled=True)
    value_piece = lax.all_gather(value_rows, "seq", axis=1, tiled=True)

    def out_one_block(block_index, state_in):
        key_first = block_index * span_len

        def out_add_block(state_old):
            key_block = take_block(out_key_piece, block_index, span_len).reshape(head_shape)
            value_block = take_block(value_piece, block_index, span_len).reshape(head_shape)
            raw_scores, allowed = block_scores(
                query_heads, key_block, my_first, key_first, score_scale
            )
            prob_block = block_probs(raw_scores, allowed, log_total).astype(jnp.bfloat16)
            return state_old + jnp.einsum(
                "shqk,skhd->sqhd", prob_block, value_block, preferred_element_type=jnp.float32
            )

        return lax.cond(key_first <= my_first, out_add_block, keep_state, state_in)

    attended = lax.fori_loop(
        0, out_key_piece.shape[1] // span_len, out_one_block, jnp.zeros(head_shape, jnp.float32)
    )
    attn_low = attended.reshape(row_count, model_width).astype(jnp.bfloat16)
    mixed_rows = (
        inputs
        + jnp.dot(attn_low, w_proj, preferred_element_type=jnp.float32)
        + b_proj.astype(jnp.float32)
    )
    normed_two, norm_pull_two = jax.vjp(
        norm_rows, mixed_rows, gain_two.astype(jnp.float32), shift_two.astype(jnp.float32)
    )
    normed_two = normed_two.astype(jnp.bfloat16)
    hidden = jnp.dot(normed_two, w_fc, preferred_element_type=jnp.float32) + b_fc.astype(
        jnp.float32
    )
    activated, gelu_pull = jax.vjp(gelu_tanh, hidden)
    activated = activated.astype(jnp.bfloat16)
    block_out = (
        mixed_rows
        + jnp.dot(activated, w_out, preferred_element_type=jnp.float32)
        + b_out.astype(jnp.float32)
    ).astype(jnp.bfloat16)
    block_out = block_out.reshape(seq_count, span_len, model_width)
    back_attn = fetch_attention(ln1_gain, ln1_bias, qkv_weight, qv_bias, proj_weight, proj_bias)
    back_mlp = fetch_mlp(ln2_gain, ln2_bias, fc_weight, fc_bias, out_weight, out_bias)
    w_qkv_back = back_attn[2]
    w_proj_back = back_attn[4]
    w_fc_back = back_mlp[2]
    w_out_back = back_mlp[4]
    grad_out = cotangent.reshape(row_count, model_width)
    out_bias_grad = jnp.sum(grad_out.astype(jnp.float32), axis=0)
    grad_activated = inner_right(grad_out, w_out_back)
    grad_hidden = gelu_pull(grad_activated)[0]
    fc_bias_grad = jnp.sum(grad_hidden, axis=0)
    hidden_low = grad_hidden.astype(jnp.bfloat16)
    grad_normed_two = inner_right(hidden_low, w_fc_back)
    grad_mixed_part, gain_two_grad, shift_two_grad = norm_pull_two(grad_normed_two)
    grad_mixed = grad_out.astype(jnp.float32) + grad_mixed_part
    proj_bias_grad = jnp.sum(grad_mixed, axis=0)
    mixed_low = grad_mixed.astype(jnp.bfloat16)
    grad_attn = inner_right(mixed_low, w_proj_back).astype(jnp.bfloat16)
    grad_heads = grad_attn.reshape(head_shape)
    grad_rows = grad_attn.reshape(seq_count, span_len, model_width)
    delta_rows = jnp.sum(grad_heads.astype(jnp.float32) * attended, axis=-1)
    delta_heads = jnp.swapaxes(delta_rows, 1, 2)
    log_rows = jnp.swapaxes(log_total, 1, 2)
    all_log, all_delta = (
        lax.all_gather(log_rows, "seq", axis=1, tiled=True),
        lax.all_gather(delta_rows, "seq", axis=1, tiled=True),
    )
    start_pair = (jnp.zeros(head_shape, jnp.float32), jnp.zeros(head_shape, jnp.float32))
    query_piece = lax.all_gather(query_rows, "seq", axis=1, tiled=True)
    grad_piece = lax.all_gather(grad_rows, "seq", axis=1, tiled=True)

    def key_one_block(block_index, state_in):
        query_first = block_index * span_len

        def key_add_block(state_old):
            grad_keys, grad_values = state_old
            query_block = take_block(query_piece, block_index, span_len).reshape(head_shape)
            grad_block = take_block(grad_piece, block_index, span_len).reshape(head_shape)
            log_block = jnp.swapaxes(
                lax.dynamic_slice_in_dim(all_log, query_first, span_len, 1), 1, 2
            )
            delta_block = jnp.swapaxes(
                lax.dynamic_slice_in_dim(all_delta, query_first, span_len, 1), 1, 2
            )
            raw_scores, allowed = block_scores(
                query_block, key_heads, query_first, my_first, score_scale
            )
            prob_block = block_probs(raw_scores, allowed, log_block)
            grad_values = grad_values + jnp.einsum(
                "shqk,sqhd->skhd",
                prob_block.astype(jnp.bfloat16),
                grad_block,
                preferred_element_type=jnp.float32,
            )
            grad_probs = jnp.einsum(
                "sqhd,skhd->shqk", grad_block, value_heads, preferred_element_type=jnp.float32
            )
            grad_scores = (prob_block * (grad_probs - delta_block[..., None])).astype(jnp.bfloat16)
            grad_keys = (
                grad_keys
                + jnp.einsum(
                    "shqk,sqhd->skhd", grad_scores, query_block, preferred_element_type=jnp.float32
                )
                * score_scale
            )
            return (grad_keys, grad_values)

        return lax.cond(query_first >= my_first, key_add_block, keep_state, state_in)

    grad_keys, grad_values = lax.fori_loop(
        0, query_piece.shape[1] // span_len, key_one_block, start_pair
    )
    query_key_piece = lax.all_gather(key_rows, "seq", axis=1, tiled=True)
    query_value_piece = lax.all_gather(value_rows, "seq", axis=1, tiled=True)

    def query_one_block(block_index, state_in):
        key_first = block_index * span_len

        def query_add_block(state_old):
            key_block = take_block(query_key_piece, block_index, span_len).reshape(head_shape)
            value_block = take_block(query_value_piece, block_index, span_len).reshape(head_shape)
            raw_scores, allowed = block_scores(
                query_heads, key_block, my_first, key_first, score_scale
            )
            prob_block = block_probs(raw_scores, allowed, log_total)
            grad_probs = jnp.einsum(
                "sqhd,skhd->shqk", grad_heads, value_block, preferred_element_type=jnp.float32
            )
            grad_scores = (prob_block * (grad_probs - delta_heads[..., None])).astype(jnp.bfloat16)
            return (
                state_old
                + jnp.einsum(
                    "shqk,skhd->sqhd", grad_scores, key_block, preferred_element_type=jnp.float32
                )
                * score_scale
            )

        return lax.cond(key_first <= my_first, query_add_block, keep_state, state_in)

    grad_queries = lax.fori_loop(
        0, query_key_piece.shape[1] // span_len, query_one_block, jnp.zeros(head_shape, jnp.float32)
    )
    query_grad_rows = grad_queries.reshape(row_count, model_width)
    key_grad_rows = grad_keys.reshape(row_count, model_width)
    value_grad_rows = grad_values.reshape(row_count, model_width)
    qv_bias_grad = jnp.concatenate(
        [jnp.sum(query_grad_rows, axis=0), jnp.sum(value_grad_rows, axis=0)]
    )
    projected_low = jnp.concatenate(
        [query_grad_rows, key_grad_rows, value_grad_rows], axis=1
    ).astype(jnp.bfloat16)
    grad_normed_one = inner_right(projected_low, w_qkv_back)
    grad_first, gain_one_grad, shift_one_grad = norm_pull_one(grad_normed_one)
    input_grad = (
        (grad_mixed + grad_first).astype(jnp.bfloat16).reshape(seq_count, span_len, model_width)
    )
    qkv_grad = weight_grad(normed_one, projected_low)
    proj_grad = weight_grad(attn_low, mixed_low)
    fc_grad = weight_grad(normed_two, hidden_low)
    out_grad = weight_grad(activated, grad_out)
    vector_shares = (
        lax.psum_scatter(
            gain_one_grad.astype(jnp.bfloat16), "seq", scatter_dimension=0, tiled=True
        ).astype(jnp.float32),
        lax.psum_scatter(
            shift_one_grad.astype(jnp.bfloat16), "seq", scatter_dimension=0, tiled=True
        ).astype(jnp.float32),
        lax.psum_scatter(
            qv_bias_grad.astype(jnp.bfloat16), "seq", scatter_dimension=0, tiled=True
        ).astype(jnp.float32),
        lax.psum_scatter(
            proj_bias_grad.astype(jnp.bfloat16), "seq", scatter_dimension=0, tiled=True
        ).astype(jnp.float32),
        lax.psum_scatter(
            gain_two_grad.astype(jnp.bfloat16), "seq", scatter_dimension=0, tiled=True
        ).astype(jnp.float32),
        lax.psum_scatter(
            shift_two_grad.astype(jnp.bfloat16), "seq", scatter_dimension=0, tiled=True
        ).astype(jnp.float32),
        lax.psum_scatter(
            fc_bias_grad.astype(jnp.bfloat16), "seq", scatter_dimension=0, tiled=True
        ).astype(jnp.float32),
        lax.psum_scatter(
            out_bias_grad.astype(jnp.bfloat16), "seq", scatter_dimension=0, tiled=True
        ).astype(jnp.float32),
    )
    summed = lax.psum(
        (
            vector_shares[0],
            vector_shares[1],
            vector_shares[2],
            vector_shares[3],
            vector_shares[4],
            vector_shares[5],
            vector_shares[6],
            vector_shares[7],
        ),
        "batch",
    )
    matrix_shares = (
        lax.psum_scatter(
            qkv_grad.astype(jnp.bfloat16), "batch", scatter_dimension=1, tiled=True
        ).astype(jnp.float32),
        lax.psum_scatter(
            proj_grad.astype(jnp.bfloat16), "batch", scatter_dimension=1, tiled=True
        ).astype(jnp.float32),
        lax.psum_scatter(
            fc_grad.astype(jnp.bfloat16), "batch", scatter_dimension=1, tiled=True
        ).astype(jnp.float32),
        lax.psum_scatter(
            out_grad.astype(jnp.bfloat16), "batch", scatter_dimension=1, tiled=True
        ).astype(jnp.float32),
    )
    return (
        block_out,
        input_grad,
        summed[0],
        summed[1],
        matrix_shares[0],
        summed[2],
        matrix_shares[1],
        summed[3],
        summed[4],
        summed[5],
        matrix_shares[2],
        summed[6],
        matrix_shares[3],
        summed[7],
    )


def solution(mesh):
    return jax.shard_map(
        per_device,
        mesh=mesh,
        in_specs=(
            P("batch", "seq", None),
            P("seq"),
            P("seq"),
            P("seq", None),
            P("seq"),
            P("seq", None),
            P("seq"),
            P("seq"),
            P("seq"),
            P("seq", None),
            P("seq"),
            P("seq", None),
            P("seq"),
            P("batch", "seq", None),
        ),
        out_specs=(
            P("batch", "seq", None),
            P("batch", "seq", None),
            P("seq"),
            P("seq"),
            P("seq", "batch"),
            P("seq"),
            P("seq", "batch"),
            P("seq"),
            P("seq"),
            P("seq"),
            P("seq", "batch"),
            P("seq"),
            P("seq", "batch"),
            P("seq"),
        ),
        check_vma=False,
    )
```

profile of v0, /device:TPU:0, one launch (start us, length us, event | category | flops | bytes accessed | tf_op | source)
XLA Modules:
  0.0 2667.1 jit_solution(1760274338055384182)
XLA Ops:
  17.2 40.9 %all-reduce.20 = (bf16[6400]{0:T(1024)(128)(2,1)S(1)}, bf16[3200]{0:T(1024)(128)(2,1)S(1)}, bf16[1600]{0:T(1024)(128)(2,1)S(1)}, bf16[1600]{0:T(1024)(128)(2,1)S...) all-reduce(bf16[6400]{0:T(1024)(128)(2,1)S(1)} %dynamic-update-slic, ...), channel_id=1, replica_groups=mesh['batch'=4,'seq'=8] {'seq'}, use_global_device_ids=true, to_apply=%add.6 | all-reduce | flops 17600 | bytes 70400
  60.8 166.0 %all-gather.14.cloned.1.call-done = bf16[1600,4800]{1,0:T(8,128)(2,1)} async-done(((bf16[200,4800]{1,0:T(8,128)(2,1)}), bf16[1600,4800]{1,0:T(8,128)(2,1)}) %all-gather.14.cloned.1.call-update) | async-done | bytes 15360016 | tf_op jit(solution)/shard_map/all_gather | solution.py:28
  226.8 12.1 fusion.39
  243.8 59.1 %all-gather.24.cloned.1.call-done = bf16[1024,1600]{0,1:T(8,128)(2,1)} async-done(((bf16[128,1600]{0,1:T(8,128)(2,1)}), bf16[1024,1600]{0,1:T(8,128)(2,1)}) %all-gather.24.cloned.1.call-update) | async-done | bytes 3276816 | tf_op jit(solution)/shard_map/all_gather | solution.py:162
  305.2 63.1 %all-gather.22.cloned.1.call-done = bf16[1024,1600]{0,1:T(8,128)(2,1)} async-done(((bf16[128,1600]{0,1:T(8,128)(2,1)}), bf16[1024,1600]{0,1:T(8,128)(2,1)}) %all-gather.22.cloned.1.call-update) | async-done | bytes 3276816 | tf_op jit(solution)/shard_map/all_gather | solution.py:163
  370.8 85.0 %all-gather.16.cloned.1.call-done = bf16[1600,1600]{1,0:T(8,128)(2,1)} async-done(((bf16[200,1600]{1,0:T(8,128)(2,1)}), bf16[1600,1600]{1,0:T(8,128)(2,1)}) %all-gather.16.cloned.1.call-update) | async-done | bytes 5120016 | tf_op jit(solution)/shard_map/all_gather | solution.py:30
  460.9 387.1 %all-gather.18.cloned.1.call-done = bf16[1600,6400]{1,0:T(8,128)(2,1)} async-done(((bf16[200,6400]{1,0:T(8,128)(2,1)}), bf16[1600,6400]{1,0:T(8,128)(2,1)}) %all-gather.18.cloned.1.call-update) | async-done | bytes 20480016 | tf_op jit(solution)/shard_map/all_gather | solution.py:39
  848.0 11.8 convolution_add_fusion
  859.9 397.5 %all-gather.20.cloned.1.call-done = bf16[6400,1600]{1,0:T(8,128)(2,1)} async-done(((bf16[800,1600]{1,0:T(8,128)(2,1)}), bf16[6400,1600]{1,0:T(8,128)(2,1)}) %all-gather.20.cloned.1.call-update) | async-done | bytes 20480016 | tf_op jit(solution)/shard_map/all_gather | solution.py:41
  1257.3 11.3 fusion.90
  1268.7 12.4 multiply_reduce_fusion
  1289.0 31.7 %all_gather.76 = f32[1,1024,25]{1,2,0:T(8,128)S(1)} all-gather(f32[1,128,25]{1,2,0:T(8,128)S(1)} %bitcast.254), channel_id=1, replica_groups=mesh['batch'=4,'seq'=8] {'seq'}, dimensions={1}, use_global_device_ids=true | all-gather | bytes 115200 | tf_op jit(solution)/shard_map/all_gather | solution.py:229
  1326.6 64.9 %all-gather.4 = f32[1024,25]{0,1:T(8,128)} all-gather(f32[128,25]{0,1:T(8,128)S(1)} %bitcast.252), channel_id=6, replica_groups=mesh['batch'=4,'seq'=8] {'seq'}, dimensions={0}, use_global_device_ids=true | all-gather | bytes 115200 | tf_op jit(solution)/shard_map/all_gather | solution.py:230
  1394.9 58.9 %while.65 = (s32[]{:T(128)}, f32[1,128,25,64]{1,3,2,0:T(8,128)}, f32[1,128,25,64]{1,3,2,0:T(8,128)S(1)}, s32[]{:T(128)}, bf16[1,1024,1600]{1,2,0:T(8,128)(2,1)},...) while((s32[]{:T(128)}, f32[1,128,25,64]{1,3,2,0:T(8,128)}, ...), condition=%wide.region_24.25_spmd, body=%wide.region_21.24_spmd.sunk | while | flops 213213440 | bytes 12399991 | solution.py:274
  1402.5 7.4 conditional.11
  1417.2 7.3 conditional.11
  1424.5 7.3 conditional.11
  1431.8 7.4 conditional.11
  1446.6 7.3 conditional.11
  1457.3 8.3 convolution_convert_fusion.2
  1467.3 10.3 convolution_convert_fusion.1
  1478.6 11.9 convolution_convert_fusion
  1490.8 28.5 %reduce-scatter.33.cloned.1.call-done = bf16[200,1600]{1,0:T(8,128)(2,1)} async-done(((bf16[1600,1600]{1,0:T(8,128)(2,1)}), bf16[200,1600]{1,0:T(8,128)(2,1)}) %reduce-scatter.33.cloned.1.call-update) | async-done | bytes 640016
  1521.7 252.7 %reduce-scatter.21.cloned.1.call-done = bf16[200,4800]{1,0:T(8,128)(2,1)} async-done(((bf16[1600,4800]{1,0:T(8,128)(2,1)}), bf16[200,4800]{1,0:T(8,128)(2,1)}) %reduce-scatter.21.cloned.1.call-update) | async-done | bytes 1920016 | tf_op jit(solution)/shard_map/reduce_scatter | solution.py:59
  1778.5 385.2 %reduce-scatter.35.cloned.1.call-done = bf16[200,6400]{1,0:T(8,128)(2,1)} async-done(((bf16[1600,6400]{1,0:T(8,128)(2,1)}), bf16[200,6400]{1,0:T(8,128)(2,1)}) %reduce-scatter.35.cloned.1.call-update) | async-done | bytes 2560016
  2168.4 346.7 %reduce-scatter.23.cloned.1.call-done = bf16[800,1600]{1,0:T(8,128)(2,1)} async-done(((bf16[6400,1600]{1,0:T(8,128)(2,1)}), bf16[800,1600]{1,0:T(8,128)(2,1)}) %reduce-scatter.23.cloned.1.call-update) | async-done | bytes 2560016 | tf_op jit(solution)/shard_map/reduce_scatter | solution.py:59
  2523.0 9.4 fusion.81
  2534.2 35.6 %all-reduce.19 = (bf16[1600]{0:T(1024)(128)(2,1)S(1)}, bf16[1600]{0:T(1024)(128)(2,1)S(1)}, bf16[1600]{0:T(1024)(128)(2,1)S(1)}, bf16[3200]{0:T(1024)(128)(2,1)S...) all-reduce(bf16[1600]{0:T(1024)(128)(2,1)S(1)} %dynamic-update-slic, ...), channel_id=1, replica_groups=mesh['batch'=4,'seq'=8] {'seq'}, use_global_device_ids=true, to_apply=%add.7 | all-reduce | flops 20800 | bytes 83200
  2570.5 11.4 all-reduce.18
  2581.9 15.5 fusion.49
  2601.7 16.8 reduce-scatter.29.cloned.1.call-done
  2621.1 36.2 %reduce-scatter.31.cloned.1.call-done = bf16[400,800]{1,0:T(8,128)(2,1)} async-done(((bf16[1600,800]{1,0:T(8,128)(2,1)}), bf16[400,800]{1,0:T(8,128)(2,1)}) %reduce-scatter.31.cloned.1.call-update) | async-done | bytes 640016
  (260 shorter events, 175.4 us)
Async XLA Ops:
  7.2 219.6 %copy-start.3 = (bf16[1,128,1600]{1,2,0:T(8,128)(2,1)S(1)}, bf16[1,128,1600]{1,2,0:T(8,128)(2,1)}, u32[]{:S(2)}) copy-start(bf16[1,128,1600]{1,2,0:T(8,128)(2,1)} %param.30) | copy-start | bytes 1228804
  7.2 219.6 %all-gather.14.cloned.1.call-start = ((), (), s32[]{:S(2)}) async-start(), calls=%async_computation.8 | async-start | bytes 17510400 | tf_op jit(solution)/shard_map/all_gather | solution.py:28
  7.9 295.0 %all-gather.24.cloned.1.call-start = ((), (), s32[]{:S(2)}) async-start(), calls=%async_computation.15 | async-start | bytes 3686400 | tf_op jit(solution)/shard_map/all_gather | solution.py:162
  240.0 128.3 %all-gather.22.cloned.1.call-start = ((), (), s32[]{:S(2)}) async-start(), calls=%async_computation.14 | async-start | bytes 3686400 | tf_op jit(solution)/shard_map/all_gather | solution.py:163
  240.7 62.2 %copy-start = (bf16[128,1600]{0,1:T(8,128)(2,1)S(1)}, bf16[128,1600]{0,1:T(8,128)(2,1)}, u32[]{:S(2)}) copy-start(bf16[128,1600]{0,1:T(8,128)(2,1)} %get-tuple-element.933) | copy-start | bytes 1228804
  240.8 215.1 %all-gather.16.cloned.1.call-start = ((), (), s32[]{:S(2)}) async-start(), calls=%async_computation.9 | async-start | bytes 5990400 | tf_op jit(solution)/shard_map/all_gather | solution.py:30
  241.3 606.7 %all-gather.18.cloned.1.call-start = ((), (), s32[]{:S(2)}) async-start(), calls=%async_computation.10 | async-start | bytes 23040000 | tf_op jit(solution)/shard_map/all_gather | solution.py:39
  241.9 1015.4 %all-gather.20.cloned.1.call-start = ((), (), s32[]{:S(2)}) async-start(), calls=%async_computation.11 | async-start | bytes 23961600 | tf_op jit(solution)/shard_map/all_gather | solution.py:41
  242.5 1149.0 %all-gather.26.cloned.1.call-start = ((), (), s32[]{:S(2)}) async-start(), calls=%async_computation.16 | async-start | bytes 3686400 | tf_op jit(solution)/shard_map/all_gather | solution.py:233
  243.2 1150.6 %all-gather.28.cloned.1.call-start = ((), (), s32[]{:S(2)}) async-start(), calls=%async_computation.17 | async-start | bytes 3686400 | tf_op jit(solution)/shard_map/all_gather | solution.py:234
  460.6 820.6 %copy-start.1 = (f32[128,1600]{0,1:T(8,128)}, f32[128,1600]{0,1:T(8,128)S(1)}, u32[]{:S(2)}) copy-start(f32[128,1600]{0,1:T(8,128)S(1)} %get-tuple-element.945) | copy-start | bytes 2457604
  460.9 796.5 %copy-start.10 = (bf16[1,128,1600]{1,2,0:T(8,128)(2,1)S(1)}, bf16[1,128,1600]{1,2,0:T(8,128)(2,1)}, u32[]{:S(2)}) copy-start(bf16[1,128,1600]{1,2,0:T(8,128)(2,1)} %param.43) | copy-start | bytes 1228804
  1268.7 12.4 copy-start.6
  1268.7 13.8 slice-start
  1268.7 13.8 slice-start.1
  1284.9 234.4 %reduce-scatter.33.cloned.1.call-start = ((), (), s32[]{:S(2)}) async-start(), calls=%async_computation.22 | async-start | bytes 5990400
  1289.0 31.8 %copy-start.5 = (bf16[128,1600]{0,1:T(8,128)(2,1)S(1)}, bf16[128,1600]{0,1:T(8,128)(2,1)}, u32[]{:S(2)}) copy-start(bf16[128,1600]{0,1:T(8,128)(2,1)} %convolution_convert_fusion.4) | copy-start | bytes 1228804
  1289.0 485.3 %reduce-scatter.21.cloned.1.call-start = ((), (), s32[]{:S(2)}) async-start(), calls=%async_computation.12 | async-start | bytes 17510400 | tf_op jit(solution)/shard_map/reduce_scatter | solution.py:59
  1453.9 3.4 copy-start.4
  1455.1 10.4 copy-start.14
  1457.3 8.3 copy-start.12
  1465.6 1.7 copy-start.7
  1465.6 698.1 %reduce-scatter.35.cloned.1.call-start = ((), (), s32[]{:S(2)}) async-start(), calls=%async_computation.23 | async-start | bytes 23040000
  1477.6 1037.4 %reduce-scatter.23.cloned.1.call-start = ((), (), s32[]{:S(2)}) async-start(), calls=%async_computation.13 | async-start | bytes 23961600 | tf_op jit(solution)/shard_map/reduce_scatter | solution.py:59
  1490.5 1106.9 %reduce-scatter.27.cloned.1.call-start = ((), (), s32[]{:S(2)}) async-start(), calls=%async_computation.19 | async-start | bytes 1024000
  1521.6 1077.7 %reduce-scatter.25.cloned.1.call-start = ((), (), s32[]{:S(2)}) async-start(), calls=%async_computation.18 | async-start | bytes 3072000
  1778.5 840.0 %reduce-scatter.29.cloned.1.call-start = ((), (), s32[]{:S(2)}) async-start(), calls=%async_computation.20 | async-start | bytes 4096000
  2168.3 354.2 %copy-start.16 = (bf16[200]{0:T(256)(128)(2,1)S(1)}, bf16[200]{0:T(256)(128)(2,1)}, u32[]{:S(2)}) copy-start(bf16[200]{0:T(256)(128)(2,1)} %param.42) | copy-start | bytes 1204
  2168.3 354.7 %copy-start.13 = (bf16[1,128,25,64]{1,3,2,0:T(8,128)(2,1)S(1)}, bf16[1,128,25,64]{1,3,2,0:T(8,128)(2,1)}, u32[]{:S(2)}) copy-start(bf16[1,128,25,64]{1,3,2,0:T(8,128)(2,1)} %copy-done.12) | copy-start | bytes 1228804
  2168.3 354.7 %copy-start.15 = (bf16[1,128,25,64]{1,3,2,0:T(8,128)(2,1)S(1)}, bf16[1,128,25,64]{1,3,2,0:T(8,128)(2,1)}, u32[]{:S(2)}) copy-start(bf16[1,128,25,64]{1,3,2,0:T(8,128)(2,1)} %copy-done.14) | copy-start | bytes 1228804
  2168.3 488.9 %reduce-scatter.31.cloned.1.call-start = ((), (), s32[]{:S(2)}) async-start(), calls=%async_computation.21 | async-start | bytes 3584000
  2523.0 10.0 copy-start.9
  (3 other events, 3.1 us)
Sparse Core Ops, SparseCore 0:
  10.2 216.5 all-gather.13
  240.1 62.7 all-gather.23
  305.5 62.7 all-gather.21
  370.4 85.4 all-gather.15
  457.2 390.7 all-gather.17
  849.4 407.8 all-gather.19
  1260.0 66.8 all-gather.25
  1329.4 64.3 all-gather.27
  1397.3 121.9 reduce-scatter.32
  1523.1 251.1 reduce-scatter.20
  1777.9 385.7 reduce-scatter.34
  2167.2 347.8 reduce-scatter.22
  2518.2 22.5 reduce-scatter.26
  2543.3 33.7 reduce-scatter.24
  2579.6 38.8 reduce-scatter.28
  2621.0 36.2 reduce-scatter.30
where the time goes:
time: 2680 us; the launch traced here: 2670 us
  waiting for transfers between devices  2230 us (83%)
  blocking collectives  185 us (7%)
  matrix products  161 us (6%)
  local copies, waits for them, and re-layouts  56.4 us (2%)
    reduce_scatter x2, waiting for transfers between devices, weight_grad(): lax.psum_scatter(inner_left(left_side, right_side).astype(jnp.bfloat16),...  599 us
    unnamed x22, waiting for transfers between devices  470 us
    all_gather x1, waiting for transfers between devices, fetch_mlp(): lax.all_gather(out_rows, 'seq', axis=0, tiled=True)  397 us
    all_gather x1, waiting for transfers between devices, fetch_mlp(): lax.all_gather(fc_rows, 'seq', axis=0, tiled=True)  387 us
    all_gather x1, waiting for transfers between devices, fetch_attention(): lax.all_gather(qkv_rows, 'seq', axis=0, tiled=True)  166 us
    all_gather x1, waiting for transfers between devices, fetch_attention(): lax.all_gather(proj_rows, 'seq', axis=0, tiled=True)  85 us
    unnamed x2, blocking collectives  76.5 us
    all_gather x1, blocking collectives, per_device(): lax.all_gather(delta_rows, 'seq', axis=1, tiled=True)  64.9 us
  transfers between devices with their start and end apart: 16, of which 13 were waited for; matrix products, arithmetic and copies ran while one was open for 8% of the time, Pallas kernels for 0%

commit v1 on v0

v1 whole, which is shorter than its diff:
```python
import functools

import jax
import jax.numpy as jnp
from jax import lax
from jax.experimental import pallas as pl
from jax.experimental.pallas import tpu as pltpu
from jax.sharding import PartitionSpec as P

HEAD_DIM = 64
HEAD_COLS = 3 * HEAD_DIM
EPSILON = 1e-05
FLOOR_SCORE = -1e30
SCALE = HEAD_DIM**-0.5
BF = jnp.bfloat16
F32 = jnp.float32


def dot_nn(a, b):
    return lax.dot_general(a, b, (((1,), (0,)), ((), ())), preferred_element_type=F32)


def dot_nt(a, b):
    return lax.dot_general(a, b, (((1,), (1,)), ((), ())), preferred_element_type=F32)


def dot_tn(a, b):
    return lax.dot_general(a, b, (((0,), (0,)), ((), ())), preferred_element_type=F32)


def steps(count, unrolled, body, carry):
    if unrolled:
        for j in range(count):
            carry = body(j, carry)
        return carry
    return lax.fori_loop(0, count, body, carry)


def rows_of(index, size):
    if isinstance(index, int):
        return pl.ds(index * size, size)
    return pl.ds(pl.multiple_of(index * size, size), size)


def causal(tile):
    key_pos = lax.broadcasted_iota(jnp.int32, (tile, tile), 0)
    query_pos = lax.broadcasted_iota(jnp.int32, (tile, tile), 1)
    return key_pos <= query_pos


def forward_kernel(tile, unrolled, x_ref, low_ref, full_ref, log_ref, value_t):
    tiles = x_ref.shape[0] // tile
    for head in range(2):
        base = head * HEAD_COLS
        k_cols = pl.ds(base + HEAD_DIM, HEAD_DIM)
        out_cols = pl.ds(head * HEAD_DIM, HEAD_DIM)

        def turn(j, carry):
            value_t[j] = x_ref[rows_of(j, tile), pl.ds(base + 2 * HEAD_DIM, HEAD_DIM)].T
            return carry

        steps(tiles, unrolled, turn, 0)

        def query_tile(i, carry):
            rows = rows_of(i, tile)
            query = x_ref[rows, pl.ds(base, HEAD_DIM)] * jnp.asarray(SCALE, BF)

            def add(j, state, masked):
                top, total, acc = state
                scores = dot_nt(x_ref[rows_of(j, tile), k_cols], query)
                if masked:
                    scores = jnp.where(causal(tile), scores, FLOOR_SCORE)
                new_top = jnp.maximum(top, jnp.max(scores, axis=0, keepdims=True))
                probs = jnp.exp(scores - new_top)
                fade = jnp.exp(top - new_top)
                total = total * fade + jnp.sum(probs, axis=0, keepdims=True)
                acc = acc * fade + dot_nn(value_t[j], probs.astype(BF))
                return new_top, total, acc

            state = (
                jnp.full((1, tile), FLOOR_SCORE, F32),
                jnp.zeros((1, tile), F32),
                jnp.zeros((HEAD_DIM, tile), F32),
            )
            state = steps(i, unrolled, lambda j, s: add(j, s, False), state)
            top, total, acc = add(i, state, True)
            result = (acc / total).T
            low_ref[rows, out_cols] = result.astype(BF)
            full_ref[rows, out_cols] = result
            log_ref[0, pl.ds(head, 1), rows] = top + jnp.log(total)
            return carry

        steps(tiles, unrolled, query_tile, 0)


def backward_kernel(
    tile, unrolled, x_ref, grad_ref, full_ref, log_ref, dx_ref, sum_ref, key_t, key_acc, value_acc
):
    tiles = x_ref.shape[0] // tile
    for head in range(2):
        base = head * HEAD_COLS
        q_cols = pl.ds(base, HEAD_DIM)
        k_cols = pl.ds(base + HEAD_DIM, HEAD_DIM)
        v_cols = pl.ds(base + 2 * HEAD_DIM, HEAD_DIM)
        out_cols = pl.ds(head * HEAD_DIM, HEAD_DIM)

        def turn(j, carry):
            key_t[j] = x_ref[rows_of(j, tile), k_cols].T
            return carry

        steps(tiles, unrolled, turn, 0)
        key_acc[...] = jnp.zeros_like(key_acc)
        value_acc[...] = jnp.zeros_like(value_acc)

        def query_tile(i, query_sum):
            rows = rows_of(i, tile)
            query = x_ref[rows, q_cols] * jnp.asarray(SCALE, BF)
            grad = grad_ref[rows, out_cols]
            delta = jnp.sum((grad.astype(F32) * full_ref[rows, out_cols]).T, axis=0, keepdims=True)
            log_row = log_ref[0, pl.ds(head, 1), rows]

            def add(j, acc, masked):
                key_rows = rows_of(j, tile)
                scores = dot_nt(x_ref[key_rows, k_cols], query)
                probs = jnp.exp(scores - log_row)
                if masked:
                    probs = jnp.where(causal(tile), probs, 0.0)
                grad_probs = dot_nt(x_ref[key_rows, v_cols], grad)
                grad_scores = (probs * (grad_probs - delta)).astype(BF)
                value_acc[key_rows, :] += dot_nn(probs.astype(BF), grad)
                key_acc[key_rows, :] += dot_nn(grad_scores, query)
                return acc + dot_nn(key_t[j], grad_scores)

            acc = jnp.zeros((HEAD_DIM, tile), F32)
            acc = steps(i, unrolled, lambda j, s: add(j, s, False), acc)
            acc = add(i, acc, True)
            result = acc.T * SCALE
            dx_ref[rows, q_cols] = result.astype(BF)
            return query_sum + jnp.sum(result, axis=0, keepdims=True)

        query_sum = steps(tiles, unrolled, query_tile, jnp.zeros((1, HEAD_DIM), F32))
        dx_ref[:, k_cols] = key_acc[...].astype(BF)
        dx_ref[:, v_cols] = value_acc[...].astype(BF)
        sum_ref[0, :, q_cols] = query_sum
        sum_ref[0, :, k_cols] = jnp.sum(key_acc[...], axis=0, keepdims=True)
        sum_ref[0, :, v_cols] = jnp.sum(value_acc[...], axis=0, keepdims=True)


def attention_tile(length):
    return min(256, length)


def attention_forward(projected, heads):
    length = projected.shape[0]
    tile = attention_tile(length)
    tiles = length // tile
    pairs = heads // 2
    return pl.pallas_call(
        functools.partial(forward_kernel, tile, tiles <= 4),
        grid=(pairs,),
        in_specs=[pl.BlockSpec((length, 2 * HEAD_COLS), lambda g: (0, g))],
        out_specs=[
            pl.BlockSpec((length, 2 * HEAD_DIM), lambda g: (0, g)),
            pl.BlockSpec((length, 2 * HEAD_DIM), lambda g: (0, g)),
            pl.BlockSpec((1, 2, length), lambda g: (g, 0, 0)),
        ],
        out_shape=[
            jax.ShapeDtypeStruct((length, heads * HEAD_DIM), BF),
            jax.ShapeDtypeStruct((length, heads * HEAD_DIM), F32),
            jax.ShapeDtypeStruct((pairs, 2, length), F32),
        ],
        scratch_shapes=[pltpu.VMEM((tiles, HEAD_DIM, tile), BF)],
        compiler_params=pltpu.CompilerParams(vmem_limit_bytes=48 << 20),
        cost_estimate=pl.CostEstimate(
            flops=4 * length * length * heads * HEAD_DIM,
            bytes_accessed=length * heads * HEAD_DIM * 12,
            transcendentals=length * length * heads // 2,
        ),
        name="attention_forward",
    )(projected)


def attention_backward(projected, grad, full, logs, heads):
    length = projected.shape[0]
    tile = attention_tile(length)
    tiles = length // tile
    pairs = heads // 2
    return pl.pallas_call(
        functools.partial(backward_kernel, tile, tiles <= 4),
        grid=(pairs,),
        in_specs=[
            pl.BlockSpec((length, 2 * HEAD_COLS), lambda g: (0, g)),
            pl.BlockSpec((length, 2 * HEAD_DIM), lambda g: (0, g)),
            pl.BlockSpec((length, 2 * HEAD_DIM), lambda g: (0, g)),
            pl.BlockSpec((1, 2, length), lambda g: (g, 0, 0)),
        ],
        out_specs=[
            pl.BlockSpec((length, 2 * HEAD_COLS), lambda g: (0, g)),
            pl.BlockSpec((1, 1, 2 * HEAD_COLS), lambda g: (g, 0, 0)),
        ],
        out_shape=[
            jax.ShapeDtypeStruct((length, heads * HEAD_COLS), BF),
            jax.ShapeDtypeStruct((pairs, 1, 2 * HEAD_COLS), F32),
        ],
        scratch_shapes=[
            pltpu.VMEM((tiles, HEAD_DIM, tile), BF),
            pltpu.VMEM((length, HEAD_DIM), F32),
            pltpu.VMEM((length, HEAD_DIM), F32),
        ],
        compiler_params=pltpu.CompilerParams(vmem_limit_bytes=48 << 20),
        cost_estimate=pl.CostEstimate(
            flops=10 * length * length * heads * HEAD_DIM,
            bytes_accessed=length * heads * HEAD_DIM * 20,
            transcendentals=length * length * heads // 2,
        ),
        name="attention_backward",
    )(projected, grad, full, logs)


def norm_stats(rows):
    mean = jnp.mean(rows, axis=-1, keepdims=True)
    centred = rows - mean
    variance = jnp.mean(centred * centred, axis=-1, keepdims=True)
    inverse = lax.rsqrt(variance + EPSILON)
    return centred * inverse, inverse


def norm_back(grad, xhat, inverse, gain):
    h = grad * gain
    return inverse * (
        h - jnp.mean(h, axis=-1, keepdims=True) - xhat * jnp.mean(h * xhat, axis=-1, keepdims=True)
    )


def gelu_both(hidden):
    activated, pull = jax.vjp(lambda v: jax.nn.gelu(v, approximate=True), hidden)
    return activated, pull(jnp.ones_like(hidden))[0]


def gather(value, axis="seq", dim=0):
    return lax.all_gather(value, axis, axis=dim, tiled=True)


def scatter_sum(value, axis="seq", dim=0):
    return lax.psum_scatter(value, axis, scatter_dimension=dim, tiled=True)


def exchange(value, split, concat, axis="seq"):
    return lax.all_to_all(value, axis, split, concat, tiled=True)


def per_device(
    shards,
    batches,
    tokens,
    ln1_gain,
    ln1_bias,
    qkv_weight,
    qv_bias,
    proj_weight,
    proj_bias,
    ln2_gain,
    ln2_bias,
    fc_weight,
    fc_bias,
    out_weight,
    out_bias,
    cotangent,
):
    _, span, width = tokens.shape
    length = span * shards
    head_count = width // HEAD_DIM
    heads = -(-head_count // shards)
    heads += heads % 2
    padded = heads * shards
    hidden_width = fc_bias.shape[0]
    me = lax.axis_index("seq")

    own_tokens = tokens[0]
    own_cot = cotangent[0]
    all_tokens = gather(own_tokens)

    small = jnp.concatenate(
        [ln1_gain, ln1_bias, qv_bias, proj_bias, ln2_gain, ln2_bias, out_bias]
    )
    part = width // shards
    small_all = gather(small.reshape(1, -1))
    gain_one = small_all[:, :part].reshape(width).astype(F32)
    shift_one = small_all[:, part : 2 * part].reshape(width).astype(F32)
    bias_qv = small_all[:, 2 * part : 4 * part].reshape(2 * width)
    b_proj = small_all[:, 4 * part : 5 * part].reshape(width).astype(F32)
    gain_two = small_all[:, 5 * part : 6 * part].reshape(width).astype(F32)
    shift_two = small_all[:, 6 * part : 7 * part].reshape(width).astype(F32)
    b_out = small_all[:, 7 * part : 8 * part].reshape(width).astype(F32)

    def by_head(rows):
        count = rows.shape[0]
        rows = rows.reshape(count, 3, head_count, HEAD_DIM)
        rows = jnp.pad(rows, ((0, 0), (0, 0), (0, padded - head_count), (0, 0)))
        return jnp.swapaxes(rows, 1, 2).reshape(count, padded * HEAD_COLS)

    w_qkv = exchange(by_head(qkv_weight), 1, 0)
    w_fc = exchange(fc_weight, 1, 0)
    w_proj = gather(proj_weight)
    all_cot = gather(own_cot)
    bias_row = jnp.concatenate([bias_qv[:width], jnp.zeros((width,), BF), bias_qv[width:]])
    slice_cols = heads * HEAD_COLS
    bias_slice = lax.dynamic_slice_in_dim(
        by_head(bias_row.reshape(1, -1)), me * slice_cols, slice_cols, 1
    ).astype(F32)

    xhat_all, _ = norm_stats(all_tokens.astype(F32))
    normed_one = (xhat_all * gain_one + shift_one).astype(BF)
    projected = (dot_nn(normed_one, w_qkv) + bias_slice).astype(BF)
    attended_heads, attended_full, log_total = attention_forward(projected, heads)
    attn_low = exchange(attended_heads, 0, 1)[:, :width]

    inputs = own_tokens.astype(F32)
    mixed = inputs + dot_nn(attn_low, w_proj) + b_proj
    xhat_two, inverse_two = norm_stats(mixed)
    normed_two = gather((xhat_two * gain_two + shift_two).astype(BF))
    hidden = dot_nn(normed_two, w_fc) + fc_bias.astype(F32)
    activated, gelu_slope = gelu_both(hidden)
    activated = activated.astype(BF)
    out_part = scatter_sum(dot_nn(activated, out_weight).astype(BF))
    block_out = (mixed + out_part.astype(F32) + b_out).astype(BF)

    grad_hidden = dot_nt(all_cot, out_weight) * gelu_slope
    fc_bias_grad = jnp.sum(grad_hidden, axis=0)
    hidden_low = grad_hidden.astype(BF)
    g_two = scatter_sum(dot_nt(hidden_low, w_fc).astype(BF)).astype(F32)
    out_grad = dot_tn(activated, all_cot).astype(BF)
    fc_grad = dot_tn(normed_two, hidden_low).astype(BF)
    cot_full = own_cot.astype(F32)
    gain_two_grad = jnp.sum(g_two * xhat_two, axis=0)
    shift_two_grad = jnp.sum(g_two, axis=0)
    grad_mixed = cot_full + norm_back(g_two, xhat_two, inverse_two, gain_two)
    mixed_low = grad_mixed.astype(BF)

    grad_attn = dot_nt(mixed_low, w_proj).astype(BF)
    grad_attn = jnp.pad(grad_attn, ((0, 0), (0, padded * HEAD_DIM - width)))
    grad_heads = exchange(grad_attn, 1, 0)
    proj_grad = dot_tn(attn_low, mixed_low).astype(BF)
    grad_projected, column_sums = attention_backward(
        projected, grad_heads, attended_full, log_total, heads
    )
    g_one = scatter_sum(dot_nt(grad_projected, w_qkv).astype(BF)).astype(F32)
    qkv_grad = dot_tn(normed_one, grad_projected).astype(BF)
    xhat_one, inverse_one = norm_stats(inputs)
    gain_one_grad = jnp.sum(g_one * xhat_one, axis=0)
    shift_one_grad = jnp.sum(g_one, axis=0)
    grad_first = norm_back(g_one, xhat_one, inverse_one, gain_one)
    input_grad = (grad_mixed + grad_first).astype(BF)

    def from_heads(rows):
        count = rows.shape[0]
        rows = rows.reshape(count, padded, 3, HEAD_DIM)[:, :head_count]
        return jnp.swapaxes(rows, 1, 2).reshape(count, 3 * width)

    qkv_share = scatter_sum(from_heads(exchange(qkv_grad, 0, 1)), "batch", 1).astype(F32)
    fc_share = scatter_sum(exchange(fc_grad, 0, 1), "batch", 1).astype(F32)
    out_share = scatter_sum(out_grad, "batch", 1).astype(F32)
    proj_share = scatter_sum(scatter_sum(proj_grad), "batch", 1).astype(F32)

    head_sums = jnp.zeros((padded * HEAD_COLS,), F32)
    head_sums = lax.dynamic_update_slice_in_dim(
        head_sums, column_sums.reshape(-1), me * slice_cols, 0
    )
    qkv_sums = from_heads(head_sums.reshape(1, -1))[0]
    qv_sums = jnp.concatenate([qkv_sums[:width], qkv_sums[2 * width :]])
    vectors = [
        gain_one_grad,
        shift_one_grad,
        qv_sums,
        jnp.sum(grad_mixed, axis=0),
        gain_two_grad,
        shift_two_grad,
        jnp.sum(cot_full, axis=0),
    ]
    table = jnp.concatenate([v.reshape(shards, -1) for v in vectors], axis=1)
    own = scatter_sum(table.reshape(-1))
    sums = lax.psum(jnp.concatenate([own, fc_bias_grad]), "batch")
    return (
        block_out[None],
        input_grad[None],
        sums[:part],
        sums[part : 2 * part],
        qkv_share,
        sums[2 * part : 4 * part],
        proj_share,
        sums[4 * part : 5 * part],
        sums[5 * part : 6 * part],
        sums[6 * part : 7 * part],
        fc_share,
        sums[8 * part : 8 * part + hidden_width],
        out_share,
        sums[7 * part : 8 * part],
    )


def solution(mesh):
    rows = P("batch", "seq", None)
    matrix, vector = P("seq", None), P("seq")
    shared = P("seq", "batch")
    return jax.shard_map(
        functools.partial(per_device, mesh.shape["seq"], mesh.shape["batch"]),
        mesh=mesh,
        in_specs=(
            rows, vector, vector, matrix, vector, matrix, vector,
            vector, vector, matrix, vector, matrix, vector, rows,
        ),
        out_specs=(
            rows, rows, vector, vector, shared, vector, shared,
            vector, vector, vector, shared, vector, shared, vector,
        ),
        check_vma=False,
    )
```

time: 2680 us -> 979 us (0.37)
  waiting for transfers between devices: 2230 us -> 399 us
  blocking collectives: 185 us -> 349 us
  matrix products: 161 us -> 70.9 us
  local copies, waits for them, and re-layouts: 56.4 us -> 83.6 us
    all_gather x8 -> x4, waiting for transfers between devices: 1160 us -> 61 us  [gather(): return lax.all_gather(value, axis, axis=dim, tiled=True)]
    reduce_scatter x2, waiting for transfers between devices: 599 us -> 17.6 us  [scatter_sum(): return lax.psum_scatter(value, axis, scatter_dimension=dim, tiled=True)]
    unnamed x22 -> x18, waiting for transfers between devices: 470 us -> 196 us
    all_to_all x0 -> x3, blocking collectives: none -> 188 us  [exchange(): return lax.all_to_all(value, axis, split, concat, tiled=True)]
    all_to_all x0 -> x3, waiting for transfers between devices: none -> 124 us  [exchange(): return lax.all_to_all(value, axis, split, concat, tiled=True)]
    all_gather x2 -> x0, blocking collectives: 96.6 us -> none  [the longest x1 64.9 us: per_device(): lax.all_gather(delta_rows, 'seq', axis=1, tiled=True)]
    dot_general x40 -> x12, matrix products: 161 us -> 70.9 us  [the longest x4 24.4 us: dot_nt(): lax.dot_general(a, b, (((1,), (1,)), ((), ())), preferred_element_type=F32)]
    unnamed x2, blocking collectives: 76.5 us -> 150 us
  transfers between devices with their start and end apart: 16 -> 15, of which waited for: 13 -> 9; matrix products, arithmetic and copies ran while one was open for 8% -> 15% of each run, Pallas kernels for 0% -> 2%
where the time goes in v1:
time: 979 us; the launch traced here: 975 us
  waiting for transfers between devices  399 us (41%)
  blocking collectives  349 us (36%)
  local copies, waits for them, and re-layouts  83.6 us (9%)
  matrix products  70.9 us (7%)
  Pallas kernels  24.1 us (2%)
  starting transfers between devices  16.9 us (2%)
  between operations  16.4 us (2%)
  other arithmetic  15.1 us (2%)
    unnamed x18, waiting for transfers between devices  196 us
    all_to_all x3, blocking collectives, exchange(): return lax.all_to_all(value, axis, split, concat, tiled=True)  188 us
    unnamed x2, blocking collectives  150 us
    all_to_all x3, waiting for transfers between devices, exchange(): return lax.all_to_all(value, axis, split, concat, tiled=True)  124 us
    all_gather x4, waiting for transfers between devices, gather(): return lax.all_gather(value, axis, axis=dim, tiled=True)  61 us
    unnamed x70, local copies, waits for them, and re-layouts  46.8 us
    dot_general x4, matrix products, dot_nt(): lax.dot_general(a, b, (((1,), (1,)), ((), ())), preferred_element_type=F32)  24.4 us
    dot_general x4, matrix products, dot_tn(): lax.dot_general(a, b, (((0,), (0,)), ((), ())), preferred_element_type=F32)  23.6 us
  transfers between devices with their start and end apart: 15, of which 9 were waited for; matrix products, arithmetic and copies ran while one was open for 15% of the time, Pallas kernels for 2%

profile of v1, /device:TPU:0, one launch (start us, length us, event | category | flops | bytes accessed | tf_op | source)
XLA Modules:
  0.0 974.7 jit_solution(4348245152659921313)
XLA Ops:
  22.0 7.4 all-to-all-start
  31.1 111.4 %all-reduce.3 = bf16[12800]{0:T(1024)(128)(2,1)S(1)} all-reduce(bf16[12800]{0:T(1024)(128)(2,1)S(1)} %dynamic-update-slice), channel_id=3, replica_groups=mesh['batch'=4,'seq'=8] {'seq'}, use_global_device_ids=true, to_apply=%add.3 | all-reduce | flops 12800 | bytes 51200
  147.5 6.3 add_convert_fusion.x_ref
  153.7 12.5 %attention_forward.1 = (bf16[1024,256]{1,0:T(8,128)(2,1)S(1)}, f32[1024,256]{1,0:T(8,128)S(1)}, f32[2,2,1024]{2,1,0:T(2,128)S(1)}) custom-call(bf16[1024,768]{1,0:T(8,128)(2,1)S(1)} %add_convert_fusion.x_ref), custom_call_target="tpu_custom_call" | custom-call | flops 1073741824 | bytes 3145728 | tf_op jit(solution)/shard_map/attention_forward/pallas_call | solution.py:158
  173.7 25.9 %all-to-all-done.1 = bf16[8,128,256]{1,2,0:T(8,128)(2,1)S(1)} async-done(((bf16[8,128,256]{1,2,0:T(8,128)(2,1)}), bf16[8,128,256]{1,2,0:T(8,128)(2,1)S(1)}, u32[]{:S(2)}, u32[]{:S(2)}) %all-to-all-start.1) | async-done | bytes 524320 | tf_op jit(solution)/shard_map/all_to_all | solution.py:249
  199.6 16.8 %all-gather.8.cloned.1.call-done = bf16[1600,1600]{1,0:T(8,128)(2,1)} async-done(((bf16[200,1600]{1,0:T(8,128)(2,1)}), bf16[1600,1600]{1,0:T(8,128)(2,1)}) %all-gather.8.cloned.1.call-update) | async-done | bytes 5120016 | tf_op jit(solution)/shard_map/all_gather | solution.py:241
  216.4 5.0 fusion.57
  222.9 7.3 all_to_all.90
  239.2 98.5 %all-to-all-done.2 = bf16[200,8,800]{2,0,1:T(8,128)(2,1)} async-done(((bf16[200,8,800]{2,0,1:T(8,128)(2,1)}), bf16[200,8,800]{2,0,1:T(8,128)(2,1)}, u32[]{:S(2)}, u32[]{:S(2)}) %all-to-all-start.2) | async-done | bytes 2560032 | tf_op jit(solution)/shard_map/all_to_all | solution.py:249
  337.8 6.0 fusion.59
  345.5 5.7 convolution_convert_fusion.3
  351.1 5.5 copy.64
  356.8 44.2 %all-gather.14.cloned.1.call-done = bf16[1,1024,1600]{1,2,0:T(8,128)(2,1)} async-done(((bf16[1,128,1600]{1,2,0:T(8,128)(2,1)}), bf16[1,1024,1600]{1,2,0:T(8,128)(2,1)}) %all-gather.14.cloned.1.call-update) | async-done | bytes 3276816 | tf_op jit(solution)/shard_map/all_gather | solution.py:241
  401.0 7.3 fusion.58
  409.4 6.9 convolution_convert_fusion.1
  416.3 5.5 copy.66
  421.8 8.5 convolution_convert_fusion.4
  430.4 5.6 convolution_convert_fusion.5
  439.6 83.2 %all_to_all.111 = bf16[8,200,800]{2,1,0:T(8,128)(2,1)} all-to-all(bf16[8,200,800]{2,1,0:T(8,128)(2,1)} %bitcast.128), channel_id=1, replica_groups=mesh['batch'=4,'seq'=8] {'seq'}, dimensions={0} | all-to-all | bytes 5120000 | tf_op jit(solution)/shard_map/all_to_all | solution.py:249
  528.9 62.2 %reduce-scatter.27.cloned.1.call-done = bf16[128,1600]{1,0:T(8,128)(2,1)} async-done(((bf16[1024,1600]{1,0:T(8,128)(2,1)}), bf16[128,1600]{1,0:T(8,128)(2,1)}) %reduce-scatter.27.cloned.1.call-update) | async-done | bytes 409616
  599.8 18.5 %all_to_all.112 = bf16[128,8,256]{2,0,1:T(8,128)(2,1)S(1)} all-to-all(bf16[128,8,256]{2,0,1:T(8,128)(2,1)} %copy.58), channel_id=1, replica_groups=mesh['batch'=4,'seq'=8] {'seq'}, dimensions={1} | all-to-all | bytes 1048576 | tf_op jit(solution)/shard_map/all_to_all | solution.py:249
  618.3 11.6 %attention_backward.1 = (bf16[1024,768]{1,0:T(8,128)(2,1)S(1)}, f32[2,1,384]{2,1,0:T(1,128)S(1)}) custom-call(bf16[1024,768]{1,0:T(8,128)(2,1)S(1)} %copy-done.3, bf16[1024,256]{1,0:T(8,128)(2,1)S(1)} %bitcast.124, f32[1024,256]{1,0:T(8,128)S(1)} %copy-done.5, f32[2,2,1024]{2,1,0:T(2,128)S(1)} %get-tuple-element.21.log_ref), custom_call_target="tpu_custom_call" | custom-call | flops 2684354560 | bytes 5242880 | tf_op jit(solution)/shard_map/attention_backward/pallas_call | solution.py:188
  631.1 5.9 convolution_convert_fusion.2
  637.0 5.6 copy.68
  649.2 5.6 convolution_convert_fusion.6
  654.8 86.7 %all_to_all.113 = bf16[8,200,768]{2,1,0:T(8,128)(2,1)S(1)} all-to-all(bf16[8,200,768]{2,1,0:T(8,128)(2,1)S(1)} %bitcast.136), channel_id=1, replica_groups=mesh['batch'=4,'seq'=8] {'seq'}, dimensions={0} | all-to-all | bytes 4915200 | tf_op jit(solution)/shard_map/all_to_all | solution.py:249
  755.6 21.2 %reduce-scatter.29.cloned.1.call-done = bf16[128,1600]{1,0:T(8,128)(2,1)} async-done(((bf16[1024,1600]{1,0:T(8,128)(2,1)}), bf16[128,1600]{1,0:T(8,128)(2,1)}) %reduce-scatter.29.cloned.1.call-update) | async-done | bytes 409616
  779.0 38.1 %all-reduce.4 = f32[12800]{0:T(1024)} all-reduce(f32[12800]{0:T(1024)S(1)} %reshape.209), channel_id=8, replica_groups=mesh['batch'=4,'seq'=8] {'seq'}, use_global_device_ids=true, to_apply=%region_19.20.clone | all-reduce | flops 12800 | bytes 102400
  818.0 86.3 %reduce-scatter.35.cloned.1.call-done = bf16[200,1600]{1,0:T(8,128)(2,1)} async-done(((bf16[1600,1600]{1,0:T(8,128)(2,1)}), bf16[200,1600]{1,0:T(8,128)(2,1)}) %reduce-scatter.35.cloned.1.call-update) | async-done | bytes 640016
  906.7 11.1 %psum.7 = f32[2400]{0:T(1024)S(1)} all-reduce(f32[2400]{0:T(1024)S(1)} %pad_maximum_fusion.1), channel_id=1, replica_groups=mesh['batch'=4,'seq'=8] {'batch'}, use_global_device_ids=true, to_apply=%region_21.22 | all-reduce | flops 2400 | bytes 19200 | tf_op jit(solution)/shard_map/psum | solution.py:382
  922.1 17.6 %reduce-scatter.21.cloned.1.call-done = bf16[200,1200]{0,1:T(8,128)(2,1)} async-done(((bf16[200,4800]{0,1:T(8,128)(2,1)}), bf16[200,1200]{0,1:T(8,128)(2,1)}) %reduce-scatter.21.cloned.1.call-update) | async-done | bytes 480016 | tf_op jit(solution)/shard_map/reduce_scatter | solution.py:245
  941.9 23.8 %reduce-scatter.31.cloned.1.call-done = bf16[400,200]{1,0:T(8,128)(2,1)} async-done(((bf16[1600,200]{1,0:T(8,128)(2,1)}), bf16[400,200]{1,0:T(8,128)(2,1)}) %reduce-scatter.31.cloned.1.call-update) | async-done | bytes 160016
  (177 shorter events, 94.8 us)
Async XLA Ops:
  7.2 338.3 %copy-start = (bf16[800,1600]{1,0:T(8,128)(2,1)S(1)}, bf16[800,1600]{1,0:T(8,128)(2,1)}, u32[]{:S(2)}) copy-start(bf16[800,1600]{1,0:T(8,128)(2,1)} %param.25) | copy-start | bytes 7680004
  7.2 136.4 %all-gather.12.cloned.1.call-start = ((), (), s32[]{:S(2)}) async-start(), calls=%async_computation.18 | async-start | bytes 3686400 | tf_op jit(solution)/shard_map/all_gather | solution.py:241
  7.9 208.5 %all-gather.8.cloned.1.call-start = ((), (), s32[]{:S(2)}) async-start(), calls=%async_computation.14 | async-start | bytes 5990400 | tf_op jit(solution)/shard_map/all_gather | solution.py:241
  21.9 7.5 copy-start.17
  21.9 8.7 copy-start.18
  21.9 8.8 copy-start.19
  21.9 8.8 copy-start.20
  21.9 8.8 copy-start.21
  21.9 8.8 copy-start.22
  22.0 8.8 copy-start.23
  22.0 8.8 copy-start.24
  22.0 125.5 %all-to-all-start = ((bf16[200,8,768]{2,0,1:T(8,128)(2,1)}), bf16[200,8,768]{2,0,1:T(8,128)(2,1)}, u32[]{:S(2)}, u32[]{:S(2)}) async-start(bf16[200,8,768]{2,0,1:T(8,128)(2,1)} %copy.54), calls=%async_computation | async-start | bytes 4915200 | tf_op jit(solution)/shard_map/all_to_all | solution.py:249
  143.6 2.9 copy-start.9
  169.4 30.2 %all-to-all-start.1 = ((bf16[8,128,256]{1,2,0:T(8,128)(2,1)}), bf16[8,128,256]{1,2,0:T(8,128)(2,1)S(1)}, u32[]{:S(2)}, u32[]{:S(2)}) async-start(bf16[8,128,256]{1,2,0:T(8,128)(2,1)} %copy.56), calls=%async_computation.1 | async-start | bytes 1048576 | tf_op jit(solution)/shard_map/all_to_all | solution.py:249
  172.9 164.9 %all-gather.10.cloned.1.call-start = ((), (), s32[]{:S(2)}) async-start(), calls=%async_computation.15 | async-start | bytes 3686400 | tf_op jit(solution)/shard_map/all_gather | solution.py:241
  199.6 16.8 %copy-start.12 = (bf16[8,128,256]{1,2,0:T(8,128)(2,1)}, bf16[8,128,256]{1,2,0:T(8,128)(2,1)S(1)}, u32[]{:S(2)}) copy-start(bf16[8,128,256]{1,2,0:T(8,128)(2,1)S(1)} %all-to-all-done.1) | copy-start | bytes 1572868
  234.0 5.2 copy-start.16
  234.0 103.8 %all-to-all-start.2 = ((bf16[200,8,800]{2,0,1:T(8,128)(2,1)}), bf16[200,8,800]{2,0,1:T(8,128)(2,1)}, u32[]{:S(2)}, u32[]{:S(2)}) async-start(bf16[200,8,800]{2,0,1:T(8,128)(2,1)} %copy.57), calls=%async_computation.2 | async-start | bytes 5734400 | tf_op jit(solution)/shard_map/all_to_all | solution.py:249
  238.6 162.4 %all-gather.14.cloned.1.call-start = ((), (), s32[]{:S(2)}) async-start(), calls=%async_computation.19 | async-start | bytes 3686400 | tf_op jit(solution)/shard_map/all_gather | solution.py:241
  239.2 288.5 %reduce-scatter.25.cloned.1.call-start = ((), (), s32[]{:S(2)}) async-start(), calls=%async_computation.20 | async-start | bytes 3833856
  356.6 234.5 %reduce-scatter.27.cloned.1.call-start = ((), (), s32[]{:S(2)}) async-start(), calls=%async_computation.21 | async-start | bytes 3833856
  421.8 327.8 %reduce-scatter.23.cloned.1.call-start = ((), (), s32[]{:S(2)}) async-start(), calls=%async_computation.17 | async-start | bytes 3584000 | tf_op jit(solution)/shard_map/reduce_scatter | solution.py:245
  430.4 322.5 %reduce-scatter.33.cloned.1.call-start = ((), (), s32[]{:S(2)}) async-start(), calls=%async_computation.24 | async-start | bytes 4096000
  527.5 65.5 %copy-start.14 = (bf16[1,128,1600]{1,2,0:T(8,128)(2,1)S(1)}, bf16[1,128,1600]{1,2,0:T(8,128)(2,1)}, u32[]{:S(2)}) copy-start(bf16[1,128,1600]{1,2,0:T(8,128)(2,1)} %param.27) | copy-start | bytes 1228804
  527.5 249.2 %reduce-scatter.29.cloned.1.call-start = ((), (), s32[]{:S(2)}) async-start(), calls=%async_computation.22 | async-start | bytes 3833856
  594.3 4.4 copy-start.10
  594.3 24.0 %copy-start.3 = (bf16[1024,768]{1,0:T(8,128)(2,1)S(1)}, bf16[1024,768]{1,0:T(8,128)(2,1)}, u32[]{:S(2)}) copy-start(bf16[1024,768]{1,0:T(8,128)(2,1)} %copy-done.2) | copy-start | bytes 4718596
  594.3 24.0 %copy-start.5 = (f32[1024,256]{1,0:T(8,128)S(1)}, f32[1024,256]{1,0:T(8,128)}, u32[]{:S(2)}) copy-start(f32[1024,256]{1,0:T(8,128)} %copy-done.4) | copy-start | bytes 3145732
  642.6 261.7 %reduce-scatter.35.cloned.1.call-start = ((), (), s32[]{:S(2)}) async-start(), calls=%async_computation.25 | async-start | bytes 5990400
  647.8 291.8 %reduce-scatter.21.cloned.1.call-start = ((), (), s32[]{:S(2)}) async-start(), calls=%async_computation.16 | async-start | bytes 3072000 | tf_op jit(solution)/shard_map/reduce_scatter | solution.py:245
  748.1 217.6 %reduce-scatter.31.cloned.1.call-start = ((), (), s32[]{:S(2)}) async-start(), calls=%async_computation.23 | async-start | bytes 1024000
  817.1 150.5 %copy-start.1 = (bf16[800,1600]{1,0:T(8,128)(2,1)S(1)}, bf16[800,1600]{1,0:T(8,128)(2,1)}, u32[]{:S(2)}) copy-start(bf16[800,1600]{1,0:T(8,128)(2,1)} %param.25) | copy-start | bytes 7680004
  (10 other events, 14.6 us)
Sparse Core Ops, SparseCore 0:
  10.1 109.8 all-gather.11
  122.2 94.1 all-gather.7
  223.0 113.7 all-gather.9
  338.7 62.2 all-gather.13
  404.4 107.0 reduce-scatter.24
  515.4 75.6 reduce-scatter.26
  593.6 35.5 reduce-scatter.22
  632.0 38.7 reduce-scatter.32
  674.4 102.3 reduce-scatter.28
  780.5 123.8 reduce-scatter.34
  906.9 32.6 reduce-scatter.20
  942.2 23.4 reduce-scatter.30

commit v2 on v1

v2 whole, which is shorter than its diff:
```python
import functools

import jax
import jax.numpy as jnp
from jax import lax
from jax.experimental import pallas as pl
from jax.experimental.pallas import tpu as pltpu
from jax.sharding import PartitionSpec as P

HEAD_DIM = 64
HEAD_COLS = 3 * HEAD_DIM
EPSILON = 1e-05
FLOOR_SCORE = -1e30
SCALE = HEAD_DIM**-0.5
BF = jnp.bfloat16
F32 = jnp.float32
VMEM_LIMIT = 56 << 20
COST = 1.6e8


def dot_nn(a, b):
    return lax.dot_general(a, b, (((1,), (0,)), ((), ())), preferred_element_type=F32)


def dot_nt(a, b):
    return lax.dot_general(a, b, (((1,), (1,)), ((), ())), preferred_element_type=F32)


def dot_tn(a, b):
    return lax.dot_general(a, b, (((0,), (0,)), ((), ())), preferred_element_type=F32)


def shape_of(dims, kind):
    return jax.ShapeDtypeStruct(dims, kind)


def whole(*dims):
    return pl.BlockSpec(dims, lambda *_: (0,) * len(dims))


def call(
    kernel, table, operands, outs, scratch=(), name=None, us=1, in_specs=None, out_specs=None, grid=(1,), wait=()
):
    count, wait = 1 + len(operands), jax.tree.leaves(wait)

    def body(*refs):
        kernel(*refs[:count], *refs[count + len(wait) :])

    return pl.pallas_call(
        body,
        grid_spec=pltpu.PrefetchScalarGridSpec(
            num_scalar_prefetch=1,
            grid=grid,
            in_specs=(in_specs or [whole(*a.shape) for a in operands])
            + [pl.BlockSpec(memory_space=pl.ANY)] * len(wait),
            out_specs=out_specs or [whole(*o.shape) for o in outs],
            scratch_shapes=list(scratch),
        ),
        out_shape=list(outs),
        compiler_params=pltpu.CompilerParams(vmem_limit_bytes=VMEM_LIMIT),
        cost_estimate=pl.CostEstimate(flops=int(us * COST), bytes_accessed=1 << 16, transcendentals=0),
        name=name,
    )(table, *operands, *wait)


def steps(count, unrolled, body, carry):
    if unrolled:
        for j in range(count):
            carry = body(j, carry)
        return carry
    return lax.fori_loop(0, count, body, carry)


def rows_of(index, size):
    if isinstance(index, int):
        return pl.ds(index * size, size)
    return pl.ds(pl.multiple_of(index * size, size), size)


def causal(tile):
    key_pos = lax.broadcasted_iota(jnp.int32, (tile, tile), 0)
    query_pos = lax.broadcasted_iota(jnp.int32, (tile, tile), 1)
    return key_pos <= query_pos


def forward_kernel(tile, unrolled, table, x_ref, low_ref, full_ref, log_ref, value_t):
    tiles = x_ref.shape[0] // tile
    for head in range(2):
        base = head * HEAD_COLS
        k_cols = pl.ds(base + HEAD_DIM, HEAD_DIM)
        out_cols = pl.ds(head * HEAD_DIM, HEAD_DIM)

        def turn(j, carry):
            value_t[j] = x_ref[rows_of(j, tile), pl.ds(base + 2 * HEAD_DIM, HEAD_DIM)].T
            return carry

        steps(tiles, unrolled, turn, 0)

        def query_tile(i, carry):
            rows = rows_of(i, tile)
            query = x_ref[rows, pl.ds(base, HEAD_DIM)] * jnp.asarray(SCALE, BF)

            def add(j, state, masked):
                top, total, acc = state
                scores = dot_nt(x_ref[rows_of(j, tile), k_cols], query)
                if masked:
                    scores = jnp.where(causal(tile), scores, FLOOR_SCORE)
                new_top = jnp.maximum(top, jnp.max(scores, axis=0, keepdims=True))
                probs = jnp.exp(scores - new_top)
                fade = jnp.exp(top - new_top)
                total = total * fade + jnp.sum(probs, axis=0, keepdims=True)
                acc = acc * fade + dot_nn(value_t[j], probs.astype(BF))
                return new_top, total, acc

            state = (
                jnp.full((1, tile), FLOOR_SCORE, F32),
                jnp.zeros((1, tile), F32),
                jnp.zeros((HEAD_DIM, tile), F32),
            )
            state = steps(i, unrolled, lambda j, s: add(j, s, False), state)
            top, total, acc = add(i, state, True)
            result = (acc / total).T
            low_ref[rows, out_cols] = result.astype(BF)
            full_ref[rows, out_cols] = result
            log_ref[0, pl.ds(head, 1), rows] = top + jnp.log(total)
            return carry

        steps(tiles, unrolled, query_tile, 0)


def backward_kernel(
    tile, unrolled, table, x_ref, grad_ref, full_ref, log_ref, dx_ref, sum_ref, key_t, key_acc, value_acc
):
    tiles = x_ref.shape[0] // tile
    for head in range(2):
        base = head * HEAD_COLS
        q_cols = pl.ds(base, HEAD_DIM)
        k_cols = pl.ds(base + HEAD_DIM, HEAD_DIM)
        v_cols = pl.ds(base + 2 * HEAD_DIM, HEAD_DIM)
        out_cols = pl.ds(head * HEAD_DIM, HEAD_DIM)

        def turn(j, carry):
            key_t[j] = x_ref[rows_of(j, tile), k_cols].T
            return carry

        steps(tiles, unrolled, turn, 0)
        key_acc[...] = jnp.zeros_like(key_acc)
        value_acc[...] = jnp.zeros_like(value_acc)

        def query_tile(i, query_sum):
            rows = rows_of(i, tile)
            query = x_ref[rows, q_cols] * jnp.asarray(SCALE, BF)
            grad = grad_ref[rows, out_cols]
            delta = jnp.sum((grad.astype(F32) * full_ref[rows, out_cols]).T, axis=0, keepdims=True)
            log_row = log_ref[0, pl.ds(head, 1), rows]

            def add(j, acc, masked):
                key_rows = rows_of(j, tile)
                scores = dot_nt(x_ref[key_rows, k_cols], query)
                probs = jnp.exp(scores - log_row)
                if masked:
                    probs = jnp.where(causal(tile), probs, 0.0)
                grad_probs = dot_nt(x_ref[key_rows, v_cols], grad)
                grad_scores = (probs * (grad_probs - delta)).astype(BF)
                value_acc[key_rows, :] += dot_nn(probs.astype(BF), grad)
                key_acc[key_rows, :] += dot_nn(grad_scores, query)
                return acc + dot_nn(key_t[j], grad_scores)

            acc = jnp.zeros((HEAD_DIM, tile), F32)
            acc = steps(i, unrolled, lambda j, s: add(j, s, False), acc)
            acc = add(i, acc, True)
            result = acc.T * SCALE
            dx_ref[rows, q_cols] = result.astype(BF)
            return query_sum + jnp.sum(result, axis=0, keepdims=True)

        query_sum = steps(tiles, unrolled, query_tile, jnp.zeros((1, HEAD_DIM), F32))
        dx_ref[:, k_cols] = key_acc[...].astype(BF)
        dx_ref[:, v_cols] = value_acc[...].astype(BF)
        sum_ref[0, :, q_cols] = query_sum
        sum_ref[0, :, k_cols] = jnp.sum(key_acc[...], axis=0, keepdims=True)
        sum_ref[0, :, v_cols] = jnp.sum(value_acc[...], axis=0, keepdims=True)


def attention_forward(projected, table, heads):
    length = projected.shape[0]
    tile = min(256, length)
    tiles, pairs = length // tile, heads // 2
    wide, narrow = 2 * HEAD_COLS, 2 * HEAD_DIM
    columns = lambda g, t: (0, g)
    return call(
        functools.partial(forward_kernel, tile, tiles <= 4),
        table,
        [projected],
        [
            shape_of((length, heads * HEAD_DIM), BF),
            shape_of((length, heads * HEAD_DIM), F32),
            shape_of((pairs, 2, length), F32),
        ],
        grid=(pairs,),
        in_specs=[pl.BlockSpec((length, wide), columns)],
        out_specs=[
            pl.BlockSpec((length, narrow), columns),
            pl.BlockSpec((length, narrow), columns),
            pl.BlockSpec((1, 2, length), lambda g, t: (g, 0, 0)),
        ],
        scratch=[pltpu.VMEM((tiles, HEAD_DIM, tile), BF)],
        us=15,
        name="attention_forward",
    )


def attention_backward(projected, grads, full, logs, table, heads, wait):
    length = projected.shape[0]
    tile = min(256, length)
    tiles, pairs = length // tile, heads // 2
    wide, narrow = 2 * HEAD_COLS, 2 * HEAD_DIM
    columns = lambda g, t: (0, g)
    return call(
        functools.partial(backward_kernel, tile, tiles <= 4),
        table,
        [projected, grads, full, logs],
        [shape_of((length, heads * HEAD_COLS), BF), shape_of((pairs, 1, wide), F32)],
        grid=(pairs,),
        in_specs=[
            pl.BlockSpec((length, wide), columns),
            pl.BlockSpec((length, narrow), columns),
            pl.BlockSpec((length, narrow), columns),
            pl.BlockSpec((1, 2, length), lambda g, t: (g, 0, 0)),
        ],
        out_specs=[
            pl.BlockSpec((length, wide), columns),
            pl.BlockSpec((1, 1, wide), lambda g, t: (g, 0, 0)),
        ],
        scratch=[
            pltpu.VMEM((tiles, HEAD_DIM, tile), BF),
            pltpu.VMEM((length, HEAD_DIM), F32),
            pltpu.VMEM((length, HEAD_DIM), F32),
        ],
        us=14,
        wait=wait,
        name="attention_backward",
    )


def norm_stats(rows):
    mean = jnp.mean(rows, axis=-1, keepdims=True)
    centred = rows - mean
    variance = jnp.mean(centred * centred, axis=-1, keepdims=True)
    inverse = lax.rsqrt(variance + EPSILON)
    return centred * inverse, inverse


def norm_back(grad, xhat, inverse, gain):
    h = grad * gain
    return inverse * (
        h - jnp.mean(h, axis=-1, keepdims=True) - xhat * jnp.mean(h * xhat, axis=-1, keepdims=True)
    )


ROOT = 0.7978845608028654
CUBE = 0.044715


def gelu_both(hidden):
    square = hidden * hidden
    bent = jnp.tanh(ROOT * hidden * (1.0 + CUBE * square))
    half = 0.5 * (1.0 + bent)
    slope = half + 0.5 * hidden * (1.0 - bent * bent) * ROOT * (1.0 + 3.0 * CUBE * square)
    return hidden * half, slope


def project_kernel(table, gain, shift, bias, weight, tokens, normed, projected, kept):
    length = tokens.shape[0]
    chunk = min(256, length)
    for first in range(0, length, chunk):
        rows = slice(first, first + chunk)
        xhat, _ = norm_stats(tokens[rows, :].astype(F32))
        kept[rows, :] = xhat.astype(BF)
        normed[rows, :] = (xhat * gain[...] + shift[...]).astype(BF)
        projected[rows, :] = (dot_nn(normed[rows, :], weight[...]) + bias[...]).astype(BF)


def unproject_kernel(shards, table, grad, weight, xhat, *refs):
    others, blocks, (sums, rows) = refs[:shards], refs[shards : 2 * shards], refs[2 * shards :]
    length = rows.shape[0]
    span, chunk = length // shards, min(256, length)
    sums[...] = jnp.zeros_like(sums)
    for first in range(0, length, chunk):
        share = dot_nt(grad[first : first + chunk, :], weight[...])
        rows[first : first + chunk, :] = share.astype(BF)
        sums[0:1, :] += jnp.sum(share * xhat[first : first + chunk, :].astype(F32), axis=0, keepdims=True)
        sums[1:2, :] += jnp.sum(share, axis=0, keepdims=True)
    for r in range(shards):
        blocks[r][:span, :] = rows[rows_of(table[r], span), :]
        blocks[r][span:, :] = others[r][...]


def mix_kernel(shards, table, tokens, weight, bias, gain, shift, heads, attended, mixed, normed, spread):
    cols, width = heads.shape[2], attended.shape[1]
    for s in range(shards):
        spread[:, s * cols : (s + 1) * cols] = heads[s]
    attended[...] = spread[:, :width]
    mixed[...] = tokens[...].astype(F32) + dot_nn(attended[...], weight[...]) + bias[...]
    xhat, _ = norm_stats(mixed[...])
    normed[...] = (xhat * gain[...] + shift[...]).astype(BF)


def unmix_kernel(shards, table, first, second, third, mixed, cotangent, weight, gain, *refs):
    grad_mixed, low, sums, pieces, spread = refs
    cols, (span, width) = pieces.shape[2], low.shape
    grad = first[...].astype(F32) + second[...].astype(F32) + third[...].astype(F32)
    xhat, inverse = norm_stats(mixed[...])
    full = cotangent[...].astype(F32) + norm_back(grad, xhat, inverse, gain[...])
    grad_mixed[...] = full
    low[...] = full.astype(BF)
    sums[0:1, :] = jnp.sum(grad * xhat, axis=0, keepdims=True)
    sums[1:2, :] = jnp.sum(grad, axis=0, keepdims=True)
    sums[2:3, :] = jnp.sum(full, axis=0, keepdims=True)
    spread[:, width:] = jnp.zeros_like(spread[:, width:])
    spread[:, :width] = dot_nt(low[...], weight[...]).astype(BF)
    for s in range(shards):
        pieces[s] = spread[:, s * cols : (s + 1) * cols]


def mlp_kernel(shards, group, table, fc, bias, out, *refs):
    blocks, cotangents, refs = refs[:shards], refs[shards : shards + group], refs[shards + group :]
    act, low, cots, sums, shares, results, normed = refs
    step = pl.program_id(0)
    span = blocks[0].shape[0]
    for first in range(0, shards, group):

        @pl.when(step == first // group)
        def _(first=first):
            for i in range(group):
                normed[i * span : (i + 1) * span, :] = blocks[first + i][...]

    for i in range(group):
        cots[i * span : (i + 1) * span, :] = cotangents[i][0]
    hidden = dot_nn(normed[...], fc[...]) + bias[...]
    activated, slope = gelu_both(hidden)
    act[...] = activated.astype(BF)
    grad = dot_nt(cots[...], out[...]) * slope
    total = jnp.sum(grad, axis=0, keepdims=True)

    @pl.when(step == 0)
    def _():
        sums[...] = total

    @pl.when(step > 0)
    def _():
        sums[...] += total

    low[...] = grad.astype(BF)
    share = dot_nt(low[...], fc[...]).astype(BF)
    result = dot_nn(act[...], out[...]).astype(BF)
    for i in range(group):
        shares[i] = share[i * span : (i + 1) * span, :]
        results[i] = result[i * span : (i + 1) * span, :]


def mlp_part(blocks, cotangent, fc, bias, out, table):
    shards = len(blocks)
    span, width = blocks[0].shape
    rows, units = shards * span, fc.shape[1]
    group = min(shards, max(1, 512 // span))
    cotangent = cotangent.reshape(shards, span, width)
    own = lambda i: pl.BlockSpec((1, span, width), lambda g, t: (t[g * group + i], 0, 0))
    rows_at = lambda cols: pl.BlockSpec((group * span, cols), lambda g, t: (g, 0))
    return call(
        functools.partial(mlp_kernel, shards, group),
        table,
        [fc, bias, out, *blocks] + [cotangent] * group,
        [shape_of((rows, units), BF)] * 2
        + [
            shape_of((rows, width), BF),
            shape_of((1, units), F32),
            shape_of((shards, span, width), BF),
            shape_of((shards, span, width), BF),
        ],
        grid=(shards // group,),
        in_specs=[whole(*a.shape) for a in (fc, bias, out, *blocks)] + [own(i) for i in range(group)],
        out_specs=[
            rows_at(units),
            rows_at(units),
            rows_at(width),
            whole(1, units),
            pl.BlockSpec((group, span, width), lambda g, t: (g, 0, 0)),
            pl.BlockSpec((group, span, width), lambda g, t: (g, 0, 0)),
        ],
        scratch=[pltpu.VMEM((group * span, width), BF)],
        us=15,
        name="mlp",
    )


def weight_kernel(shards, batches, row_blocks, count, table, *refs):
    lefts, rights, refs = refs[:count], refs[count:-batches], refs[-batches:]
    left = jnp.concatenate([v[...] for v in lefts])
    right = jnp.concatenate([v[...] for v in rights])
    product = dot_tn(left, right).astype(BF)
    cols = product.shape[1] // batches
    size = product.shape[0] // row_blocks
    for member in range(batches):

        @pl.when(table[shards] == member)
        def _(member=member):
            for apart in range(batches):
                first = (member ^ apart) * cols
                for s in range(row_blocks):
                    refs[apart][s] = product[s * size : (s + 1) * size, first : first + cols]


def weight_shares(lefts, rights, table, shards, batches, row_blocks, name, wait=()):
    rows, cols = lefts[0].shape[1], rights[0].shape[1]
    length = sum(v.shape[0] for v in lefts)
    dims = (row_blocks, rows // row_blocks, cols // batches)
    return call(
        functools.partial(weight_kernel, shards, batches, row_blocks, len(lefts)),
        table,
        [*lefts, *rights],
        [shape_of(dims, BF)] * batches,
        us=9,
        wait=wait,
        name=name,
    )


def pack_kernel(shards, batches, ranges, table, weight, *refs):
    out, rows = refs[-1], weight.shape[0]
    for extra in refs[:-1]:
        count = (out.shape[1] - rows) // extra.shape[0]
        size = extra.shape[1] // count
        for shard in range(shards):
            for i in range(extra.shape[0]):
                for j in range(count):
                    at = rows + i * count + j
                    out[shard, at : at + 1, :size] = extra[i : i + 1, j * size : (j + 1) * size]
    for member in range(batches):

        @pl.when(table[shards] == member)
        def _(member=member):
            for shard in range(shards):
                at = 0
                for first, size in ranges(shard, member):
                    if first is None:
                        out[shard, :rows, at : at + size] = jnp.zeros((rows, size), BF)
                    else:
                        out[shard, :rows, at : at + size] = weight[:, first : first + size]
                    at += size


def pack(weight, table, shards, batches, cols, ranges, extra=(), wait=()):
    rows = weight.shape[0] + sum(v.shape[0] * -(-v.shape[1] // cols) for v in extra)
    return call(
        functools.partial(pack_kernel, shards, batches, ranges),
        table,
        [weight, *extra],
        [shape_of((shards, rows, cols), BF)],
        us=3.5,
        wait=wait,
        name="pack",
    )[0]


def assemble_kernel(shards, batches, rows, table, *refs):
    parts, out = refs[:batches], refs[batches]
    blocks, _, cols = parts[0].shape
    for member in range(batches):

        @pl.when(table[shards] == member)
        def _(member=member):
            for apart in range(batches):
                at = (member ^ apart) * cols
                for block in range(blocks):
                    out[block * rows : (block + 1) * rows, at : at + cols] = parts[apart][block, :rows, :]


def assemble(parts, table, shards, rows, wait=()):
    blocks, _, cols = parts[0].shape
    return call(
        functools.partial(assemble_kernel, shards, len(parts), rows),
        table,
        parts,
        [shape_of((blocks * rows, len(parts) * cols), BF)],
        us=5,
        wait=wait,
        name="assemble",
    )[0]


def join_kernel(table, source, out):
    out[...] = source[...]


def join(source, table, wait):
    shards, rows, cols = source.shape
    return call(
        join_kernel,
        table,
        [source],
        [shape_of(source.shape, BF)],
        grid=(shards,),
        in_specs=[pl.BlockSpec((1, rows, cols), lambda g, t: (g, 0, 0))],
        out_specs=[pl.BlockSpec((1, rows, cols), lambda g, t: (t[g], 0, 0))],
        us=4,
        wait=wait,
        name="join",
    )[0]


def proj_grad_kernel(shards, batches, table, *refs):
    lefts, rights, refs = refs[:batches], refs[batches : 2 * batches], refs[2 * batches :]
    blocks, quarter, product = refs[:-2], refs[-2], refs[-1]
    span, cols = rights[0].shape[0], quarter.shape[1]
    for member in range(batches):

        @pl.when(table[shards] == member)
        def _(member=member):
            for i in range(batches):
                quarter[i * span : (i + 1) * span, :] = rights[i][:, member * cols : (member + 1) * cols]

    left = jnp.concatenate([v[...] for v in lefts])
    result = dot_tn(left, quarter[...]).astype(BF)
    rows = result.shape[0] // shards
    piece = -(-rows // batches)
    product[...] = jnp.zeros_like(product)
    for s in range(shards):
        for i in range(batches):
            size = min(piece, rows - i * piece)
            first = s * rows + i * piece
            product[s, :size, i * cols : (i + 1) * cols] = result[first : first + size, :]
    for r in range(shards):
        blocks[r][...] = product[table[r]]


def proj_grad(lefts, rights, table, shards, span):
    batches, rows = len(lefts), lefts[0].shape[1]
    width = rights[0].shape[1]
    piece = -(-(rows // shards) // batches)
    dims = (piece + -(span + piece) % 8, width)
    return call(
        functools.partial(proj_grad_kernel, shards, batches),
        table,
        [*lefts, *rights],
        [shape_of(dims, BF)] * shards,
        scratch=[
            pltpu.VMEM((batches * lefts[0].shape[0], width // batches), BF),
            pltpu.VMEM((shards, *dims), BF),
        ],
        us=6,
        name="proj_grad",
    )


def copy_kernel(shards, batches, copies, table, source, out):
    for member in range(batches):

        @pl.when(table[shards] == member)
        def _(member=member):
            for block, first, to_block, to, size in copies(member):
                piece = source[block, :, first : first + size].astype(out.dtype)
                out[to_block, :, to : to + size] = piece


def copy_columns(source, table, shards, batches, dims, kind, copies):
    return call(
        functools.partial(copy_kernel, shards, batches, copies),
        table,
        [source],
        [shape_of(dims, kind)],
        us=4,
        name="copy_columns",
    )[0]


def cut(value):
    rows = value.shape[-2]
    if rows % 8:
        return value
    groups = max(g for g in range(1, 33) if rows // 8 % g == 0)
    return value.reshape(*value.shape[:-2], rows // 8 // groups, groups, 8, value.shape[-1])


def permute(value, axis, pairs):
    return lax.ppermute(cut(value), axis, pairs).reshape(value.shape)


def gate_kernel(count, total, *refs):
    outs = refs[-total:]
    for i in range(count):
        outs[i][...] = (refs[i][...].astype(F32) + refs[total + i][...].astype(F32)).astype(BF)


def gate(values, *others, parts=()):
    values, others, parts = list(values), jax.tree.leaves(others), list(parts)
    if not values:
        return []
    count, total = len(parts), len(values)
    anywhere = pl.BlockSpec(memory_space=pl.ANY)
    blocks = [pl.BlockSpec(memory_space=pltpu.VMEM)] * count
    return pl.pallas_call(
        functools.partial(gate_kernel, count, total),
        in_specs=blocks + [anywhere] * (total - count) + blocks + [anywhere] * len(others),
        out_specs=blocks + [anywhere] * (total - count),
        out_shape=[shape_of(v.shape, v.dtype) for v in values],
        input_output_aliases={i: i for i in range(count, total)},
        name="gate",
    )(*values, *parts, *others)


def after(value, *others):
    return gate([value], *others)[0]


class Rounds:
    def __init__(self):
        self.chains, self.mark = [], None

    def add(self, chain):
        self.chains.append([chain, None])

    def end(self, start, parts=()):
        pending, alive = [], []
        for chain, gated in self.chains:
            try:
                pending.append(list(chain.send(gated)))
                alive.append(chain)
            except StopIteration:
                pass
        values = list(start())
        out = gate(values + [v for p in pending for v in p], parts=parts)
        at, self.chains = len(values), []
        for chain, p in zip(alive, pending):
            self.chains.append([chain, out[at : at + len(p)]])
            at += len(p)
        if out:
            self.mark = out[0]
        return out[: len(values)]

    def finish(self):
        while self.chains:
            self.end(lambda: [])


class Ring:
    def __init__(self, size, rounds):
        self.size, self.rounds = size, rounds
        self.order = list(range(0, size, 2)) + list(range(size - 1, 0, -2))

    def shift(self, value, by):
        pairs = [(self.order[i], self.order[(i + by) % self.size]) for i in range(self.size)]
        return permute(value, "seq", pairs)

    def both(self, right, left):
        return [self.shift(v, 1) for v in right] + [self.shift(v, -1) for v in left]

    def gather(self, value):
        got = [value] * self.size
        right = left = value
        for far in range(1, self.size // 2 + 1):
            left = left if far < self.size - far else []
            came = self.rounds.end(lambda: self.both(right, left))
            right, left = came[: len(value)], came[len(value) :]
            got[self.size - far] = right
            if left:
                got[far] = left
        return got

    def scatter_sum(self, parts):
        size = self.size
        right, left = [parts[size // 2]], []
        for far in range(size // 2 - 1, -1, -1):
            adds = [] if not far else [parts[far]] + [parts[size - far]] * len(left)
            right, *left = self.rounds.end(lambda: self.both(right, left), adds)
            right = [right]
            if far and not left:
                left = [parts[size - far]]
        return right[0], left[0], parts[0]


def add(a, b):
    return (a.astype(F32) + b.astype(F32)).astype(BF)


def swap_blocks(value, axis="seq"):
    return lax.all_to_all(cut(value), axis, 0, 0, tiled=True).reshape(value.shape)


def over_batch(value, batches, apart):
    return permute(value, "batch", [(b, b ^ apart) for b in range(batches)])


def batch_gather_steps(value, batches):
    parts, bit = {0: value}, batches // 2
    while bit:
        came = {apart ^ bit: over_batch(part, batches, bit) for apart, part in parts.items()}
        parts.update(zip(came, (yield list(came.values()))))
        bit //= 2
    return [parts[apart] for apart in range(batches)]


def vector_kernel(shards, table, *refs):
    *rows, last, out = refs
    at = 0
    for ref in rows:
        size = ref.shape[1] // shards
        for i in range(ref.shape[0]):
            for s in range(shards):
                out[s, :, at : at + size] = ref[i : i + 1, s * size : (s + 1) * size]
            at += size
    for i in range(last.shape[0]):
        for s in range(shards):
            out[s, :, at : at + last.shape[2]] = last[i]
        at += last.shape[2]


def cut_vectors(rows, last, table, shards):
    cols = sum(v.size for v in rows) // shards + last.size
    return call(
        functools.partial(vector_kernel, shards),
        table,
        [*rows, last],
        [shape_of((shards, 1, cols), F32)],
        us=3,
        name="vectors",
    )[0]


def per_device(
    shards,
    batches,
    tokens,
    ln1_gain,
    ln1_bias,
    qkv_weight,
    qv_bias,
    proj_weight,
    proj_bias,
    ln2_gain,
    ln2_bias,
    fc_weight,
    fc_bias,
    out_weight,
    out_bias,
    cotangent,
):
    _, span, width = tokens.shape
    head_count = width // HEAD_DIM
    heads = -(-head_count // shards)
    heads += heads % 2
    padded = heads * shards
    length = span * shards
    units = fc_bias.shape[0]
    part = width // shards
    me, member = lax.axis_index("seq"), lax.axis_index("batch")
    rounds = Rounds()
    ring = Ring(shards, rounds)
    place = jnp.where(me % 2 == 0, me // 2, shards - 1 - me // 2)
    place = (place + jnp.arange(shards, dtype=jnp.int32)) % shards
    order = jnp.where(place < shards // 2, 2 * place, 2 * shards - 2 * place - 1)
    table = jnp.concatenate([order, member[None]]).astype(jnp.int32)
    row = lambda v: v.reshape(1, -1).astype(F32)

    slice_cols = heads * HEAD_COLS
    quarter = slice_cols // batches
    fc_quarter = units // batches

    def head_ranges(shard, b):
        found = []
        for col in range(shard * slice_cols + b * quarter, shard * slice_cols + (b + 1) * quarter):
            head, kind, at = col // HEAD_COLS, col % HEAD_COLS // HEAD_DIM, col % HEAD_DIM
            first = kind * width + head * HEAD_DIM + at if head < head_count else None
            if found and first is not None and found[-1][0] is not None and first == sum(found[-1]):
                found[-1] = (found[-1][0], found[-1][1] + 1)
            elif found and first is None and found[-1][0] is None:
                found[-1] = (None, found[-1][1] + 1)
            else:
                found.append((first, 1))
        return found

    def fc_ranges(shard, b):
        return [(shard * units + b * fc_quarter, fc_quarter)]

    own_tokens, own_cot = tokens[0], cotangent[0]
    far = shards // 2
    out_cols = width // batches
    out_cols = width // batches
    proj_part = lax.dynamic_slice_in_dim(proj_weight, member * out_cols, out_cols, 1)
    small = jnp.stack(
        [ln1_gain, ln1_bias, qv_bias[:part], qv_bias[part:], proj_bias, ln2_gain, ln2_bias, out_bias]
    )
    packed = pack(qkv_weight, table, shards, batches, quarter, head_ranges, [small])
    held = {}

    def first_weights():
        (got,) = yield [swap_blocks(packed)]
        held["small"] = got[:, part:, : part // ((got.shape[1] - part) // 8)]
        parts = yield from batch_gather_steps(got, batches)
        held["qkv"] = assemble(parts, table, shards, part)
        held["qkv"] = (yield [held["qkv"]])[0]

    def fc_weights():
        yield []
        got = pack(fc_weight, table, shards, batches, fc_quarter, fc_ranges, wait=[rounds.mark])
        (got,) = yield [got]
        while "qkv" not in held:
            yield []
        got = swap_blocks(after(got, rounds.mark))
        yield []
        (got,) = yield [got]
        while "normed_two" not in held:
            yield []
        came = over_batch(after(got, rounds.mark), batches, batches // 2)
        yield []
        parts = {0: got, batches // 2: (yield [came])[0]}
        bit = batches // 4
        while bit:
            came = {apart ^ bit: over_batch(p, batches, bit) for apart, p in parts.items()}
            parts.update(zip(came, (yield list(came.values()))))
            bit //= 2
        parts = [parts[apart] for apart in range(batches)]
        held["fc"] = (yield [assemble(parts, table, shards, part)])[0]

    rounds.add(first_weights())
    rounds.add(fc_weights())
    all_tokens = lax.all_gather(cut(own_tokens), "seq", axis=0, tiled=True).reshape(length, width)
    while "qkv" not in held:
        rounds.end(lambda: [])
    w_qkv = held["qkv"]
    proj_rows = after(proj_part, all_tokens, rounds.mark)
    proj_rows = lax.all_gather(cut(proj_rows), "seq", axis=0, tiled=True).reshape(shards, part, out_cols)
    small = held["small"].reshape(shards, -1)
    gain_one = row(small[:, :part])
    shift_one = row(small[:, part : 2 * part])
    bias_qv = small[:, 2 * part : 4 * part].reshape(2 * width)
    b_proj = row(small[:, 4 * part : 5 * part])
    gain_two = row(small[:, 5 * part : 6 * part])
    shift_two = row(small[:, 6 * part : 7 * part])
    b_out = row(small[:, 7 * part : 8 * part])
    bias_row = jnp.concatenate([bias_qv[:width], jnp.zeros((width,), BF), bias_qv[width:]])
    bias_heads = jnp.pad(
        bias_row.reshape(3, head_count, HEAD_DIM), ((0, 0), (0, padded - head_count), (0, 0))
    )
    bias_heads = jnp.swapaxes(bias_heads, 0, 1).reshape(1, padded * HEAD_COLS)
    bias_slice = lax.dynamic_slice_in_dim(bias_heads, me * slice_cols, slice_cols, 1).astype(F32)
    def project():
        return call(
            project_kernel,
            table,
            [gain_one, shift_one, bias_slice, w_qkv, all_tokens],
            [
                shape_of((length, width), BF),
                shape_of((length, slice_cols), BF),
                shape_of((length, width), BF),
            ],
            us=11,
            name="project",
        )

    def proj_weights():
        yield []
        yield []
        got = proj_rows
        came = over_batch(after(got, rounds.mark), batches, batches // 2)
        (came,) = yield [came]
        parts = {0: got, batches // 2: came}
        bit = batches // 4
        while bit:
            came = {apart ^ bit: over_batch(p, batches, bit) for apart, p in parts.items()}
            parts.update(zip(came, (yield list(came.values()))))
            bit //= 2
        parts = [parts[apart] for apart in range(batches)]
        held["w_proj"] = (yield [assemble(parts, table, shards, part)])[0]

    rounds.add(proj_weights())
    normed_one, projected, xhat_one = rounds.end(project)
    attended_heads, attended_full, log_total = rounds.end(lambda: attention_forward(projected, table, heads))
    all_cot = lax.all_gather(cut(after(own_cot, proj_rows, rounds.mark)), "seq", axis=0, tiled=True)
    all_cot = all_cot.reshape(length, width)
    (attended_heads,) = rounds.end(
        lambda: [swap_blocks(attended_heads.reshape(shards, span, heads * HEAD_DIM))]
    )
    while "w_proj" not in held:
        rounds.end(lambda: [])
    w_proj = held["w_proj"]
    attended, mixed, normed_two = call(
        functools.partial(mix_kernel, shards),
        table,
        [own_tokens, w_proj, b_proj, gain_two, shift_two, attended_heads],
        [shape_of((span, width), BF), shape_of((span, width), F32), shape_of((span, width), BF)],
        scratch=[pltpu.VMEM((span, padded * HEAD_DIM), BF)],
        us=6,
        name="mix",
    )

    held["normed_two"] = normed_two
    gathered = {}

    def batch_rows(value, name, flag):
        while flag not in held:
            yield []
        value = after(value, rounds.mark)
        gathered[name] = yield from batch_gather_steps(value, batches)

    rounds.add(batch_rows(attended, "attended", "mlp"))
    normed_blocks = [block for (block,) in ring.gather([normed_two])]
    while "fc" not in held:
        rounds.end(lambda: [])
    w_fc = held["fc"]
    activated, hidden_low, cot_rows, fc_sums, g_two, out_rows = mlp_part(
        normed_blocks, all_cot, w_fc, row(fc_bias), out_weight, table
    )

    shares = functools.partial(weight_shares, table=table, shards=shards, batches=batches)

    def near_sums(found):
        came = yield [over_batch(found[apart ^ 1], batches, 1) for apart in range(0, batches, 2)]
        return [add(found[2 * i], c) for i, c in enumerate(came)]

    def far_sum(kept):
        came = yield [over_batch(kept[1], batches, 2)]
        return add(kept[0], came[0])

    def fc_gradient():
        yield []
        yield []
        found = yield shares(
            normed_blocks, [hidden_low], row_blocks=shards, name="fc_grad", wait=[rounds.mark]
        )
        kept = yield from near_sums(found)
        came = over_batch(after(kept[1], rounds.mark), batches, 2)
        yield []
        share = add(kept[0], *(yield [came]))
        share = swap_blocks(share)
        yield []
        (share,) = yield [share]
        held["fc_grad"] = (yield [swap_blocks(share, "batch")])[0]

    def out_gradient():
        yield []
        yield []
        yield []
        found = yield shares([activated], [cot_rows], row_blocks=1, name="out_grad", wait=[rounds.mark])
        yield []
        kept = yield from near_sums(found)
        came = over_batch(after(kept[1], rounds.mark), batches, 2)
        yield []
        held["out_grad"] = add(kept[0], *(yield [came]))

    def out_result():
        yield []
        (total,) = yield [join(out_rows, table, [rounds.mark])]
        held["out"] = lax.psum_scatter(cut(total), "seq", scatter_dimension=0, tiled=True)

    held["mlp"] = True
    rounds.add(out_result())
    rounds.add(fc_gradient())
    rounds.add(out_gradient())
    g_two = ring.scatter_sum([g_two[r] for r in range(shards)])

    def unmix():
        return call(
            functools.partial(unmix_kernel, shards),
            table,
            [*g_two, mixed, own_cot, w_proj, gain_two],
            [
                shape_of((span, width), F32),
                shape_of((span, width), BF),
                shape_of((3, width), F32),
                shape_of((shards, span, heads * HEAD_DIM), BF),
            ],
            scratch=[pltpu.VMEM((span, padded * HEAD_DIM), BF)],
            us=7,
            name="unmix",
        )

    grad_mixed, mixed_low, norm_sums, grad_messages = rounds.end(unmix)

    rounds.add(batch_rows(mixed_low, "mixed_low", "mlp"))
    (grad_heads,) = rounds.end(lambda: [swap_blocks(grad_messages)])
    held["grad_heads"] = grad_heads
    grad_projected, column_sums = rounds.end(
        lambda: attention_backward(
            projected, grad_heads.reshape(length, -1), attended_full, log_total, table, heads, []
        )
    )
    qkv_kept = rounds.end(
        lambda: shares([normed_one], [grad_projected], row_blocks=shards, name="qkv_grad")
    )
    proj_blocks = proj_grad(gathered["attended"], gathered["mixed_low"], table, shards, span)
    share_cols = 3 * width // batches

    def overlaps(source, target):
        found = []
        for shard in range(shards):
            at = 0
            for first, size in head_ranges(shard, source):
                if first is not None:
                    low = max(first, target * share_cols)
                    high = min(first + size, (target + 1) * share_cols)
                    if low < high:
                        found.append((shard, at + low - first, low - target * share_cols, high - low))
                at += size
        return found

    most = max(sum(o[3] for o in overlaps(q, b)) for q in range(batches) for b in range(batches))
    most = -(-most // 128) * 128

    def outgoing(b):
        copies = []
        for target in range(batches):
            at = 0
            for shard, first, _, size in overlaps(b, target):
                copies.append((shard, first, target, at, size))
                at += size
        return copies

    def incoming(b):
        copies = []
        for source in range(batches):
            at = 0
            for _, _, to, size in overlaps(source, b):
                copies.append((source, at, 0, to, size))
                at += size
        return copies

    def qkv_gradient():
        kept = yield from near_sums(qkv_kept)
        share = yield from far_sum(kept)
        (share,) = yield [swap_blocks(share)]
        share = copy_columns(share, table, shards, batches, (batches, part, most), BF, outgoing)
        (share,) = yield [swap_blocks(share, "batch")]
        held["qkv_grad"] = copy_columns(share, table, shards, batches, (1, part, share_cols), F32, incoming)[0]

    def vector_gradients():
        yield []
        cot_sums = jnp.sum(own_cot.astype(F32), axis=0, keepdims=True)
        rows = cut_vectors([held["norm_one"], norm_sums, cot_sums], column_sums, table, shards)
        (rows,) = yield [lax.all_to_all(rows, "seq", 0, 0, tiled=True)]
        part_sums = jnp.sum(rows[:, :, : 6 * part], axis=0)
        head_sums = rows[:, 0, 6 * part :].reshape(padded, 3, HEAD_DIM)[:head_count]
        qv_sums = jnp.concatenate([head_sums[:, 0], head_sums[:, 2]]).reshape(1, 2 * width)
        qv_sums = lax.dynamic_slice_in_dim(qv_sums, me * 2 * part, 2 * part, 1)
        sums = jnp.concatenate([part_sums, qv_sums, fc_sums], axis=1)
        bit = 1
        while bit < batches:
            (came,) = yield [lax.ppermute(sums, "batch", [(b, b ^ bit) for b in range(batches)])]
            sums = sums + came
            bit *= 2
        held["sums"] = sums[0]

    rounds.add(qkv_gradient())
    rounds.add(vector_gradients())

    def unproject():
        return call(
            functools.partial(unproject_kernel, shards),
            table,
            [grad_projected, w_qkv, xhat_one, *proj_blocks],
            [shape_of((span + proj_blocks[0].shape[0], width), BF)] * shards + [shape_of((2, width), F32)],
            scratch=[pltpu.VMEM((length, width), BF)],
            us=9,
            name="unproject",
        )

    *g_one, held["norm_one"] = rounds.end(unproject)
    total = sum(term.astype(F32) for term in ring.scatter_sum(g_one))
    g_one, pieces = total[:span], -(-part // batches)
    proj_share = [total[span : span + pieces, b * out_cols : (b + 1) * out_cols] for b in range(batches)]
    proj_share = jnp.concatenate(proj_share)[:part]
    xhat, inverse = norm_stats(own_tokens.astype(F32))
    block_out = (mixed + b_out + held["out"].reshape(span, width).astype(F32)).astype(BF)
    input_grad = (grad_mixed + norm_back(g_one, xhat, inverse, gain_one)).astype(BF)
    rounds.finish()

    runs = shards // batches

    def fc_copies(b):
        return [
            (q * runs + run, 0, 0, (run * batches + q) * fc_quarter, fc_quarter)
            for q in range(batches)
            for run in range(runs)
        ]

    fc_share = held["fc_grad"]
    fc_share = copy_columns(fc_share, table, shards, batches, (1, part, runs * units), F32, fc_copies)[0]
    sums = held["sums"]
    vectors = [sums[i * part : (i + 1) * part] for i in range(6)]
    return (
        block_out[None],
        input_grad[None],
        vectors[0],
        vectors[1],
        held["qkv_grad"],
        sums[6 * part : 8 * part],
        proj_share,
        vectors[4],
        vectors[2],
        vectors[3],
        fc_share,
        sums[8 * part : 8 * part + units],
        held["out_grad"][0].astype(F32),
        vectors[5],
    )


def solution(mesh):
    rows = P("batch", "seq", None)
    matrix, vector = P("seq", None), P("seq")
    shared = P("seq", "batch")
    return jax.shard_map(
        functools.partial(per_device, mesh.shape["seq"], mesh.shape["batch"]),
        mesh=mesh,
        in_specs=(
            rows, vector, vector, matrix, vector, matrix, vector,
            vector, vector, matrix, vector, matrix, vector, rows,
        ),
        out_specs=(
            rows, rows, vector, vector, shared, vector, shared,
            vector, vector, vector, shared, vector, shared, vector,
        ),
        check_vma=False,
    )
```

time: 979 us -> 579 us (0.59)
  blocking collectives: 349 us -> 39.1 us
  waiting for transfers between devices: 399 us -> 194 us
  Pallas kernels: 24.1 us -> 174 us
  matrix products: 70.9 us -> 0 us
  starting transfers between devices: 16.9 us -> 74.4 us
  local copies, waits for them, and re-layouts: 83.6 us -> 55.4 us
    unnamed x18 -> x4, waiting for transfers between devices: 196 us -> 0.07 us
    pallas_call x2 -> x56, Pallas kernels: 24.1 us -> 174 us  [the longest x21 159 us: call(): pl.pallas_call(body, grid_spec=pltpu.PrefetchScalarGridSpec(num_scalar_pr...]
    unnamed x2 -> x0, blocking collectives: 150 us -> none
    all_to_all x3 -> x1, blocking collectives: 188 us -> 39.1 us  [swap_blocks(): lax.all_to_all(cut(value), axis, 0, 0, tiled=True).reshape(value.shape)]
    ppermute x0 -> x47, waiting for transfers between devices: none -> 141 us  [the longest x45 141 us: permute(): return lax.ppermute(cut(value), axis, pairs).reshape(value.shape)]
    all_to_all x3 -> x8, waiting for transfers between devices: 124 us -> 49.3 us  [the longest x7 39 us: swap_blocks(): lax.all_to_all(cut(value), axis, 0, 0, tiled=True).reshape(value.shape)]
    dot_general x12 -> x0, matrix products: 70.9 us -> none  [the longest x4 24.4 us: dot_nt(): lax.dot_general(a, b, (((1,), (1,)), ((), ())), preferred_element_type=F32)]
    all_gather x4 -> x3, waiting for transfers between devices: 61 us -> 3.79 us  [the longest x1 3.78 us: per_device(): lax.all_gather(cut(proj_rows), 'seq', axis=0, tiled=True)]
  transfers between devices with their start and end apart: 15 -> 59, of which waited for: 9 -> 26; matrix products, arithmetic and copies ran while one was open for 15% -> 8% of each run, Pallas kernels for 2% -> 30%
where the time goes in v2:
time: 579 us; the launch traced here: 573 us
  waiting for transfers between devices  194 us (34%)
  Pallas kernels  174 us (30%)
  starting transfers between devices  74.4 us (13%)
  local copies, waits for them, and re-layouts  55.4 us (10%)
  blocking collectives  39.1 us (7%)
  other arithmetic  20.4 us (4%)
  between operations  14.7 us (3%)
    pallas_call x21, Pallas kernels, call(): pl.pallas_call(body, grid_spec=pltpu.PrefetchScalarGridSpec(num_scalar_pr...  159 us
    ppermute x45, waiting for transfers between devices, permute(): return lax.ppermute(cut(value), axis, pairs).reshape(value.shape)  141 us
    all_to_all x1, blocking collectives, swap_blocks(): lax.all_to_all(cut(value), axis, 0, 0, tiled=True).reshape(value.shape)  39.1 us
    all_to_all x7, waiting for transfers between devices, swap_blocks(): lax.all_to_all(cut(value), axis, 0, 0, tiled=True).reshape(value.shape)  39 us
    ppermute x45, starting transfers between devices, permute(): return lax.ppermute(cut(value), axis, pairs).reshape(value.shape)  38.3 us
    unnamed x171, local copies, waits for them, and re-layouts  36.9 us
    all_to_all x7, starting transfers between devices, swap_blocks(): lax.all_to_all(cut(value), axis, 0, 0, tiled=True).reshape(value.shape)  28.9 us
    pallas_call x35, Pallas kernels, gate(): pl.pallas_call(functools.partial(gate_kernel, count, total), in_specs=blo...  14.8 us
  transfers between devices with their start and end apart: 59, of which 26 were waited for; matrix products, arithmetic and copies ran while one was open for 8% of the time, Pallas kernels for 30%

profile of v2, /device:TPU:0, one launch (start us, length us, event | category | flops | bytes accessed | tf_op | source)
XLA Modules:
  0.0 572.6 jit_solution(14056523908368239962)
XLA Ops:
  18.8 39.1 %all_to_all.45 = bf16[8,1,27,8,192]{4,3,2,1,0:T(8,128)(2,1)} all-to-all(bf16[8,1,27,8,192]{4,3,2,1,0:T(8,128)(2,1)} %bitcast.220), channel_id=1, replica_groups=mesh['batch'=4,'seq'=8] {'seq'}, dimensions={0} | all-to-all | bytes 1327104 | tf_op jit(solution)/shard_map/all_to_all | solution.py:686
  63.1 16.5 %collective-permute-done.1 = bf16[8,1,27,8,192]{4,3,2,0,1:T(8,128)(2,1)S(1)} collective-permute-done((bf16[8,1,27,8,192]{4,3,2,0,1:T(8,128)(2,1)}, bf16[8,1,27,8,192]{4,3,2,0,1:T(8,128)(2,1)S(1)}, u32[]{:S(2)}, u32[]{:S(2)}) %collective-permute-start.1) | collective-permute-done | bytes 663584 | tf_op jit(solution)/shard_map/ppermute | solution.py:585
  84.1 4.5 assemble.3.refs_4_.refs_2_
  101.0 10.4 %project.1 = (bf16[1024,1600]{1,0:T(8,128)(2,1)}, bf16[1024,768]{1,0:T(8,128)(2,1)}, bf16[1024,1600]{1,0:T(8,128)(2,1)}) custom-call(s32[9]{0:T(128)} %pad_add_fusion.refs_0_, f32[1,1600]{1,0:T(1,128)} %reshape.594.refs_1_, f32[1,1600]{1,0:T(1,128)} %reshape.595.refs_2_, f32[1,768]{1,0:T(1,128)} %dynamic-slice_convert_fusion.refs_3_, ...), custom_call_target="tpu_custom_call" | custom-call | flops 1760000000 | bytes 65536 | tf_op jit(solution)/shard_map/project/pallas_call | solution.py:49
  111.4 12.2 %all-to-all-done.1 = bf16[8,1,25,8,200]{4,3,2,1,0:T(8,128)(2,1)S(1)} async-done(((bf16[8,1,25,8,200]{4,3,2,1,0:T(8,128)(2,1)}), bf16[8,1,25,8,200]{4,3,2,1,0:T(8,128)(2,1)S(1)}, u32[]{:S(2)}, u32[]{:S(2)}) %all-to-all-start.1) | async-done | bytes 640032 | tf_op jit(solution)/shard_map/all_to_all | solution.py:686
  124.5 14.9 %attention_forward.1 = (bf16[1024,256]{1,0:T(8,128)(2,1)}, f32[1024,256]{1,0:T(8,128)}, f32[2,2,1024]{2,1,0:T(2,128)}) custom-call(s32[9]{0:T(128)} %pad_add_fusion.refs_0_, bf16[1024,768]{1,0:T(8,128)(2,1)} %get-tuple-element.162.refs_1_), custom_call_target="tpu_custom_call" | custom-call | flops 2400000000 | bytes 65536 | tf_op jit(solution)/shard_map/attention_forward/pallas_call | solution.py:49
  151.3 25.9 %all-to-all-done.2 = bf16[8,1,16,8,256]{4,3,2,1,0:T(8,128)(2,1)S(1)} async-done(((bf16[8,1,16,8,256]{4,3,2,1,0:T(8,128)(2,1)}), bf16[8,1,16,8,256]{4,3,2,1,0:T(8,128)(2,1)S(1)}, u32[]{:S(2)}, u32[]{:S(2)}) %all-to-all-start.2) | async-done | bytes 524320 | tf_op jit(solution)/shard_map/all_to_all | solution.py:686
  177.3 5.7 collective-permute-done.4
  186.8 7.5 %assemble.4.refs_0_ = bf16[1600,1600]{1,0:T(8,128)(2,1)} custom-call(s32[9]{0:T(128)} %pad_add_fusion.refs_0_, bf16[8,200,400]{2,1,0:T(8,128)(2,1)} %bitcast.187, bf16[8,200,400]{2,1,0:T(8,128)(2,1)} %get-tuple-element.168.refs_2_, bf16[8,200,400]{2,1,0:T(8,128)(2,1)} %get-tuple-element.167.refs_3_, bf16[8,200,400]{2,1,0:T(8,128)(2,1)} %get-tuple-element.169.refs_4_), custom_call_target="tpu_custom_call" | custom-call | flops 800000000 | bytes 65536 | tf_op jit(solution)/shard_map/assemble/pallas_call | solution.py:49
  194.2 5.6 mix.1
  204.2 16.3 %collective-permute-done.6 = bf16[1,16,8,1600]{3,2,1,0:T(8,128)(2,1)S(1)} collective-permute-done((bf16[1,16,8,1600]{3,2,1,0:T(8,128)(2,1)}, bf16[1,16,8,1600]{3,2,1,0:T(8,128)(2,1)S(1)}, u32[]{:S(2)}, u32[]{:S(2)}) %collective-permute-start.6) | collective-permute-done | bytes 409632 | tf_op jit(solution)/shard_map/ppermute | solution.py:585
  225.6 9.3 %collective-permute-done.8 = bf16[1,16,8,1600]{3,2,1,0:T(8,128)(2,1)S(1)} collective-permute-done((bf16[1,16,8,1600]{3,2,1,0:T(8,128)(2,1)}, bf16[1,16,8,1600]{3,2,1,0:T(8,128)(2,1)S(1)}, u32[]{:S(2)}, u32[]{:S(2)}) %collective-permute-start.8) | collective-permute-done | bytes 409632 | tf_op jit(solution)/shard_map/ppermute | solution.py:585
  238.1 10.4 %collective-permute-done.11 = bf16[1,16,8,1600]{3,2,1,0:T(8,128)(2,1)S(1)} collective-permute-done((bf16[1,16,8,1600]{3,2,1,0:T(8,128)(2,1)}, bf16[1,16,8,1600]{3,2,1,0:T(8,128)(2,1)S(1)}, u32[]{:S(2)}, u32[]{:S(2)}) %collective-permute-start.11) | collective-permute-done | bytes 409632 | tf_op jit(solution)/shard_map/ppermute | solution.py:585
  251.5 5.3 assemble.5.refs_1_
  263.6 22.3 %mlp.1 = (bf16[1024,800]{1,0:T(8,128)(2,1)}, bf16[1024,800]{1,0:T(8,128)(2,1)}, bf16[1024,1600]{1,0:T(8,128)(2,1)}, f32[1,800]{1,0:T(1,128)}, bf16[8,128,1600]{2...) custom-call(s32[9]{0:T(128)} %pad_add_fusion.refs_0_, bf16[1600,800]{1,0:T(8,128)(2,1)} %get-tuple-element.182.refs_1_, ...), custom_call_target="tpu_custom_call" | custom-call | flops 2400000000 | bytes 65536 | tf_op jit(solution)/shard_map/mlp/pallas_call | solution.py:49
  291.4 7.9 %collective-permute-done.16 = bf16[1,16,8,1600]{3,2,1,0:T(8,128)(2,1)S(1)} collective-permute-done((bf16[1,16,8,1600]{3,2,1,0:T(8,128)(2,1)S(1)}, bf16[1,16,8,1600]{3,2,1,0:T(8,128)(2,1)S(1)}, u32[]{:S(2)}, u32[]{:S(2)}) %collective-permute-start.16) | collective-permute-done | bytes 409632 | tf_op jit(solution)/shard_map/ppermute | solution.py:585
  303.0 6.9 %join.1.refs_4_ = bf16[8,128,1600]{2,1,0:T(8,128)(2,1)} custom-call(s32[9]{0:T(128)} %pad_add_fusion.refs_0_, bf16[8,128,1600]{2,1,0:T(8,128)(2,1)} %get-tuple-element.189.refs_1_, bf16[128,1600]{1,0:T(8,128)(2,1)} %get-tuple-element.187.refs_2_), custom_call_target="tpu_custom_call" | custom-call | flops 640000000 | bytes 65536 | tf_op jit(solution)/shard_map/join/pallas_call | solution.py:49
  316.6 9.9 %fc_grad.1 = (bf16[8,200,200]{2,1,0:T(8,128)(2,1)}, bf16[8,200,200]{2,1,0:T(8,128)(2,1)}, bf16[8,200,200]{2,1,0:T(8,128)(2,1)}, bf16[8,200,200]{2,1,0:T(8,128)(2,1)}) custom-call(s32[9]{0:T(128)} %pad_add_fusion.refs_0_, bf16[128,1600]{1,0:T(8,128)(2,1)} %get-tuple-element.172.refs_4_.refs_1_, bf16[128,1600]{1,0:T(8,128)(2,1)} %get-tuple-element.174.refs_5_.refs_2_, ...), custom_call_target="tpu_custom_call" | custom-call | flops 1440000000 | bytes 65536 | tf_op jit(solution)/shard_map/fc_grad/pallas_call | solution.py:49
  332.5 8.9 %out_grad.1 = (bf16[1,800,400]{2,1,0:T(8,128)(2,1)}, bf16[1,800,400]{2,1,0:T(8,128)(2,1)}, bf16[1,800,400]{2,1,0:T(8,128)(2,1)}, bf16[1,800,400]{2,1,0:T(8,128)(2,1)}) custom-call(s32[9]{0:T(128)} %pad_add_fusion.refs_0_, bf16[1024,800]{1,0:T(8,128)(2,1)} %get-tuple-element.202.refs_1_, bf16[1024,1600]{1,0:T(8,128)(2,1)} %get-tuple-element.203.refs_2_, ...), custom_call_target="tpu_custom_call" | custom-call | flops 1440000000 | bytes 65536 | tf_op jit(solution)/shard_map/out_grad/pallas_call | solution.py:49
  345.0 5.7 collective-permute-done.25
  352.0 7.2 %unmix.1 = (f32[128,1600]{1,0:T(8,128)}, bf16[128,1600]{1,0:T(8,128)(2,1)}, f32[3,1600]{1,0:T(4,128)}, bf16[8,128,256]{2,1,0:T(8,128)(2,1)}) custom-call(s32[9]{0:T(128)} %pad_add_fusion.refs_0_, bf16[128,1600]{1,0:T(8,128)(2,1)} %get-tuple-element.208.refs_1_, bf16[128,1600]{1,0:T(8,128)(2,1)} %get-tuple-element.209.refs_2_, ...), custom_call_target="tpu_custom_call" | custom-call | flops 1120000000 | bytes 65536 | tf_op jit(solution)/shard_map/unmix/pallas_call | solution.py:49
  367.0 21.3 %collective-permute-done.31 = bf16[1,16,8,1600]{3,2,1,0:T(8,128)(2,1)S(1)} collective-permute-done((bf16[1,16,8,1600]{3,2,1,0:T(8,128)(2,1)}, bf16[1,16,8,1600]{3,2,1,0:T(8,128)(2,1)S(1)}, u32[]{:S(2)}, u32[]{:S(2)}) %collective-permute-start.31) | collective-permute-done | bytes 409632 | tf_op jit(solution)/shard_map/ppermute | solution.py:585
  393.8 5.8 %all-to-all-start.4 = ((bf16[8,1,25,8,200]{4,3,2,1,0:T(8,128)(2,1)}), bf16[8,1,25,8,200]{4,3,2,1,0:T(8,128)(2,1)S(1)}, u32[]{:S(2)}, u32[]{:S(2)}) async-start(bf16[8,1,25,8,200]{4,3,2,1,0:T(8,128)(2,1)} %fusion.11), calls=%async_computation.5 | async-start | bytes 1638400 | tf_op jit(solution)/shard_map/all_to_all | solution.py:686
  402.3 14.4 %attention_backward.1 = (bf16[1024,768]{1,0:T(8,128)(2,1)}, f32[2,1,384]{2,1,0:T(1,128)}) custom-call(s32[9]{0:T(128)} %pad_add_fusion.refs_0_, bf16[1024,768]{1,0:T(8,128)(2,1)} %get-tuple-element.162.refs_1_, bf16[1024,256]{1,0:T(8,128)(2,1)} %bitcast.204, f32[1024,256]{1,0:T(8,128)} %get-tuple-element.222.refs_3_, f32[2,2,1024]{2,1,0:T(2,128)} %get-tuple-element.223.refs_4_), custom_call_target="tpu_custom_call" | custom-call | flops 2240000000 | bytes 65536 | tf_op jit(solution)/shard_map/attention_backward/pallas_call | solution.py:49
  417.6 8.3 %qkv_grad.1 = (bf16[8,200,192]{2,1,0:T(8,128)(2,1)}, bf16[8,200,192]{2,1,0:T(8,128)(2,1)}, bf16[8,200,192]{2,1,0:T(8,128)(2,1)}, bf16[8,200,192]{2,1,0:T(8,128)(2,1)}) custom-call(s32[9]{0:T(128)} %pad_add_fusion.refs_0_, bf16[1024,1600]{1,0:T(8,128)(2,1)} %get-tuple-element.250.refs_1_, bf16[1024,768]{1,0:T(8,128)(2,1)} %get-tuple-element.227.refs_1_.refs_2_), custom_call_target="tpu_custom_call" | custom-call | flops 1440000000 | bytes 65536 | tf_op jit(solution)/shard_map/qkv_grad/pallas_call | solution.py:49
  431.7 5.2 proj_grad.1
  436.9 9.6 %unproject.1 = (bf16[184,1600]{1,0:T(8,128)(2,1)}, bf16[184,1600]{1,0:T(8,128)(2,1)}, bf16[184,1600]{1,0:T(8,128)(2,1)}, bf16[184,1600]{1,0:T(8,128)(2,1)}, bf16...) custom-call(s32[9]{0:T(128)} %pad_add_fusion.refs_0_, ...), custom_call_target="tpu_custom_call" | custom-call | flops 1440000000 | bytes 65536 | tf_op jit(solution)/shard_map/unproject/pallas_call | solution.py:49
  457.6 4.7 all-to-all-start.6
  462.5 10.3 %all-to-all-done.6.refs_2_ = f32[8,1,1968]{2,1,0:T(1,128)S(1)} async-done(((f32[8,1,1968]{2,1,0:T(1,128)}), f32[8,1,1968]{2,1,0:T(1,128)S(1)}, u32[]{:S(2)}, u32[]{:S(2)}) %all-to-all-start.6) | async-done | bytes 63008 | tf_op jit(solution)/shard_map/all_to_all | solution.py:1039
  478.3 4.9 all-to-all-start.7
  486.3 25.4 %collective-permute-done.40 = bf16[1,23,8,1600]{3,2,1,0:T(8,128)(2,1)S(1)} collective-permute-done((bf16[1,23,8,1600]{3,2,1,0:T(8,128)(2,1)S(1)}, bf16[1,23,8,1600]{3,2,1,0:T(8,128)(2,1)S(1)}, u32[]{:S(2)}, u32[]{:S(2)}) %collective-permute-start.40) | collective-permute-done | bytes 588832 | tf_op jit(solution)/shard_map/ppermute | solution.py:585
  515.9 6.0 %collective-permute-start.42 = (bf16[1,23,8,1600]{3,2,1,0:T(8,128)(2,1)}, bf16[1,23,8,1600]{3,2,1,0:T(8,128)(2,1)}, u32[]{:S(2)}, u32[]{:S(2)}) collective-permute-start(bf16[1,23,8,1600]{3,2,1,0:T(8,128)(2,1)} %bitcast.288), channel_id=1, source_target_pairs={{0,2},{2,4},{4,6},{6,7},{7,5},{5,3},{3,1},{1,0},{8,10},{10,12},{12... | collective-permute-start | bytes 1766408 | tf_op jit(solution)/shard_map/ppermute | solution.py:585
  (387 shorter events, 189.5 us)
Async XLA Ops:
  7.2 84.7 %all-gather.4.cloned.1.call-start = ((), (), s32[]{:S(2)}) async-start(), calls=%async_computation.10 | async-start | bytes 3833856 | tf_op jit(solution)/shard_map/all_gather | solution.py:826
  9.3 133.8 %all-gather.6.cloned.1.call-start = ((), (), s32[]{:S(2)}) async-start(), calls=%async_computation.11 | async-start | bytes 1843200 | tf_op jit(solution)/shard_map/all_gather | solution.py:831
  58.0 21.6 %collective-permute-start.1 = (bf16[8,1,27,8,192]{4,3,2,0,1:T(8,128)(2,1)}, bf16[8,1,27,8,192]{4,3,2,0,1:T(8,128)(2,1)S(1)}, u32[]{:S(2)}, u32[]{:S(2)}) collective-permute-start(bf16[8,1,27,8,192]{4,3,2,0,1:T(8,128)(2,1)} %bitcast.191), channel_id=1, source_target_pairs={{0,16},{8,24},{16,0},{24,8},{1,17},{9,25},{17,1},{25,9},{2,18},{10... | collective-permute-start | bytes 1990664 | tf_op jit(solution)/shard_map/ppermute | solution.py:585
  59.4 21.9 %collective-permute-start = (bf16[8,1,27,8,192]{4,3,2,0,1:T(8,128)(2,1)}, bf16[8,1,27,8,192]{4,3,2,0,1:T(8,128)(2,1)S(1)}, u32[]{:S(2)}, u32[]{:S(2)}) collective-permute-start(bf16[8,1,27,8,192]{4,3,2,0,1:T(8,128)(2,1)} %bitcast.192), channel_id=1, source_target_pairs={{0,8},{8,0},{16,24},{24,16},{1,9},{9,1},{17,25},{25,17},{2,10},{10... | collective-permute-start | bytes 1990664 | tf_op jit(solution)/shard_map/ppermute | solution.py:585
  92.0 31.6 %all-to-all-start.1 = ((bf16[8,1,25,8,200]{4,3,2,1,0:T(8,128)(2,1)}), bf16[8,1,25,8,200]{4,3,2,1,0:T(8,128)(2,1)S(1)}, u32[]{:S(2)}, u32[]{:S(2)}) async-start(bf16[8,1,25,8,200]{4,3,2,1,0:T(8,128)(2,1)} %bitcast.195), calls=%async_computation.1 | async-start | bytes 1638400 | tf_op jit(solution)/shard_map/all_to_all | solution.py:686
  95.7 168.0 %all-gather.8.cloned.1.call-start = ((), (), s32[]{:S(2)}) async-start(), calls=%async_computation.12 | async-start | bytes 3833856 | tf_op jit(solution)/shard_map/all_gather | solution.py:878
  145.8 37.2 %collective-permute-start.4 = (bf16[8,1,25,8,400]{4,3,2,0,1:T(8,128)(2,1)}, bf16[8,1,25,8,400]{4,3,2,0,1:T(8,128)(2,1)}, u32[]{:S(2)}, u32[]{:S(2)}) collective-permute-start(bf16[8,1,25,8,400]{4,3,2,0,1:T(8,128)(2,1)} %bitcast.202), channel_id=1, source_target_pairs={{0,16},{8,24},{16,0},{24,8},{1,17},{9,25},{17,1},{25,9},{2,18},{10... | collective-permute-start | bytes 3840008 | tf_op jit(solution)/shard_map/ppermute | solution.py:585
  147.7 29.5 %all-to-all-start.2 = ((bf16[8,1,16,8,256]{4,3,2,1,0:T(8,128)(2,1)}), bf16[8,1,16,8,256]{4,3,2,1,0:T(8,128)(2,1)S(1)}, u32[]{:S(2)}, u32[]{:S(2)}) async-start(bf16[8,1,16,8,256]{4,3,2,1,0:T(8,128)(2,1)} %bitcast.21), calls=%async_computation.2 | async-start | bytes 1048576 | tf_op jit(solution)/shard_map/all_to_all | solution.py:686
  151.2 398.7 %reduce-scatter.2.cloned.1.call-start = ((), (), s32[]{:S(2)}) async-start(), calls=%async_computation.13 | async-start | bytes 3833856 | tf_op jit(solution)/shard_map/reduce_scatter | solution.py:953
  151.3 33.7 %collective-permute-start.3 = (bf16[8,1,25,8,400]{4,3,2,0,1:T(8,128)(2,1)S(1)}, bf16[8,1,25,8,400]{4,3,2,0,1:T(8,128)(2,1)}, u32[]{:S(2)}, u32[]{:S(2)}) collective-permute-start(bf16[8,1,25,8,400]{4,3,2,0,1:T(8,128)(2,1)S(1)} %bitcast.189), channel_id=1, source_target_pairs={{0,8},{8,0},{16,24},{24,16},{1,9},{9,1},{17,25},{25,17},{2,10},{10... | collective-permute-start | bytes 3840008 | tf_op jit(solution)/shard_map/ppermute | solution.py:585
  199.9 20.6 %collective-permute-start.6 = (bf16[1,16,8,1600]{3,2,1,0:T(8,128)(2,1)}, bf16[1,16,8,1600]{3,2,1,0:T(8,128)(2,1)S(1)}, u32[]{:S(2)}, u32[]{:S(2)}) collective-permute-start(bf16[1,16,8,1600]{3,2,1,0:T(8,128)(2,1)} %bitcast.247), channel_id=1, source_target_pairs={{0,2},{2,4},{4,6},{6,7},{7,5},{5,3},{3,1},{1,0},{8,10},{10,12},{12... | collective-permute-start | bytes 1228808 | tf_op jit(solution)/shard_map/ppermute | solution.py:585
  201.8 20.9 %collective-permute-start.7 = (bf16[1,16,8,1600]{3,2,1,0:T(8,128)(2,1)}, bf16[1,16,8,1600]{3,2,1,0:T(8,128)(2,1)S(1)}, u32[]{:S(2)}, u32[]{:S(2)}) collective-permute-start(bf16[1,16,8,1600]{3,2,1,0:T(8,128)(2,1)} %bitcast.248), channel_id=1, source_target_pairs={{0,1},{2,0},{4,2},{6,4},{7,6},{5,7},{3,5},{1,3},{8,9},{10,8},{12,1... | collective-permute-start | bytes 1228808 | tf_op jit(solution)/shard_map/ppermute | solution.py:585
  202.8 22.8 %collective-permute-start.10 = (bf16[8,1,25,8,200]{4,3,2,0,1:T(8,128)(2,1)}, bf16[8,1,25,8,200]{4,3,2,0,1:T(8,128)(2,1)S(1)}, u32[]{:S(2)}, u32[]{:S(2)}) collective-permute-start(bf16[8,1,25,8,200]{4,3,2,0,1:T(8,128)(2,1)} %bitcast.240), channel_id=1, source_target_pairs={{0,16},{8,24},{16,0},{24,8},{1,17},{9,25},{17,1},{25,9},{2,18},{10... | collective-permute-start | bytes 1920008 | tf_op jit(solution)/shard_map/ppermute | solution.py:585
  262.1 29.3 %collective-permute-start.17 = (bf16[1,16,8,1600]{3,2,1,0:T(8,128)(2,1)}, bf16[1,16,8,1600]{3,2,1,0:T(8,128)(2,1)S(1)}, u32[]{:S(2)}, u32[]{:S(2)}) collective-permute-start(bf16[1,16,8,1600]{3,2,1,0:T(8,128)(2,1)} %bitcast.272), channel_id=1, source_target_pairs={{0,16},{8,24},{16,0},{24,8},{1,17},{9,25},{17,1},{25,9},{2,18},{10... | collective-permute-start | bytes 1228808 | tf_op jit(solution)/shard_map/ppermute | solution.py:585
  290.3 19.7 %collective-permute-start.20 = (bf16[1,16,8,1600]{3,2,1,0:T(8,128)(2,1)S(1)}, bf16[1,16,8,1600]{3,2,1,0:T(8,128)(2,1)S(1)}, u32[]{:S(2)}, u32[]{:S(2)}) collective-permute-start(bf16[1,16,8,1600]{3,2,1,0:T(8,128)(2,1)S(1)} %bitcast.273), channel_id=1, source_target_pairs={{0,8},{8,0},{16,24},{24,16},{1,9},{9,1},{17,25},{25,17},{2,10},{10... | collective-permute-start | bytes 1228808 | tf_op jit(solution)/shard_map/ppermute | solution.py:585
  290.3 19.7 %collective-permute-start.19 = (bf16[1,16,8,1600]{3,2,1,0:T(8,128)(2,1)S(1)}, bf16[1,16,8,1600]{3,2,1,0:T(8,128)(2,1)S(1)}, u32[]{:S(2)}, u32[]{:S(2)}) collective-permute-start(bf16[1,16,8,1600]{3,2,1,0:T(8,128)(2,1)S(1)} %get-tuple-element.359), channel_id=1, source_target_pairs={{0,1},{2,0},{4,2},{6,4},{7,6},{5,7},{3,5},{1,3},{8,9},{10,8},{12,1... | collective-permute-start | bytes 1228808 | tf_op jit(solution)/shard_map/ppermute | solution.py:585
  329.9 20.8 %collective-permute-start.26 = (bf16[8,1,25,8,200]{4,3,2,0,1:T(8,128)(2,1)}, bf16[8,1,25,8,200]{4,3,2,0,1:T(8,128)(2,1)S(1)}, u32[]{:S(2)}, u32[]{:S(2)}) collective-permute-start(bf16[8,1,25,8,200]{4,3,2,0,1:T(8,128)(2,1)} %bitcast.252), channel_id=1, source_target_pairs={{0,8},{8,0},{16,24},{24,16},{1,9},{9,1},{17,25},{25,17},{2,10},{10... | collective-permute-start | bytes 1920008 | tf_op jit(solution)/shard_map/ppermute | solution.py:585
  329.9 20.8 %collective-permute-start.27 = (bf16[8,1,25,8,200]{4,3,2,0,1:T(8,128)(2,1)}, bf16[8,1,25,8,200]{4,3,2,0,1:T(8,128)(2,1)S(1)}, u32[]{:S(2)}, u32[]{:S(2)}) collective-permute-start(bf16[8,1,25,8,200]{4,3,2,0,1:T(8,128)(2,1)} %bitcast.253), channel_id=1, source_target_pairs={{0,8},{8,0},{16,24},{24,16},{1,9},{9,1},{17,25},{25,17},{2,10},{10... | collective-permute-start | bytes 1920008 | tf_op jit(solution)/shard_map/ppermute | solution.py:585
  359.3 29.1 %all-to-all-start.3 = ((bf16[8,1,16,8,256]{4,3,2,1,0:T(8,128)(2,1)}), bf16[8,1,16,8,256]{4,3,2,1,0:T(8,128)(2,1)S(1)}, u32[]{:S(2)}, u32[]{:S(2)}) async-start(bf16[8,1,16,8,256]{4,3,2,1,0:T(8,128)(2,1)} %bitcast.245), calls=%async_computation.4 | async-start | bytes 1048576 | tf_op jit(solution)/shard_map/all_to_all | solution.py:686
  364.5 23.8 %collective-permute-start.28 = (bf16[8,1,25,8,200]{4,3,2,0,1:T(8,128)(2,1)}, bf16[8,1,25,8,200]{4,3,2,0,1:T(8,128)(2,1)S(1)}, u32[]{:S(2)}, u32[]{:S(2)}) collective-permute-start(bf16[8,1,25,8,200]{4,3,2,0,1:T(8,128)(2,1)} %bitcast.232), channel_id=1, source_target_pairs={{0,16},{8,24},{16,0},{24,8},{1,17},{9,25},{17,1},{25,9},{2,18},{10... | collective-permute-start | bytes 1920008 | tf_op jit(solution)/shard_map/ppermute | solution.py:585
  364.5 23.8 %collective-permute-start.29 = (bf16[1,4,25,8,400]{4,3,2,1,0:T(8,128)(2,1)}, bf16[1,4,25,8,400]{4,3,2,1,0:T(8,128)(2,1)S(1)}, u32[]{:S(2)}, u32[]{:S(2)}) collective-permute-start(bf16[1,4,25,8,400]{4,3,2,1,0:T(8,128)(2,1)} %bitcast.86), channel_id=1, source_target_pairs={{0,8},{8,0},{16,24},{24,16},{1,9},{9,1},{17,25},{25,17},{2,10},{10... | collective-permute-start | bytes 1920008 | tf_op jit(solution)/shard_map/ppermute | solution.py:585
  364.5 23.9 %collective-permute-start.30 = (bf16[1,4,25,8,400]{4,3,2,1,0:T(8,128)(2,1)}, bf16[1,4,25,8,400]{4,3,2,1,0:T(8,128)(2,1)S(1)}, u32[]{:S(2)}, u32[]{:S(2)}) collective-permute-start(bf16[1,4,25,8,400]{4,3,2,1,0:T(8,128)(2,1)} %bitcast.256), channel_id=1, source_target_pairs={{0,8},{8,0},{16,24},{24,16},{1,9},{9,1},{17,25},{25,17},{2,10},{10... | collective-permute-start | bytes 1920008 | tf_op jit(solution)/shard_map/ppermute | solution.py:585
  365.0 23.3 %collective-permute-start.31 = (bf16[1,16,8,1600]{3,2,1,0:T(8,128)(2,1)}, bf16[1,16,8,1600]{3,2,1,0:T(8,128)(2,1)S(1)}, u32[]{:S(2)}, u32[]{:S(2)}) collective-permute-start(bf16[1,16,8,1600]{3,2,1,0:T(8,128)(2,1)} %bitcast.250), channel_id=1, source_target_pairs={{0,16},{8,24},{16,0},{24,8},{1,17},{9,25},{17,1},{25,9},{2,18},{10... | collective-permute-start | bytes 1228808 | tf_op jit(solution)/shard_map/ppermute | solution.py:585
  393.8 32.9 %all-to-all-start.4 = ((bf16[8,1,25,8,200]{4,3,2,1,0:T(8,128)(2,1)}), bf16[8,1,25,8,200]{4,3,2,1,0:T(8,128)(2,1)S(1)}, u32[]{:S(2)}, u32[]{:S(2)}) async-start(bf16[8,1,25,8,200]{4,3,2,1,0:T(8,128)(2,1)} %fusion.11), calls=%async_computation.5 | async-start | bytes 1638400 | tf_op jit(solution)/shard_map/all_to_all | solution.py:686
  400.8 25.1 %collective-permute-start.34 = (bf16[1,4,25,8,400]{4,3,2,1,0:T(8,128)(2,1)}, bf16[1,4,25,8,400]{4,3,2,1,0:T(8,128)(2,1)S(1)}, u32[]{:S(2)}, u32[]{:S(2)}) collective-permute-start(bf16[1,4,25,8,400]{4,3,2,1,0:T(8,128)(2,1)} %bitcast.230), channel_id=1, source_target_pairs={{0,16},{8,24},{16,0},{24,8},{1,17},{9,25},{17,1},{25,9},{2,18},{10... | collective-permute-start | bytes 1920008 | tf_op jit(solution)/shard_map/ppermute | solution.py:585
  451.4 21.4 %collective-permute-start.38 = (bf16[8,1,25,8,192]{4,3,2,0,1:T(8,128)(2,1)}, bf16[8,1,25,8,192]{4,3,2,0,1:T(8,128)(2,1)S(1)}, u32[]{:S(2)}, u32[]{:S(2)}) collective-permute-start(bf16[8,1,25,8,192]{4,3,2,0,1:T(8,128)(2,1)} %fusion.12), channel_id=1, source_target_pairs={{0,16},{8,24},{16,0},{24,8},{1,17},{9,25},{17,1},{25,9},{2,18},{10... | collective-permute-start | bytes 1843208 | tf_op jit(solution)/shard_map/ppermute | solution.py:585
  453.5 19.3 %collective-permute-start.37 = (bf16[1,23,8,1600]{3,2,1,0:T(8,128)(2,1)}, bf16[1,23,8,1600]{3,2,1,0:T(8,128)(2,1)}, u32[]{:S(2)}, u32[]{:S(2)}) collective-permute-start(bf16[1,23,8,1600]{3,2,1,0:T(8,128)(2,1)} %bitcast.108), channel_id=1, source_target_pairs={{0,2},{2,4},{4,6},{6,7},{7,5},{5,3},{3,1},{1,0},{8,10},{10,12},{12... | collective-permute-start | bytes 1766408 | tf_op jit(solution)/shard_map/ppermute | solution.py:585
  478.3 33.5 %all-to-all-start.7 = ((bf16[8,1,25,8,192]{4,3,2,1,0:T(8,128)(2,1)}), bf16[8,1,25,8,192]{4,3,2,1,0:T(8,128)(2,1)S(1)}, u32[]{:S(2)}, u32[]{:S(2)}) async-start(bf16[8,1,25,8,192]{4,3,2,1,0:T(8,128)(2,1)} %fusion.13), calls=%async_computation.8 | async-start | bytes 1638400 | tf_op jit(solution)/shard_map/all_to_all | solution.py:686
  483.2 28.5 %collective-permute-start.40 = (bf16[1,23,8,1600]{3,2,1,0:T(8,128)(2,1)S(1)}, bf16[1,23,8,1600]{3,2,1,0:T(8,128)(2,1)S(1)}, u32[]{:S(2)}, u32[]{:S(2)}) collective-permute-start(bf16[1,23,8,1600]{3,2,1,0:T(8,128)(2,1)S(1)} %bitcast.260), channel_id=1, source_target_pairs={{0,1},{2,0},{4,2},{6,4},{7,6},{5,7},{3,5},{1,3},{8,9},{10,8},{12,1... | collective-permute-start | bytes 1766408 | tf_op jit(solution)/shard_map/ppermute | solution.py:585
  485.3 26.5 %collective-permute-start.39 = (bf16[1,23,8,1600]{3,2,1,0:T(8,128)(2,1)}, bf16[1,23,8,1600]{3,2,1,0:T(8,128)(2,1)S(1)}, u32[]{:S(2)}, u32[]{:S(2)}) collective-permute-start(bf16[1,23,8,1600]{3,2,1,0:T(8,128)(2,1)} %bitcast.286), channel_id=1, source_target_pairs={{0,2},{2,4},{4,6},{6,7},{7,5},{5,3},{3,1},{1,0},{8,10},{10,12},{12... | collective-permute-start | bytes 1766408 | tf_op jit(solution)/shard_map/ppermute | solution.py:585
  486.0 25.8 %collective-permute-start.41 = (f32[1,2400]{1,0:T(1,128)S(1)}, f32[1,2400]{1,0:T(1,128)S(1)}, u32[]{:S(2)}, u32[]{:S(2)}) collective-permute-start(f32[1,2400]{1,0:T(1,128)S(1)} %concatenate.25), channel_id=1, source_target_pairs={{0,8},{8,0},{16,24},{24,16},{1,9},{9,1},{17,25},{25,17},{2,10},{10... | collective-permute-start | bytes 28808 | tf_op jit(solution)/shard_map/ppermute | solution.py:1047
  515.9 22.7 %collective-permute-start.42 = (bf16[1,23,8,1600]{3,2,1,0:T(8,128)(2,1)}, bf16[1,23,8,1600]{3,2,1,0:T(8,128)(2,1)}, u32[]{:S(2)}, u32[]{:S(2)}) collective-permute-start(bf16[1,23,8,1600]{3,2,1,0:T(8,128)(2,1)} %bitcast.288), channel_id=1, source_target_pairs={{0,2},{2,4},{4,6},{6,7},{7,5},{5,3},{3,1},{1,0},{8,10},{10,12},{12... | collective-permute-start | bytes 1766408 | tf_op jit(solution)/shard_map/ppermute | solution.py:585
  (108 other events, 740.8 us)
Sparse Core Ops, SparseCore 0:
  10.2 79.8 all-gather.3
  92.9 50.2 all-gather.5
  145.4 75.2 all-gather.7
  332.6 96.0 reduce-scatter.1

commit v3 on v2

--- a/solution.py
+++ b/solution.py
@@ -15,6 +15,7 @@
 BF = jnp.bfloat16
 F32 = jnp.float32
 VMEM_LIMIT = 56 << 20
+MOST_ROWS = 1024
 COST = 1.6e8
 
 
@@ -35,7 +36,7 @@
 
 
 def whole(*dims):
-    return pl.BlockSpec(dims, lambda *_: (0,) * len(dims))
+    return pl.BlockSpec(dims, lambda *_: (0,) * len(dims), pipeline_mode=pl.Buffered(1))
 
 
 def call(
@@ -269,30 +270,75 @@
     return hidden * half, slope
 
 
-def project_kernel(table, gain, shift, bias, weight, tokens, normed, projected, kept):
-    length = tokens.shape[0]
+def project_kernel(shards, table, gain, shift, bias, weight, *refs):
+    blocks, (normed, projected, kept) = refs[:shards], refs[shards:]
+    span = blocks[0].shape[0]
+    for r in range(shards):
+        normed[rows_of(table[r], span), :] = blocks[r][...]
+    length = span * shards
     chunk = min(256, length)
-    for first in range(0, length, chunk):
-        rows = slice(first, first + chunk)
-        xhat, _ = norm_stats(tokens[rows, :].astype(F32))
+
+    def some_rows(i, carry):
+        rows = rows_of(i, chunk)
+        xhat, _ = norm_stats(normed[rows, :].astype(F32))
         kept[rows, :] = xhat.astype(BF)
         normed[rows, :] = (xhat * gain[...] + shift[...]).astype(BF)
         projected[rows, :] = (dot_nn(normed[rows, :], weight[...]) + bias[...]).astype(BF)
-
-
-def unproject_kernel(shards, table, grad, weight, xhat, *refs):
-    others, blocks, (sums, rows) = refs[:shards], refs[shards : 2 * shards], refs[2 * shards :]
+        return carry
+
+    lax.fori_loop(0, length // chunk, some_rows, 0)
+
+
+def unproject_kernel(shards, batches, heads, table, grad, weight, xhat, norms, cots, head_sums, *refs):
+    others, blocks, (sums, rows, vectors) = refs[:shards], refs[shards : 2 * shards], refs[2 * shards :]
     length = rows.shape[0]
     span, chunk = length // shards, min(256, length)
     sums[...] = jnp.zeros_like(sums)
-    for first in range(0, length, chunk):
-        share = dot_nt(grad[first : first + chunk, :], weight[...])
-        rows[first : first + chunk, :] = share.astype(BF)
-        sums[0:1, :] += jnp.sum(share * xhat[first : first + chunk, :].astype(F32), axis=0, keepdims=True)
+
+    def some_rows(i, carry):
+        at = rows_of(i, chunk)
+        share = dot_nt(grad[at, :], weight[...])
+        rows[at, :] = share.astype(BF)
+        sums[0:1, :] += jnp.sum(share * xhat[at, :].astype(F32), axis=0, keepdims=True)
         sums[1:2, :] += jnp.sum(share, axis=0, keepdims=True)
+        return carry
+
+    lax.fori_loop(0, length // chunk, some_rows, 0)
+    width = sums.shape[1]
+    part = width // shards
+    for s in range(shards):
+        for i, source in enumerate([sums[0:1], sums[1:2], norms[0:1], norms[1:2], norms[2:3], cots[...]]):
+            vectors[s, :, i * part : (i + 1) * part] = source[:, s * part : (s + 1) * part]
+        vectors[s, :, 6 * part :] = jnp.zeros((1, width - 6 * part), F32)
+    for s in range(shards):
+
+        @pl.when(table[0] == s)
+        def _(s=s):
+            for first, shard, to, size in head_copies(s, shards, heads, width):
+                pair, at = first
+                vectors[shard, :, 6 * part + to : 6 * part + to + size] = head_sums[pair, :, at : at + size]
+
+    last = others[0].shape[0] - 1
     for r in range(shards):
         blocks[r][:span, :] = rows[rows_of(table[r], span), :]
-        blocks[r][span:, :] = others[r][...]
+        blocks[r][span : span + last, :] = others[r][:last, :]
+        blocks[r][span + last :, :] = vectors[table[r]].astype(BF)
+
+
+def head_copies(shard, shards, heads, width):
+    found, piece = [], 2 * width // shards
+    for head in range(heads):
+        number = shard * heads + head
+        if (number + 1) * HEAD_DIM > width:
+            continue
+        for kind, base in ((0, 0), (2, width)):
+            at, end = base + number * HEAD_DIM, base + (number + 1) * HEAD_DIM
+            first = head % 2 * HEAD_COLS + kind * HEAD_DIM
+            while at < end:
+                size = min(end, (at // piece + 1) * piece) - at
+                found.append(((head // 2, first), at // piece, at % piece, size))
+                at, first = at + size, first + size
+    return found
 
 
 def mix_kernel(shards, table, tokens, weight, bias, gain, shift, heads, attended, mixed, normed, spread):
@@ -323,8 +369,9 @@
 
 
 def mlp_kernel(shards, group, table, fc, bias, out, *refs):
-    blocks, cotangents, refs = refs[:shards], refs[shards : shards + group], refs[shards + group :]
-    act, low, cots, sums, shares, results, normed = refs
+    blocks, cotangents, refs = refs[:shards], refs[shards : 2 * shards], refs[2 * shards :]
+    act, low, sums, results = refs[:4]
+    shares, (normed, cots) = refs[4 : 4 + shards], refs[4 + shards :]
     step = pl.program_id(0)
     span = blocks[0].shape[0]
     for first in range(0, shards, group):
@@ -333,9 +380,8 @@
         def _(first=first):
             for i in range(group):
                 normed[i * span : (i + 1) * span, :] = blocks[first + i][...]
-
-    for i in range(group):
-        cots[i * span : (i + 1) * span, :] = cotangents[i][0]
+                cots[i * span : (i + 1) * span, :] = cotangents[first + i][...]
+
     hidden = dot_nn(normed[...], fc[...]) + bias[...]
     activated, slope = gelu_both(hidden)
     act[...] = activated.astype(BF)
@@ -354,43 +400,57 @@
     share = dot_nt(low[...], fc[...]).astype(BF)
     result = dot_nn(act[...], out[...]).astype(BF)
     for i in range(group):
-        shares[i] = share[i * span : (i + 1) * span, :]
         results[i] = result[i * span : (i + 1) * span, :]
-
-
-def mlp_part(blocks, cotangent, fc, bias, out, table):
+    for first in range(0, shards, group):
+
+        @pl.when(step == first // group)
+        def _(first=first):
+            for i in range(group):
+                shares[first + i][...] = share[i * span : (i + 1) * span, :]
+
+
+def mlp_part(blocks, cotangents, fc, bias, out, table):
     shards = len(blocks)
     span, width = blocks[0].shape
     rows, units = shards * span, fc.shape[1]
+    if rows > MOST_ROWS:
+        half = shards // 2
+        halves = [mlp_part(blocks[i:][:half], cotangents[i:][:half], fc, bias, out, table) for i in (0, half)]
+        first, second = halves
+        results = jnp.concatenate([first[3], second[3]])
+        return first[0] + second[0], first[1] + second[1], first[2] + second[2], results, first[4] + second[4]
     group = min(shards, max(1, 512 // span))
-    cotangent = cotangent.reshape(shards, span, width)
-    own = lambda i: pl.BlockSpec((1, span, width), lambda g, t: (t[g * group + i], 0, 0))
     rows_at = lambda cols: pl.BlockSpec((group * span, cols), lambda g, t: (g, 0))
-    return call(
+    got = call(
         functools.partial(mlp_kernel, shards, group),
         table,
-        [fc, bias, out, *blocks] + [cotangent] * group,
+        [fc, bias, out, *blocks, *cotangents],
         [shape_of((rows, units), BF)] * 2
         + [
-            shape_of((rows, width), BF),
             shape_of((1, units), F32),
             shape_of((shards, span, width), BF),
-            shape_of((shards, span, width), BF),
-        ],
+        ]
+        + [shape_of((span, width), BF)] * shards,
         grid=(shards // group,),
-        in_specs=[whole(*a.shape) for a in (fc, bias, out, *blocks)] + [own(i) for i in range(group)],
         out_specs=[
             rows_at(units),
             rows_at(units),
-            rows_at(width),
             whole(1, units),
             pl.BlockSpec((group, span, width), lambda g, t: (g, 0, 0)),
-            pl.BlockSpec((group, span, width), lambda g, t: (g, 0, 0)),
-        ],
-        scratch=[pltpu.VMEM((group * span, width), BF)],
+        ]
+        + [whole(span, width)] * shards,
+        scratch=[pltpu.VMEM((group * span, width), BF)] * 2,
         us=15,
         name="mlp",
     )
+    return got[:1], got[1:2], got[2], got[3], got[4:]
+
+
+def take_rows(pieces):
+    found = []
+    while pieces and sum(v.shape[0] for v in found) < MOST_ROWS:
+        found.append(pieces.pop(0))
+    return found
 
 
 def weight_kernel(shards, batches, row_blocks, count, table, *refs):
@@ -412,8 +472,15 @@
 
 def weight_shares(lefts, rights, table, shards, batches, row_blocks, name, wait=()):
     rows, cols = lefts[0].shape[1], rights[0].shape[1]
-    length = sum(v.shape[0] for v in lefts)
     dims = (row_blocks, rows // row_blocks, cols // batches)
+    if sum(v.shape[0] for v in lefts) > MOST_ROWS:
+        cut_rows = lambda vs: [v[i : i + MOST_ROWS] for v in vs for i in range(0, v.shape[0], MOST_ROWS)]
+        total, lefts, rights = None, cut_rows(lefts), cut_rows(rights)
+        while lefts:
+            some = [take_rows(lefts), take_rows(rights)]
+            found = weight_shares(*some, table, shards, batches, row_blocks, name, wait)
+            total = found if total is None else [add(a, b) for a, b in zip(total, found)]
+        return total
     return call(
         functools.partial(weight_kernel, shards, batches, row_blocks, len(lefts)),
         table,
@@ -462,26 +529,28 @@
     )[0]
 
 
-def assemble_kernel(shards, batches, rows, table, *refs):
-    parts, out = refs[:batches], refs[batches]
-    blocks, _, cols = parts[0].shape
+def assemble_kernel(shards, batches, rows, pieces, table, *refs):
+    out = refs[-1]
+    blocks, _, cols = refs[0].shape
     for member in range(batches):
 
         @pl.when(table[shards] == member)
         def _(member=member):
             for apart in range(batches):
                 at = (member ^ apart) * cols
-                for block in range(blocks):
-                    out[block * rows : (block + 1) * rows, at : at + cols] = parts[apart][block, :rows, :]
-
-
-def assemble(parts, table, shards, rows, wait=()):
+                for i in range(pieces * blocks):
+                    source = refs[apart * pieces + i // blocks][i % blocks, :rows, :]
+                    out[i * rows : (i + 1) * rows, at : at + cols] = source
+
+
+def assemble(parts, table, shards, rows, pieces=1, wait=()):
     blocks, _, cols = parts[0].shape
+    batches = len(parts) // pieces
     return call(
-        functools.partial(assemble_kernel, shards, len(parts), rows),
+        functools.partial(assemble_kernel, shards, batches, rows, pieces),
         table,
         parts,
-        [shape_of((blocks * rows, len(parts) * cols), BF)],
+        [shape_of((pieces * blocks * rows, batches * cols), BF)],
         us=5,
         wait=wait,
         name="assemble",
@@ -537,7 +606,7 @@
     batches, rows = len(lefts), lefts[0].shape[1]
     width = rights[0].shape[1]
     piece = -(-(rows // shards) // batches)
-    dims = (piece + -(span + piece) % 8, width)
+    dims = (piece + 1 + -(span + piece + 1) % 8, width)
     return call(
         functools.partial(proj_grad_kernel, shards, batches),
         table,
@@ -614,7 +683,7 @@
 
 class Rounds:
     def __init__(self):
-        self.chains, self.mark = [], None
+        self.chains, self.mark, self.waits = [], None, []
 
     def add(self, chain):
         self.chains.append([chain, None])
@@ -628,7 +697,8 @@
             except StopIteration:
                 pass
         values = list(start())
-        out = gate(values + [v for p in pending for v in p], parts=parts)
+        out = gate(values + [v for p in pending for v in p], self.waits, parts=parts)
+        self.waits = []
         at, self.chains = len(values), []
         for chain, p in zip(alive, pending):
             self.chains.append([chain, out[at : at + len(p)]])
@@ -697,33 +767,6 @@
         parts.update(zip(came, (yield list(came.values()))))
         bit //= 2
     return [parts[apart] for apart in range(batches)]
-
-
-def vector_kernel(shards, table, *refs):
-    *rows, last, out = refs
-    at = 0
-    for ref in rows:
-        size = ref.shape[1] // shards
-        for i in range(ref.shape[0]):
-            for s in range(shards):
-                out[s, :, at : at + size] = ref[i : i + 1, s * size : (s + 1) * size]
-            at += size
-    for i in range(last.shape[0]):
-        for s in range(shards):
-            out[s, :, at : at + last.shape[2]] = last[i]
-        at += last.shape[2]
-
-
-def cut_vectors(rows, last, table, shards):
-    cols = sum(v.size for v in rows) // shards + last.size
-    return call(
-        functools.partial(vector_kernel, shards),
-        table,
-        [*rows, last],
-        [shape_of((shards, 1, cols), F32)],
-        us=3,
-        name="vectors",
-    )[0]
 
 
 def per_device(
@@ -797,20 +840,21 @@
         held["small"] = got[:, part:, : part // ((got.shape[1] - part) // 8)]
         parts = yield from batch_gather_steps(got, batches)
         held["qkv"] = assemble(parts, table, shards, part)
-        held["qkv"] = (yield [held["qkv"]])[0]
+        rounds.waits.append(held["qkv"])
+
+    far = shards // 2
 
     def fc_weights():
         yield []
         got = pack(fc_weight, table, shards, batches, fc_quarter, fc_ranges, wait=[rounds.mark])
         (got,) = yield [got]
-        while "qkv" not in held:
+        for _ in range(far - 2):
             yield []
-        got = swap_blocks(after(got, rounds.mark))
-        yield []
-        (got,) = yield [got]
+        (got,) = yield [swap_blocks(after(got, rounds.mark))]
         while "normed_two" not in held:
             yield []
-        came = over_batch(after(got, rounds.mark), batches, batches // 2)
+        got = after(got, rounds.mark)
+        came = over_batch(got, batches, batches // 2)
         yield []
         parts = {0: got, batches // 2: (yield [came])[0]}
         bit = batches // 4
@@ -821,14 +865,32 @@
         parts = [parts[apart] for apart in range(batches)]
         held["fc"] = (yield [assemble(parts, table, shards, part)])[0]
 
+    def proj_weights():
+        got = lax.all_gather(cut(proj_part), "seq", axis=0, tiled=True)
+        for _ in range(far):
+            yield []
+        got = after(got.reshape(shards, part, out_cols), rounds.mark)
+        got = [got[:far], got[far:]]
+        came = [over_batch(v, batches, batches // 2) for v in got]
+        came[0] = (yield came[:1])[0]
+        came[1] = (yield came[1:])[0]
+        parts = {0: got, batches // 2: came}
+        bit = batches // 4
+        while bit:
+            parts.update(
+                {apart ^ bit: [over_batch(v, batches, bit) for v in p] for apart, p in parts.items()}
+            )
+            bit //= 2
+        parts = [v for apart in range(batches) for v in parts[apart]]
+        held["w_proj"] = (yield [assemble(parts, table, shards, part, 2)])[0]
+
     rounds.add(first_weights())
     rounds.add(fc_weights())
-    all_tokens = lax.all_gather(cut(own_tokens), "seq", axis=0, tiled=True).reshape(length, width)
+    rounds.add(proj_weights())
+    token_blocks = [block for (block,) in ring.gather([own_tokens])]
     while "qkv" not in held:
         rounds.end(lambda: [])
     w_qkv = held["qkv"]
-    proj_rows = after(proj_part, all_tokens, rounds.mark)
-    proj_rows = lax.all_gather(cut(proj_rows), "seq", axis=0, tiled=True).reshape(shards, part, out_cols)
     small = held["small"].reshape(shards, -1)
     gain_one = row(small[:, :part])
     shift_one = row(small[:, part : 2 * part])
@@ -843,11 +905,23 @@
     )
     bias_heads = jnp.swapaxes(bias_heads, 0, 1).reshape(1, padded * HEAD_COLS)
     bias_slice = lax.dynamic_slice_in_dim(bias_heads, me * slice_cols, slice_cols, 1).astype(F32)
+    cot_blocks = [own_cot] * shards
+
+    def cotangents():
+        right = left = after(own_cot, rounds.mark)
+        for step in range(1, far + 1):
+            came = yield ring.both([right], [left] if step < shards - step else [])
+            right = cot_blocks[shards - step] = came[0]
+            if step < shards - step:
+                left = cot_blocks[step] = came[1]
+
+    rounds.add(cotangents())
+
     def project():
         return call(
-            project_kernel,
+            functools.partial(project_kernel, shards),
             table,
-            [gain_one, shift_one, bias_slice, w_qkv, all_tokens],
+            [gain_one, shift_one, bias_slice, w_qkv, *token_blocks],
             [
                 shape_of((length, width), BF),
                 shape_of((length, slice_cols), BF),
@@ -857,28 +931,14 @@
             name="project",
         )
 
-    def proj_weights():
-        yield []
-        yield []
-        got = proj_rows
-        came = over_batch(after(got, rounds.mark), batches, batches // 2)
-        (came,) = yield [came]
-        parts = {0: got, batches // 2: came}
-        bit = batches // 4
-        while bit:
-            came = {apart ^ bit: over_batch(p, batches, bit) for apart, p in parts.items()}
-            parts.update(zip(came, (yield list(came.values()))))
-            bit //= 2
-        parts = [parts[apart] for apart in range(batches)]
-        held["w_proj"] = (yield [assemble(parts, table, shards, part)])[0]
-
-    rounds.add(proj_weights())
     normed_one, projected, xhat_one = rounds.end(project)
     attended_heads, attended_full, log_total = rounds.end(lambda: attention_forward(projected, table, heads))
-    all_cot = lax.all_gather(cut(after(own_cot, proj_rows, rounds.mark)), "seq", axis=0, tiled=True)
-    all_cot = all_cot.reshape(length, width)
     (attended_heads,) = rounds.end(
-        lambda: [swap_blocks(attended_heads.reshape(shards, span, heads * HEAD_DIM))]
+        lambda: [
+            swap_blocks(
+                attended_heads.reshape(shards, span, heads * HEAD_DIM)
+            )
+        ]
     )
     while "w_proj" not in held:
         rounds.end(lambda: [])
@@ -907,8 +967,8 @@
     while "fc" not in held:
         rounds.end(lambda: [])
     w_fc = held["fc"]
-    activated, hidden_low, cot_rows, fc_sums, g_two, out_rows = mlp_part(
-        normed_blocks, all_cot, w_fc, row(fc_bias), out_weight, table
+    activated, hidden_low, fc_sums, out_rows, g_two = mlp_part(
+        normed_blocks, cot_blocks, w_fc, row(fc_bias), out_weight, table
     )
 
     shares = functools.partial(weight_shares, table=table, shards=shards, batches=batches)
@@ -925,24 +985,29 @@
         yield []
         yield []
         found = yield shares(
-            normed_blocks, [hidden_low], row_blocks=shards, name="fc_grad", wait=[rounds.mark]
+            normed_blocks, hidden_low, row_blocks=shards, name="fc_grad", wait=[rounds.mark]
         )
         kept = yield from near_sums(found)
+        yield []
+        yield []
         came = over_batch(after(kept[1], rounds.mark), batches, 2)
-        yield []
         share = add(kept[0], *(yield [came]))
         share = swap_blocks(share)
         yield []
         (share,) = yield [share]
-        held["fc_grad"] = (yield [swap_blocks(share, "batch")])[0]
+        for _ in range(far - 1):
+            yield []
+        held["fc_grad"] = (yield [swap_blocks(after(share, rounds.mark), "batch")])[0]
 
     def out_gradient():
         yield []
         yield []
         yield []
-        found = yield shares([activated], [cot_rows], row_blocks=1, name="out_grad", wait=[rounds.mark])
+        found = yield shares(activated, cot_blocks, row_blocks=1, name="out_grad", wait=[rounds.mark])
         yield []
         kept = yield from near_sums(found)
+        while "unproject" not in held:
+            yield []
         came = over_batch(after(kept[1], rounds.mark), batches, 2)
         yield []
         held["out_grad"] = add(kept[0], *(yield [came]))
@@ -950,13 +1015,16 @@
     def out_result():
         yield []
         (total,) = yield [join(out_rows, table, [rounds.mark])]
-        held["out"] = lax.psum_scatter(cut(total), "seq", scatter_dimension=0, tiled=True)
+        for _ in range(far - 2):
+            yield []
+        total = cut(after(total, rounds.mark))
+        held["out"] = lax.psum_scatter(total, "seq", scatter_dimension=0, tiled=True)
 
     held["mlp"] = True
     rounds.add(out_result())
     rounds.add(fc_gradient())
     rounds.add(out_gradient())
-    g_two = ring.scatter_sum([g_two[r] for r in range(shards)])
+    g_two = ring.scatter_sum(g_two)
 
     def unmix():
         return call(
@@ -984,8 +1052,9 @@
             projected, grad_heads.reshape(length, -1), attended_full, log_total, table, heads, []
         )
     )
-    qkv_kept = rounds.end(
-        lambda: shares([normed_one], [grad_projected], row_blocks=shards, name="qkv_grad")
+    held["qkv_found"] = shares([normed_one], [grad_projected], row_blocks=shards, name="qkv_grad")
+    qkv_near = rounds.end(
+        lambda: [over_batch(held["qkv_found"][apart ^ 1], batches, 1) for apart in range(0, batches, 2)]
     )
     proj_blocks = proj_grad(gathered["attended"], gathered["mixed_low"], table, shards, span)
     share_cols = 3 * width // batches
@@ -1025,45 +1094,37 @@
         return copies
 
     def qkv_gradient():
-        kept = yield from near_sums(qkv_kept)
+        kept = [add(held["qkv_found"][2 * i], c) for i, c in enumerate(qkv_near)]
         share = yield from far_sum(kept)
-        (share,) = yield [swap_blocks(share)]
+        share = swap_blocks(share)
+        yield []
+        (share,) = yield [share]
         share = copy_columns(share, table, shards, batches, (batches, part, most), BF, outgoing)
         (share,) = yield [swap_blocks(share, "batch")]
         held["qkv_grad"] = copy_columns(share, table, shards, batches, (1, part, share_cols), F32, incoming)[0]
 
-    def vector_gradients():
-        yield []
-        cot_sums = jnp.sum(own_cot.astype(F32), axis=0, keepdims=True)
-        rows = cut_vectors([held["norm_one"], norm_sums, cot_sums], column_sums, table, shards)
-        (rows,) = yield [lax.all_to_all(rows, "seq", 0, 0, tiled=True)]
-        part_sums = jnp.sum(rows[:, :, : 6 * part], axis=0)
-        head_sums = rows[:, 0, 6 * part :].reshape(padded, 3, HEAD_DIM)[:head_count]
-        qv_sums = jnp.concatenate([head_sums[:, 0], head_sums[:, 2]]).reshape(1, 2 * width)
-        qv_sums = lax.dynamic_slice_in_dim(qv_sums, me * 2 * part, 2 * part, 1)
-        sums = jnp.concatenate([part_sums, qv_sums, fc_sums], axis=1)
-        bit = 1
-        while bit < batches:
-            (came,) = yield [lax.ppermute(sums, "batch", [(b, b ^ bit) for b in range(batches)])]
-            sums = sums + came
-            bit *= 2
-        held["sums"] = sums[0]
-
     rounds.add(qkv_gradient())
-    rounds.add(vector_gradients())
+
+    cot_sums = jnp.sum(own_cot.astype(F32), axis=0, keepdims=True)
 
     def unproject():
         return call(
-            functools.partial(unproject_kernel, shards),
+            functools.partial(unproject_kernel, shards, batches, heads),
             table,
-            [grad_projected, w_qkv, xhat_one, *proj_blocks],
-            [shape_of((span + proj_blocks[0].shape[0], width), BF)] * shards + [shape_of((2, width), F32)],
-            scratch=[pltpu.VMEM((length, width), BF)],
+            [grad_projected, w_qkv, xhat_one, norm_sums, cot_sums, column_sums, *proj_blocks],
+            [shape_of((span + proj_blocks[0].shape[0], width), BF)] * shards,
+            scratch=[
+                pltpu.VMEM((2, width), F32),
+                pltpu.VMEM((length, width), BF),
+                pltpu.VMEM((shards, 1, width), F32),
+            ],
             us=9,
             name="unproject",
         )
 
-    *g_one, held["norm_one"] = rounds.end(unproject)
+    g_one = rounds.end(unproject)
+    held["unproject"] = True
+    rounds.waits.append(held["out"])
     total = sum(term.astype(F32) for term in ring.scatter_sum(g_one))
     g_one, pieces = total[:span], -(-part // batches)
     proj_share = [total[span : span + pieces, b * out_cols : (b + 1) * out_cols] for b in range(batches)]
@@ -1071,6 +1132,17 @@
     xhat, inverse = norm_stats(own_tokens.astype(F32))
     block_out = (mixed + b_out + held["out"].reshape(span, width).astype(F32)).astype(BF)
     input_grad = (grad_mixed + norm_back(g_one, xhat, inverse, gain_one)).astype(BF)
+
+    def vector_gradients():
+        sums = jnp.concatenate([total[-1:, : 8 * part], fc_sums], axis=1)
+        bit = 1
+        while bit < batches:
+            (came,) = yield [lax.ppermute(sums, "batch", [(b, b ^ bit) for b in range(batches)])]
+            sums = sums + came
+            bit *= 2
+        held["sums"] = sums[0]
+
+    rounds.add(vector_gradients())
     rounds.finish()
 
     runs = shards // batches

time: 579 us -> 556 us (0.960)
  blocking collectives: 39.1 us -> 0 us
  starting transfers between devices: 74.4 us -> 97.3 us
  local copies, waits for them, and re-layouts: 55.4 us -> 48.9 us
    all_to_all x1 -> x0, blocking collectives: 39.1 us -> none  [swap_blocks(): lax.all_to_all(cut(value), axis, 0, 0, tiled=True).reshape(value.shape)]
    ppermute x45 -> x62, starting transfers between devices: 38.3 us -> 62.7 us  [permute(): return lax.ppermute(cut(value), axis, pairs).reshape(value.shape)]
    ppermute x45 -> x62, waiting for transfers between devices: 141 us -> 154 us  [permute(): return lax.ppermute(cut(value), axis, pairs).reshape(value.shape)]
    all_to_all x1 -> x0, waiting for transfers between devices: 10.3 us -> none  [vector_gradients(): rows, = (yield [lax.all_to_all(rows, 'seq', 0, 0, tiled=True)])]
    unnamed x171 -> x194, local copies, waits for them, and re-layouts: 36.9 us -> 31.2 us
    all_to_all x7 -> x8, starting transfers between devices: 28.9 us -> 34.1 us  [swap_blocks(): lax.all_to_all(cut(value), axis, 0, 0, tiled=True).reshape(value.shape)]
    pallas_call x21 -> x20, Pallas kernels: 159 us -> 162 us  [call(): pl.pallas_call(body, grid_spec=pltpu.PrefetchScalarGridSpec(num_scalar_pr...]
    all_to_all x7 -> x8, waiting for transfers between devices: 39 us -> 38.2 us  [swap_blocks(): lax.all_to_all(cut(value), axis, 0, 0, tiled=True).reshape(value.shape)]
  transfers between devices with their start and end apart: 59 -> 74, of which waited for: 26 -> 35; matrix products, arithmetic and copies ran while one was open for 8% -> 5% of each run, Pallas kernels for 30% -> 25%
where the time goes in v3:
time: 556 us; the launch traced here: 547 us
  waiting for transfers between devices  192 us (35%)
  Pallas kernels  177 us (32%)
  starting transfers between devices  97.3 us (18%)
  local copies, waits for them, and re-layouts  48.9 us (9%)
  other arithmetic  16.8 us (3%)
  between operations  14.9 us (3%)
    pallas_call x20, Pallas kernels, call(): pl.pallas_call(body, grid_spec=pltpu.PrefetchScalarGridSpec(num_scalar_pr...  162 us
    ppermute x62, waiting for transfers between devices, permute(): return lax.ppermute(cut(value), axis, pairs).reshape(value.shape)  154 us
    ppermute x62, starting transfers between devices, permute(): return lax.ppermute(cut(value), axis, pairs).reshape(value.shape)  62.7 us
    all_to_all x8, waiting for transfers between devices, swap_blocks(): lax.all_to_all(cut(value), axis, 0, 0, tiled=True).reshape(value.shape)  38.2 us
    all_to_all x8, starting transfers between devices, swap_blocks(): lax.all_to_all(cut(value), axis, 0, 0, tiled=True).reshape(value.shape)  34.1 us
    unnamed x194, local copies, waits for them, and re-layouts  31.2 us
    pallas_call x37, Pallas kernels, gate(): pl.pallas_call(functools.partial(gate_kernel, count, total), in_specs=blo...  14.8 us
  transfers between devices with their start and end apart: 74, of which 35 were waited for; matrix products, arithmetic and copies ran while one was open for 5% of the time, Pallas kernels for 25%

profile of v3, /device:TPU:0, one launch (start us, length us, event | category | flops | bytes accessed | tf_op | source)
XLA Modules:
  0.0 547.2 jit_solution(7405191678530088108)
XLA Ops:
  16.7 7.4 %all-to-all-start = ((bf16[8,1,27,8,192]{4,3,2,1,0:T(8,128)(2,1)}), bf16[8,1,27,8,192]{4,3,2,1,0:T(8,128)(2,1)S(1)}, u32[]{:S(2)}, u32[]{:S(2)}) async-start(bf16[8,1,27,8,192]{4,3,2,1,0:T(8,128)(2,1)} %bitcast.238), calls=%async_computation | async-start | bytes 1769472 | tf_op jit(solution)/shard_map/all_to_all | solution.py:756
  27.4 27.6 %collective-permute-done = bf16[1,16,8,1600]{3,2,1,0:T(8,128)(2,1)S(1)} collective-permute-done((bf16[1,16,8,1600]{3,2,1,0:T(8,128)(2,1)S(1)}, bf16[1,16,8,1600]{3,2,1,0:T(8,128)(2,1)S(1)}, u32[]{:S(2)}, u32[]{:S(2)}) %collective-permute-start) | collective-permute-done | bytes 409632 | tf_op jit(solution)/shard_map/ppermute | solution.py:654
  59.4 6.2 %collective-permute-start.2 = (bf16[1,16,8,1600]{3,2,1,0:T(8,128)(2,1)}, bf16[1,16,8,1600]{3,2,1,0:T(8,128)(2,1)S(1)}, u32[]{:S(2)}, u32[]{:S(2)}) collective-permute-start(bf16[1,16,8,1600]{3,2,1,0:T(8,128)(2,1)} %bitcast.268), channel_id=1, source_target_pairs={{0,2},{2,4},{4,6},{6,7},{7,5},{5,3},{3,1},{1,0},{8,10},{10,12},{12... | collective-permute-start | bytes 1228808 | tf_op jit(solution)/shard_map/ppermute | solution.py:654
  69.2 9.7 %collective-permute-done.2 = bf16[1,16,8,1600]{3,2,1,0:T(8,128)(2,1)S(1)} collective-permute-done((bf16[1,16,8,1600]{3,2,1,0:T(8,128)(2,1)}, bf16[1,16,8,1600]{3,2,1,0:T(8,128)(2,1)S(1)}, u32[]{:S(2)}, u32[]{:S(2)}) %collective-permute-start.2) | collective-permute-done | bytes 409632 | tf_op jit(solution)/shard_map/ppermute | solution.py:654
  78.9 6.0 %collective-permute-done.3 = bf16[1,16,8,1600]{3,2,1,0:T(8,128)(2,1)S(1)} collective-permute-done((bf16[1,16,8,1600]{3,2,1,0:T(8,128)(2,1)}, bf16[1,16,8,1600]{3,2,1,0:T(8,128)(2,1)S(1)}, u32[]{:S(2)}, u32[]{:S(2)}) %collective-permute-start.3) | collective-permute-done | bytes 409632 | tf_op jit(solution)/shard_map/ppermute | solution.py:654
  88.0 10.4 %collective-permute-done.5 = bf16[1,16,8,1600]{3,2,1,0:T(8,128)(2,1)S(1)} collective-permute-done((bf16[1,16,8,1600]{3,2,1,0:T(8,128)(2,1)}, bf16[1,16,8,1600]{3,2,1,0:T(8,128)(2,1)S(1)}, u32[]{:S(2)}, u32[]{:S(2)}) %collective-permute-start.5) | collective-permute-done | bytes 409632 | tf_op jit(solution)/shard_map/ppermute | solution.py:654
  126.6 11.7 %project.1 = (bf16[1024,1600]{1,0:T(8,128)(2,1)}, bf16[1024,768]{1,0:T(8,128)(2,1)}, bf16[1024,1600]{1,0:T(8,128)(2,1)}) custom-call(s32[9]{0:T(128)} %pad_add_fusion.refs_0_, f32[1,1600]{1,0:T(1,128)} %reshape.709.refs_1_, f32[1,1600]{1,0:T(1,128)} %reshape.710.refs_2_, f32[1,768]{1,0:T(1,128)} %dynamic-slice_convert_fusion.refs_3_, ...), custom_call_target="tpu_custom_call" | custom-call | flops 1760000000 | bytes 65536 | tf_op jit(solution)/shard_map/project/pallas_call | solution.py:50
  142.5 5.0 collective-permute-start.14
  147.9 14.9 %attention_forward.1 = (bf16[1024,256]{1,0:T(8,128)(2,1)}, f32[1024,256]{1,0:T(8,128)}, f32[2,2,1024]{2,1,0:T(2,128)}) custom-call(s32[9]{0:T(128)} %pad_add_fusion.refs_0_, bf16[1024,768]{1,0:T(8,128)(2,1)} %get-tuple-element.178.refs_1_), custom_call_target="tpu_custom_call" | custom-call | flops 2400000000 | bytes 65536 | tf_op jit(solution)/shard_map/attention_forward/pallas_call | solution.py:50
  174.1 7.2 %assemble.4.refs_1_ = bf16[1600,1600]{1,0:T(8,128)(2,1)} custom-call(s32[9]{0:T(128)} %pad_add_fusion.refs_0_, bf16[4,200,400]{2,1,0:T(8,128)(2,1)} %get-tuple-element.375.refs_1_, bf16[4,200,400]{2,1,0:T(8,128)(2,1)} %get-tuple-element.372.refs_2_, bf16[4,200,400]{2,1,0:T(8,128)(2,1)} %bitcast.274, bf16[4,200,400]{2,1,0:T(8,128)(2,1)} %bitcast.275, ...), custom_call_target="tpu_custom_call" | custom-call | flops 800000000 | bytes 65536 | tf_op jit(solution)/shard_map/assemble/pallas_call | solution.py:50
  181.3 5.4 collective-permute-done.20
  196.1 5.5 %mix.1 = (bf16[128,1600]{1,0:T(8,128)(2,1)}, f32[128,1600]{1,0:T(8,128)}, bf16[128,1600]{1,0:T(8,128)(2,1)}) custom-call(s32[9]{0:T(128)} %pad_add_fusion.refs_0_, bf16[128,1600]{1,0:T(8,128)(2,1)} %bitcast.193, bf16[1600,1600]{1,0:T(8,128)(2,1)} %get-tuple-element.189.refs_2_.refs_6_, f32[1,1600]{1,0:T(1,128)} %reshape.711.refs_3_, ...), custom_call_target="tpu_custom_call" | custom-call | flops 960000000 | bytes 65536 | tf_op jit(solution)/shard_map/mix/pallas_call | solution.py:50
  205.8 6.8 %collective-permute-done.22 = bf16[1,16,8,1600]{3,2,1,0:T(8,128)(2,1)S(1)} collective-permute-done((bf16[1,16,8,1600]{3,2,1,0:T(8,128)(2,1)}, bf16[1,16,8,1600]{3,2,1,0:T(8,128)(2,1)S(1)}, u32[]{:S(2)}, u32[]{:S(2)}) %collective-permute-start.22) | collective-permute-done | bytes 409632 | tf_op jit(solution)/shard_map/ppermute | solution.py:654
  216.3 8.5 %collective-permute-done.24 = bf16[1,16,8,1600]{3,2,1,0:T(8,128)(2,1)S(1)} collective-permute-done((bf16[1,16,8,1600]{3,2,1,0:T(8,128)(2,1)}, bf16[1,16,8,1600]{3,2,1,0:T(8,128)(2,1)S(1)}, u32[]{:S(2)}, u32[]{:S(2)}) %collective-permute-start.24) | collective-permute-done | bytes 409632 | tf_op jit(solution)/shard_map/ppermute | solution.py:654
  229.6 10.4 %collective-permute-done.28 = bf16[1,16,8,1600]{3,2,1,0:T(8,128)(2,1)S(1)} collective-permute-done((bf16[1,16,8,1600]{3,2,1,0:T(8,128)(2,1)}, bf16[1,16,8,1600]{3,2,1,0:T(8,128)(2,1)S(1)}, u32[]{:S(2)}, u32[]{:S(2)}) %collective-permute-start.28) | collective-permute-done | bytes 409632 | tf_op jit(solution)/shard_map/ppermute | solution.py:654
  242.9 5.3 assemble.5.refs_1_
  253.7 24.7 %mlp.1 = (bf16[1024,800]{1,0:T(8,128)(2,1)}, bf16[1024,800]{1,0:T(8,128)(2,1)}, f32[1,800]{1,0:T(1,128)}, bf16[8,128,1600]{2,1,0:T(8,128)(2,1)}, bf16[128,1600]{...) custom-call(s32[9]{0:T(128)} %pad_add_fusion.refs_0_, ...), custom_call_target="tpu_custom_call" | custom-call | flops 2400000000 | bytes 65536 | tf_op jit(solution)/shard_map/mlp/pallas_call | solution.py:50
  282.0 6.9 %collective-permute-done.33 = bf16[1,16,8,1600]{3,2,1,0:T(8,128)(2,1)S(1)} collective-permute-done((bf16[1,16,8,1600]{3,2,1,0:T(8,128)(2,1)}, bf16[1,16,8,1600]{3,2,1,0:T(8,128)(2,1)S(1)}, u32[]{:S(2)}, u32[]{:S(2)}) %collective-permute-start.33) | collective-permute-done | bytes 409632 | tf_op jit(solution)/shard_map/ppermute | solution.py:654
  293.2 6.9 %join.1.refs_4_ = bf16[8,128,1600]{2,1,0:T(8,128)(2,1)} custom-call(s32[9]{0:T(128)} %pad_add_fusion.refs_0_, bf16[8,128,1600]{2,1,0:T(8,128)(2,1)} %get-tuple-element.213.refs_1_, bf16[128,1600]{1,0:T(8,128)(2,1)} %get-tuple-element.210.refs_2_), custom_call_target="tpu_custom_call" | custom-call | flops 640000000 | bytes 65536 | tf_op jit(solution)/shard_map/join/pallas_call | solution.py:50
  306.9 9.7 %fc_grad.1 = (bf16[8,200,200]{2,1,0:T(8,128)(2,1)}, bf16[8,200,200]{2,1,0:T(8,128)(2,1)}, bf16[8,200,200]{2,1,0:T(8,128)(2,1)}, bf16[8,200,200]{2,1,0:T(8,128)(2,1)}) custom-call(s32[9]{0:T(128)} %pad_add_fusion.refs_0_, bf16[128,1600]{1,0:T(8,128)(2,1)} %get-tuple-element.192.refs_4_.refs_1_, bf16[128,1600]{1,0:T(8,128)(2,1)} %get-tuple-element.194.refs_5_.refs_2_, ...), custom_call_target="tpu_custom_call" | custom-call | flops 1440000000 | bytes 65536 | tf_op jit(solution)/shard_map/fc_grad/pallas_call | solution.py:50
  323.5 9.1 %out_grad.1 = (bf16[1,800,400]{2,1,0:T(8,128)(2,1)}, bf16[1,800,400]{2,1,0:T(8,128)(2,1)}, bf16[1,800,400]{2,1,0:T(8,128)(2,1)}, bf16[1,800,400]{2,1,0:T(8,128)(2,1)}) custom-call(s32[9]{0:T(128)} %pad_add_fusion.refs_0_, bf16[1024,800]{1,0:T(8,128)(2,1)} %get-tuple-element.230.refs_1_, bf16[128,1600]{1,0:T(8,128)(2,1)} %bitcast.196, ...), custom_call_target="tpu_custom_call" | custom-call | flops 1440000000 | bytes 65536 | tf_op jit(solution)/shard_map/out_grad/pallas_call | solution.py:50
  335.6 7.2 %unmix.1 = (f32[128,1600]{1,0:T(8,128)}, bf16[128,1600]{1,0:T(8,128)(2,1)}, f32[3,1600]{1,0:T(4,128)}, bf16[8,128,256]{2,1,0:T(8,128)(2,1)}) custom-call(s32[9]{0:T(128)} %pad_add_fusion.refs_0_, bf16[128,1600]{1,0:T(8,128)(2,1)} %get-tuple-element.235.refs_1_, bf16[128,1600]{1,0:T(8,128)(2,1)} %get-tuple-element.236.refs_2_, ...), custom_call_target="tpu_custom_call" | custom-call | flops 1120000000 | bytes 65536 | tf_op jit(solution)/shard_map/unmix/pallas_call | solution.py:50
  349.6 9.4 %collective-permute-done.47 = bf16[1,16,8,1600]{3,2,1,0:T(8,128)(2,1)S(1)} collective-permute-done((bf16[1,16,8,1600]{3,2,1,0:T(8,128)(2,1)}, bf16[1,16,8,1600]{3,2,1,0:T(8,128)(2,1)S(1)}, u32[]{:S(2)}, u32[]{:S(2)}) %collective-permute-start.47) | collective-permute-done | bytes 409632 | tf_op jit(solution)/shard_map/ppermute | solution.py:654
  359.0 15.1 %all-to-all-done.3 = bf16[8,1,16,8,256]{4,3,2,1,0:T(8,128)(2,1)S(1)} async-done(((bf16[8,1,16,8,256]{4,3,2,1,0:T(8,128)(2,1)}), bf16[8,1,16,8,256]{4,3,2,1,0:T(8,128)(2,1)S(1)}, u32[]{:S(2)}, u32[]{:S(2)}) %all-to-all-start.3) | async-done | bytes 524320 | tf_op jit(solution)/shard_map/all_to_all | solution.py:756
  376.6 14.2 %attention_backward.1 = (bf16[1024,768]{1,0:T(8,128)(2,1)}, f32[2,1,384]{2,1,0:T(1,128)}) custom-call(s32[9]{0:T(128)} %pad_add_fusion.refs_0_, bf16[1024,768]{1,0:T(8,128)(2,1)} %get-tuple-element.178.refs_1_, bf16[1024,256]{1,0:T(8,128)(2,1)} %bitcast.212, f32[1024,256]{1,0:T(8,128)} %get-tuple-element.248.refs_3_, f32[2,2,1024]{2,1,0:T(2,128)} %get-tuple-element.249.refs_4_), custom_call_target="tpu_custom_call" | custom-call | flops 2240000000 | bytes 65536 | tf_op jit(solution)/shard_map/attention_backward/pallas_call | solution.py:50
  393.9 8.8 %qkv_grad.1 = (bf16[8,200,192]{2,1,0:T(8,128)(2,1)}, bf16[8,200,192]{2,1,0:T(8,128)(2,1)}, bf16[8,200,192]{2,1,0:T(8,128)(2,1)}, bf16[8,200,192]{2,1,0:T(8,128)(2,1)}) custom-call(s32[9]{0:T(128)} %pad_add_fusion.refs_0_, bf16[1024,1600]{1,0:T(8,128)(2,1)} %get-tuple-element.282.refs_1_, bf16[1024,768]{1,0:T(8,128)(2,1)} %get-tuple-element.255.refs_1_.refs_2_), custom_call_target="tpu_custom_call" | custom-call | flops 1440000000 | bytes 65536 | tf_op jit(solution)/shard_map/qkv_grad/pallas_call | solution.py:50
  413.4 5.0 proj_grad.1
  418.4 10.5 %unproject.1 = (bf16[184,1600]{1,0:T(8,128)(2,1)}, bf16[184,1600]{1,0:T(8,128)(2,1)}, bf16[184,1600]{1,0:T(8,128)(2,1)}, bf16[184,1600]{1,0:T(8,128)(2,1)}, bf16...) custom-call(s32[9]{0:T(128)} %pad_add_fusion.refs_0_, ...), custom_call_target="tpu_custom_call" | custom-call | flops 1440000000 | bytes 65536 | tf_op jit(solution)/shard_map/unproject/pallas_call | solution.py:50
  429.0 10.1 %all-to-all-done.4 = bf16[8,1,25,8,200]{4,3,2,1,0:T(8,128)(2,1)S(1)} async-done(((bf16[8,1,25,8,200]{4,3,2,1,0:T(8,128)(2,1)}), bf16[8,1,25,8,200]{4,3,2,1,0:T(8,128)(2,1)S(1)}, u32[]{:S(2)}, u32[]{:S(2)}) %all-to-all-start.4) | async-done | bytes 640032 | tf_op jit(solution)/shard_map/all_to_all | solution.py:756
  452.4 6.4 %collective-permute-done.54 = bf16[1,23,8,1600]{3,2,1,0:T(8,128)(2,1)} collective-permute-done((bf16[1,23,8,1600]{3,2,1,0:T(8,128)(2,1)}, bf16[1,23,8,1600]{3,2,1,0:T(8,128)(2,1)}, u32[]{:S(2)}, u32[]{:S(2)}) %collective-permute-start.54) | collective-permute-done | bytes 588832 | tf_op jit(solution)/shard_map/ppermute | solution.py:654
  461.2 15.4 %collective-permute-done.56 = bf16[1,23,8,1600]{3,2,1,0:T(8,128)(2,1)S(1)} collective-permute-done((bf16[1,23,8,1600]{3,2,1,0:T(8,128)(2,1)S(1)}, bf16[1,23,8,1600]{3,2,1,0:T(8,128)(2,1)S(1)}, u32[]{:S(2)}, u32[]{:S(2)}) %collective-permute-start.56) | collective-permute-done | bytes 588832 | tf_op jit(solution)/shard_map/ppermute | solution.py:654
  495.1 8.8 %all-to-all-done.6 = bf16[4,1,25,8,384]{4,3,2,1,0:T(8,128)(2,1)S(1)} async-done(((bf16[4,1,25,8,384]{4,3,2,1,0:T(8,128)(2,1)}), bf16[4,1,25,8,384]{4,3,2,1,0:T(8,128)(2,1)S(1)}, u32[]{:S(2)}, u32[]{:S(2)}) %all-to-all-start.6) | async-done | bytes 614432 | tf_op jit(solution)/shard_map/all_to_all | solution.py:756
  (429 shorter events, 215.8 us)
Async XLA Ops:
  16.7 40.1 %all-to-all-start = ((bf16[8,1,27,8,192]{4,3,2,1,0:T(8,128)(2,1)}), bf16[8,1,27,8,192]{4,3,2,1,0:T(8,128)(2,1)S(1)}, u32[]{:S(2)}, u32[]{:S(2)}) async-start(bf16[8,1,27,8,192]{4,3,2,1,0:T(8,128)(2,1)} %bitcast.238), calls=%async_computation | async-start | bytes 1769472 | tf_op jit(solution)/shard_map/all_to_all | solution.py:756
  24.1 92.5 %all-gather.2.cloned.1.call-start = ((), (), s32[]{:S(2)}) async-start(), calls=%async_computation.9 | async-start | bytes 1843200 | tf_op jit(solution)/shard_map/all_gather | solution.py:869
  25.3 29.7 %collective-permute-start = (bf16[1,16,8,1600]{3,2,1,0:T(8,128)(2,1)S(1)}, bf16[1,16,8,1600]{3,2,1,0:T(8,128)(2,1)S(1)}, u32[]{:S(2)}, u32[]{:S(2)}) collective-permute-start(bf16[1,16,8,1600]{3,2,1,0:T(8,128)(2,1)S(1)} %bitcast.190), channel_id=1, source_target_pairs={{0,2},{2,4},{4,6},{6,7},{7,5},{5,3},{3,1},{1,0},{8,10},{10,12},{12... | collective-permute-start | bytes 1228808 | tf_op jit(solution)/shard_map/ppermute | solution.py:654
  27.3 29.5 %collective-permute-start.1 = (bf16[1,16,8,1600]{3,2,1,0:T(8,128)(2,1)S(1)}, bf16[1,16,8,1600]{3,2,1,0:T(8,128)(2,1)S(1)}, u32[]{:S(2)}, u32[]{:S(2)}) collective-permute-start(bf16[1,16,8,1600]{3,2,1,0:T(8,128)(2,1)S(1)} %bitcast.191), channel_id=1, source_target_pairs={{0,1},{2,0},{4,2},{6,4},{7,6},{5,7},{3,5},{1,3},{8,9},{10,8},{12,1... | collective-permute-start | bytes 1228808 | tf_op jit(solution)/shard_map/ppermute | solution.py:654
  57.9 27.1 %collective-permute-start.4 = (bf16[8,1,27,8,192]{4,3,2,0,1:T(8,128)(2,1)}, bf16[8,1,27,8,192]{4,3,2,0,1:T(8,128)(2,1)S(1)}, u32[]{:S(2)}, u32[]{:S(2)}) collective-permute-start(bf16[8,1,27,8,192]{4,3,2,0,1:T(8,128)(2,1)} %bitcast.205), channel_id=1, source_target_pairs={{0,16},{8,24},{16,0},{24,8},{1,17},{9,25},{17,1},{25,9},{2,18},{10... | collective-permute-start | bytes 1990664 | tf_op jit(solution)/shard_map/ppermute | solution.py:654
  59.4 19.5 %collective-permute-start.2 = (bf16[1,16,8,1600]{3,2,1,0:T(8,128)(2,1)}, bf16[1,16,8,1600]{3,2,1,0:T(8,128)(2,1)S(1)}, u32[]{:S(2)}, u32[]{:S(2)}) collective-permute-start(bf16[1,16,8,1600]{3,2,1,0:T(8,128)(2,1)} %bitcast.268), channel_id=1, source_target_pairs={{0,2},{2,4},{4,6},{6,7},{7,5},{5,3},{3,1},{1,0},{8,10},{10,12},{12... | collective-permute-start | bytes 1228808 | tf_op jit(solution)/shard_map/ppermute | solution.py:654
  65.6 19.4 %collective-permute-start.3 = (bf16[1,16,8,1600]{3,2,1,0:T(8,128)(2,1)}, bf16[1,16,8,1600]{3,2,1,0:T(8,128)(2,1)S(1)}, u32[]{:S(2)}, u32[]{:S(2)}) collective-permute-start(bf16[1,16,8,1600]{3,2,1,0:T(8,128)(2,1)} %bitcast.315), channel_id=1, source_target_pairs={{0,1},{2,0},{4,2},{6,4},{7,6},{5,7},{3,5},{1,3},{8,9},{10,8},{12,1... | collective-permute-start | bytes 1228808 | tf_op jit(solution)/shard_map/ppermute | solution.py:654
  65.6 22.4 %collective-permute-start.7 = (bf16[8,1,27,8,192]{4,3,2,0,1:T(8,128)(2,1)}, bf16[8,1,27,8,192]{4,3,2,0,1:T(8,128)(2,1)S(1)}, u32[]{:S(2)}, u32[]{:S(2)}) collective-permute-start(bf16[8,1,27,8,192]{4,3,2,0,1:T(8,128)(2,1)} %bitcast.206), channel_id=1, source_target_pairs={{0,8},{8,0},{16,24},{24,16},{1,9},{9,1},{17,25},{25,17},{2,10},{10... | collective-permute-start | bytes 1990664 | tf_op jit(solution)/shard_map/ppermute | solution.py:654
  112.5 28.8 %all-to-all-start.1 = ((bf16[8,1,25,8,200]{4,3,2,1,0:T(8,128)(2,1)}), bf16[8,1,25,8,200]{4,3,2,1,0:T(8,128)(2,1)S(1)}, u32[]{:S(2)}, u32[]{:S(2)}) async-start(bf16[8,1,25,8,200]{4,3,2,1,0:T(8,128)(2,1)} %bitcast.200), calls=%async_computation.1 | async-start | bytes 1638400 | tf_op jit(solution)/shard_map/all_to_all | solution.py:756
  119.9 21.4 %collective-permute-start.10 = (bf16[4,1,25,8,400]{4,3,2,0,1:T(8,128)(2,1)}, bf16[4,1,25,8,400]{4,3,2,0,1:T(8,128)(2,1)S(1)}, u32[]{:S(2)}, u32[]{:S(2)}) collective-permute-start(bf16[4,1,25,8,400]{4,3,2,0,1:T(8,128)(2,1)} %get-tuple-element.373), channel_id=1, source_target_pairs={{0,16},{8,24},{16,0},{24,8},{1,17},{9,25},{17,1},{25,9},{2,18},{10... | collective-permute-start | bytes 1920008 | tf_op jit(solution)/shard_map/ppermute | solution.py:654
  123.7 16.8 %collective-permute-start.12 = (bf16[1,16,8,1600]{3,2,1,0:T(8,128)(2,1)}, bf16[1,16,8,1600]{3,2,1,0:T(8,128)(2,1)S(1)}, u32[]{:S(2)}, u32[]{:S(2)}) collective-permute-start(bf16[1,16,8,1600]{3,2,1,0:T(8,128)(2,1)} %bitcast.266), channel_id=1, source_target_pairs={{0,1},{2,0},{4,2},{6,4},{7,6},{5,7},{3,5},{1,3},{8,9},{10,8},{12,1... | collective-permute-start | bytes 1228808 | tf_op jit(solution)/shard_map/ppermute | solution.py:654
  125.4 37.4 %collective-permute-start.13 = (bf16[4,1,25,8,400]{4,3,2,0,1:T(8,128)(2,1)}, bf16[4,1,25,8,400]{4,3,2,0,1:T(8,128)(2,1)S(1)}, u32[]{:S(2)}, u32[]{:S(2)}) collective-permute-start(bf16[4,1,25,8,400]{4,3,2,0,1:T(8,128)(2,1)} %get-tuple-element.374), channel_id=1, source_target_pairs={{0,16},{8,24},{16,0},{24,8},{1,17},{9,25},{17,1},{25,9},{2,18},{10... | collective-permute-start | bytes 1920008 | tf_op jit(solution)/shard_map/ppermute | solution.py:654
  142.5 20.3 %collective-permute-start.14 = (bf16[1,16,8,1600]{3,2,1,0:T(8,128)(2,1)}, bf16[1,16,8,1600]{3,2,1,0:T(8,128)(2,1)S(1)}, u32[]{:S(2)}, u32[]{:S(2)}) collective-permute-start(bf16[1,16,8,1600]{3,2,1,0:T(8,128)(2,1)} %bitcast.234), channel_id=1, source_target_pairs={{0,2},{2,4},{4,6},{6,7},{7,5},{5,3},{3,1},{1,0},{8,10},{10,12},{12... | collective-permute-start | bytes 1228808 | tf_op jit(solution)/shard_map/ppermute | solution.py:654
  147.8 23.0 %collective-permute-start.16 = (bf16[4,1,25,8,400]{4,3,2,0,1:T(8,128)(2,1)}, bf16[4,1,25,8,400]{4,3,2,0,1:T(8,128)(2,1)S(1)}, u32[]{:S(2)}, u32[]{:S(2)}) collective-permute-start(bf16[4,1,25,8,400]{4,3,2,0,1:T(8,128)(2,1)} %get-tuple-element.373), channel_id=1, source_target_pairs={{0,8},{8,0},{16,24},{24,16},{1,9},{9,1},{17,25},{25,17},{2,10},{10... | collective-permute-start | bytes 1920008 | tf_op jit(solution)/shard_map/ppermute | solution.py:654
  164.0 25.0 %all-to-all-start.2 = ((bf16[8,1,16,8,256]{4,3,2,1,0:T(8,128)(2,1)}), bf16[8,1,16,8,256]{4,3,2,1,0:T(8,128)(2,1)S(1)}, u32[]{:S(2)}, u32[]{:S(2)}) async-start(bf16[8,1,16,8,256]{4,3,2,1,0:T(8,128)(2,1)} %bitcast.263), calls=%async_computation.2 | async-start | bytes 1048576 | tf_op jit(solution)/shard_map/all_to_all | solution.py:756
  168.2 290.6 %reduce-scatter.2.cloned.1.call-start = ((), (), s32[]{:S(2)}) async-start(), calls=%async_computation.10 | async-start | bytes 3833856 | tf_op jit(solution)/shard_map/reduce_scatter | solution.py:1021
  169.0 17.7 %collective-permute-start.20 = (bf16[1,16,8,1600]{3,2,1,0:T(8,128)(2,1)}, bf16[1,16,8,1600]{3,2,1,0:T(8,128)(2,1)S(1)}, u32[]{:S(2)}, u32[]{:S(2)}) collective-permute-start(bf16[1,16,8,1600]{3,2,1,0:T(8,128)(2,1)} %bitcast.219), channel_id=1, source_target_pairs={{0,2},{2,4},{4,6},{6,7},{7,5},{5,3},{3,1},{1,0},{8,10},{10,12},{12... | collective-permute-start | bytes 1228808 | tf_op jit(solution)/shard_map/ppermute | solution.py:654
  171.7 17.2 %collective-permute-start.21 = (bf16[1,16,8,1600]{3,2,1,0:T(8,128)(2,1)}, bf16[1,16,8,1600]{3,2,1,0:T(8,128)(2,1)S(1)}, u32[]{:S(2)}, u32[]{:S(2)}) collective-permute-start(bf16[1,16,8,1600]{3,2,1,0:T(8,128)(2,1)} %bitcast.221), channel_id=1, source_target_pairs={{0,1},{2,0},{4,2},{6,4},{7,6},{5,7},{3,5},{1,3},{8,9},{10,8},{12,1... | collective-permute-start | bytes 1228808 | tf_op jit(solution)/shard_map/ppermute | solution.py:654
  204.4 22.1 %collective-permute-start.27 = (bf16[8,1,25,8,200]{4,3,2,0,1:T(8,128)(2,1)}, bf16[8,1,25,8,200]{4,3,2,0,1:T(8,128)(2,1)S(1)}, u32[]{:S(2)}, u32[]{:S(2)}) collective-permute-start(bf16[8,1,25,8,200]{4,3,2,0,1:T(8,128)(2,1)} %bitcast.202), channel_id=1, source_target_pairs={{0,16},{8,24},{16,0},{24,8},{1,17},{9,25},{17,1},{25,9},{2,18},{10... | collective-permute-start | bytes 1920008 | tf_op jit(solution)/shard_map/ppermute | solution.py:654
  280.7 19.4 %collective-permute-start.37 = (bf16[1,16,8,1600]{3,2,1,0:T(8,128)(2,1)}, bf16[1,16,8,1600]{3,2,1,0:T(8,128)(2,1)S(1)}, u32[]{:S(2)}, u32[]{:S(2)}) collective-permute-start(bf16[1,16,8,1600]{3,2,1,0:T(8,128)(2,1)} %bitcast.308), channel_id=1, source_target_pairs={{0,8},{8,0},{16,24},{24,16},{1,9},{9,1},{17,25},{25,17},{2,10},{10... | collective-permute-start | bytes 1228808 | tf_op jit(solution)/shard_map/ppermute | solution.py:654
  280.7 19.4 %collective-permute-start.36 = (bf16[1,16,8,1600]{3,2,1,0:T(8,128)(2,1)}, bf16[1,16,8,1600]{3,2,1,0:T(8,128)(2,1)S(1)}, u32[]{:S(2)}, u32[]{:S(2)}) collective-permute-start(bf16[1,16,8,1600]{3,2,1,0:T(8,128)(2,1)} %bitcast.328), channel_id=1, source_target_pairs={{0,1},{2,0},{4,2},{6,4},{7,6},{5,7},{3,5},{1,3},{8,9},{10,8},{12,1... | collective-permute-start | bytes 1228808 | tf_op jit(solution)/shard_map/ppermute | solution.py:654
  342.8 31.4 %all-to-all-start.3 = ((bf16[8,1,16,8,256]{4,3,2,1,0:T(8,128)(2,1)}), bf16[8,1,16,8,256]{4,3,2,1,0:T(8,128)(2,1)S(1)}, u32[]{:S(2)}, u32[]{:S(2)}) async-start(bf16[8,1,16,8,256]{4,3,2,1,0:T(8,128)(2,1)} %bitcast.264), calls=%async_computation.4 | async-start | bytes 1048576 | tf_op jit(solution)/shard_map/all_to_all | solution.py:756
  375.0 18.0 %collective-permute-start.48 = (bf16[8,1,25,8,200]{4,3,2,0,1:T(8,128)(2,1)}, bf16[8,1,25,8,200]{4,3,2,0,1:T(8,128)(2,1)S(1)}, u32[]{:S(2)}, u32[]{:S(2)}) collective-permute-start(bf16[8,1,25,8,200]{4,3,2,0,1:T(8,128)(2,1)} %bitcast.251), channel_id=1, source_target_pairs={{0,16},{8,24},{16,0},{24,8},{1,17},{9,25},{17,1},{25,9},{2,18},{10... | collective-permute-start | bytes 1920008 | tf_op jit(solution)/shard_map/ppermute | solution.py:654
  404.4 34.7 %all-to-all-start.4 = ((bf16[8,1,25,8,200]{4,3,2,1,0:T(8,128)(2,1)}), bf16[8,1,25,8,200]{4,3,2,1,0:T(8,128)(2,1)S(1)}, u32[]{:S(2)}, u32[]{:S(2)}) async-start(bf16[8,1,25,8,200]{4,3,2,1,0:T(8,128)(2,1)} %fusion.11), calls=%async_computation.5 | async-start | bytes 1638400 | tf_op jit(solution)/shard_map/all_to_all | solution.py:756
  411.2 27.9 %collective-permute-start.53 = (bf16[8,1,25,8,192]{4,3,2,0,1:T(8,128)(2,1)S(1)}, bf16[8,1,25,8,192]{4,3,2,0,1:T(8,128)(2,1)S(1)}, u32[]{:S(2)}, u32[]{:S(2)}) collective-permute-start(bf16[8,1,25,8,192]{4,3,2,0,1:T(8,128)(2,1)S(1)} %fusion.12), channel_id=1, source_target_pairs={{0,16},{8,24},{16,0},{24,8},{1,17},{9,25},{17,1},{25,9},{2,18},{10... | collective-permute-start | bytes 1843208 | tf_op jit(solution)/shard_map/ppermute | solution.py:654
  440.3 18.5 %collective-permute-start.54 = (bf16[1,23,8,1600]{3,2,1,0:T(8,128)(2,1)}, bf16[1,23,8,1600]{3,2,1,0:T(8,128)(2,1)}, u32[]{:S(2)}, u32[]{:S(2)}) collective-permute-start(bf16[1,23,8,1600]{3,2,1,0:T(8,128)(2,1)} %bitcast.282), channel_id=1, source_target_pairs={{0,2},{2,4},{4,6},{6,7},{7,5},{5,3},{3,1},{1,0},{8,10},{10,12},{12... | collective-permute-start | bytes 1766408 | tf_op jit(solution)/shard_map/ppermute | solution.py:654
  444.0 32.6 %all-to-all-start.5 = ((bf16[8,1,25,8,192]{4,3,2,1,0:T(8,128)(2,1)}), bf16[8,1,25,8,192]{4,3,2,1,0:T(8,128)(2,1)S(1)}, u32[]{:S(2)}, u32[]{:S(2)}) async-start(bf16[8,1,25,8,192]{4,3,2,1,0:T(8,128)(2,1)} %fusion.13), calls=%async_computation.6 | async-start | bytes 1638400 | tf_op jit(solution)/shard_map/all_to_all | solution.py:756
  448.9 27.7 %collective-permute-start.57 = (bf16[1,4,25,8,400]{4,3,2,1,0:T(8,128)(2,1)}, bf16[1,4,25,8,400]{4,3,2,1,0:T(8,128)(2,1)S(1)}, u32[]{:S(2)}, u32[]{:S(2)}) collective-permute-start(bf16[1,4,25,8,400]{4,3,2,1,0:T(8,128)(2,1)} %bitcast.249), channel_id=1, source_target_pairs={{0,16},{8,24},{16,0},{24,8},{1,17},{9,25},{17,1},{25,9},{2,18},{10... | collective-permute-start | bytes 1920008 | tf_op jit(solution)/shard_map/ppermute | solution.py:654
  450.4 26.3 %collective-permute-start.56 = (bf16[1,23,8,1600]{3,2,1,0:T(8,128)(2,1)S(1)}, bf16[1,23,8,1600]{3,2,1,0:T(8,128)(2,1)S(1)}, u32[]{:S(2)}, u32[]{:S(2)}) collective-permute-start(bf16[1,23,8,1600]{3,2,1,0:T(8,128)(2,1)S(1)} %bitcast.283), channel_id=1, source_target_pairs={{0,1},{2,0},{4,2},{6,4},{7,6},{5,7},{3,5},{1,3},{8,9},{10,8},{12,1... | collective-permute-start | bytes 1766408 | tf_op jit(solution)/shard_map/ppermute | solution.py:654
  461.1 19.3 %collective-permute-start.55 = (bf16[1,23,8,1600]{3,2,1,0:T(8,128)(2,1)}, bf16[1,23,8,1600]{3,2,1,0:T(8,128)(2,1)}, u32[]{:S(2)}, u32[]{:S(2)}) collective-permute-start(bf16[1,23,8,1600]{3,2,1,0:T(8,128)(2,1)} %bitcast.288), channel_id=1, source_target_pairs={{0,2},{2,4},{4,6},{6,7},{7,5},{5,3},{3,1},{1,0},{8,10},{10,12},{12... | collective-permute-start | bytes 1766408 | tf_op jit(solution)/shard_map/ppermute | solution.py:654
  483.2 20.6 %collective-permute-start.58 = (bf16[1,23,8,1600]{3,2,1,0:T(8,128)(2,1)}, bf16[1,23,8,1600]{3,2,1,0:T(8,128)(2,1)S(1)}, u32[]{:S(2)}, u32[]{:S(2)}) collective-permute-start(bf16[1,23,8,1600]{3,2,1,0:T(8,128)(2,1)} %bitcast.327), channel_id=1, source_target_pairs={{0,2},{2,4},{4,6},{6,7},{7,5},{5,3},{3,1},{1,0},{8,10},{10,12},{12... | collective-permute-start | bytes 1766408 | tf_op jit(solution)/shard_map/ppermute | solution.py:654
  507.9 18.1 %collective-permute-start.60 = (bf16[1,23,8,1600]{3,2,1,0:T(8,128)(2,1)}, bf16[1,23,8,1600]{3,2,1,0:T(8,128)(2,1)}, u32[]{:S(2)}, u32[]{:S(2)}) collective-permute-start(bf16[1,23,8,1600]{3,2,1,0:T(8,128)(2,1)} %bitcast.284), channel_id=1, source_target_pairs={{0,2},{2,4},{4,6},{6,7},{7,5},{5,3},{3,1},{1,0},{8,10},{10,12},{12... | collective-permute-start | bytes 1766408 | tf_op jit(solution)/shard_map/ppermute | solution.py:654
  (136 other events, 808.3 us)
Sparse Core Ops, SparseCore 0:
  27.7 56.3 all-gather.1
  335.7 95.6 reduce-scatter.1

commit v4 on v3

--- a/solution.py
+++ b/solution.py
@@ -86,100 +86,111 @@
 
 def forward_kernel(tile, unrolled, table, x_ref, low_ref, full_ref, log_ref, value_t):
     tiles = x_ref.shape[0] // tile
-    for head in range(2):
-        base = head * HEAD_COLS
-        k_cols = pl.ds(base + HEAD_DIM, HEAD_DIM)
-        out_cols = pl.ds(head * HEAD_DIM, HEAD_DIM)
-
-        def turn(j, carry):
-            value_t[j] = x_ref[rows_of(j, tile), pl.ds(base + 2 * HEAD_DIM, HEAD_DIM)].T
-            return carry
-
-        steps(tiles, unrolled, turn, 0)
-
-        def query_tile(i, carry):
-            rows = rows_of(i, tile)
-            query = x_ref[rows, pl.ds(base, HEAD_DIM)] * jnp.asarray(SCALE, BF)
-
-            def add(j, state, masked):
-                top, total, acc = state
-                scores = dot_nt(x_ref[rows_of(j, tile), k_cols], query)
+    heads = range(2)
+    cols = lambda head, kind: pl.ds(head * HEAD_COLS + kind * HEAD_DIM, HEAD_DIM)
+
+    def turn(j, carry):
+        for head in heads:
+            value_t[head, j] = x_ref[rows_of(j, tile), cols(head, 2)].T
+        return carry
+
+    steps(tiles, unrolled, turn, 0)
+
+    def query_tile(i, carry):
+        rows = rows_of(i, tile)
+        queries = [x_ref[rows, cols(head, 0)] * jnp.asarray(SCALE, BF) for head in heads]
+
+        def add(j, states, masked):
+            key_rows = rows_of(j, tile)
+            scores = [dot_nt(x_ref[key_rows, cols(head, 1)], queries[head]) for head in heads]
+            found = []
+            for head in heads:
+                (top, total, acc), score = states[head], scores[head]
                 if masked:
-                    scores = jnp.where(causal(tile), scores, FLOOR_SCORE)
-                new_top = jnp.maximum(top, jnp.max(scores, axis=0, keepdims=True))
-                probs = jnp.exp(scores - new_top)
+                    score = jnp.where(causal(tile), score, FLOOR_SCORE)
+                new_top = jnp.maximum(top, jnp.max(score, axis=0, keepdims=True))
+                probs = jnp.exp(score - new_top)
                 fade = jnp.exp(top - new_top)
                 total = total * fade + jnp.sum(probs, axis=0, keepdims=True)
-                acc = acc * fade + dot_nn(value_t[j], probs.astype(BF))
-                return new_top, total, acc
-
-            state = (
-                jnp.full((1, tile), FLOOR_SCORE, F32),
-                jnp.zeros((1, tile), F32),
-                jnp.zeros((HEAD_DIM, tile), F32),
-            )
-            state = steps(i, unrolled, lambda j, s: add(j, s, False), state)
-            top, total, acc = add(i, state, True)
+                acc = acc * fade + dot_nn(value_t[head, j], probs.astype(BF))
+                found.append((new_top, total, acc))
+            return tuple(found)
+
+        state = (
+            jnp.full((1, tile), FLOOR_SCORE, F32),
+            jnp.zeros((1, tile), F32),
+            jnp.zeros((HEAD_DIM, tile), F32),
+        )
+        states = steps(i, unrolled, lambda j, s: add(j, s, False), (state, state))
+        for head, (top, total, acc) in enumerate(add(i, states, True)):
             result = (acc / total).T
+            out_cols = pl.ds(head * HEAD_DIM, HEAD_DIM)
             low_ref[rows, out_cols] = result.astype(BF)
             full_ref[rows, out_cols] = result
             log_ref[0, pl.ds(head, 1), rows] = top + jnp.log(total)
-            return carry
-
-        steps(tiles, unrolled, query_tile, 0)
+        return carry
+
+    steps(tiles, unrolled, query_tile, 0)
 
 
 def backward_kernel(
     tile, unrolled, table, x_ref, grad_ref, full_ref, log_ref, dx_ref, sum_ref, key_t, key_acc, value_acc
 ):
     tiles = x_ref.shape[0] // tile
-    for head in range(2):
-        base = head * HEAD_COLS
-        q_cols = pl.ds(base, HEAD_DIM)
-        k_cols = pl.ds(base + HEAD_DIM, HEAD_DIM)
-        v_cols = pl.ds(base + 2 * HEAD_DIM, HEAD_DIM)
-        out_cols = pl.ds(head * HEAD_DIM, HEAD_DIM)
-
-        def turn(j, carry):
-            key_t[j] = x_ref[rows_of(j, tile), k_cols].T
-            return carry
-
-        steps(tiles, unrolled, turn, 0)
-        key_acc[...] = jnp.zeros_like(key_acc)
-        value_acc[...] = jnp.zeros_like(value_acc)
-
-        def query_tile(i, query_sum):
-            rows = rows_of(i, tile)
-            query = x_ref[rows, q_cols] * jnp.asarray(SCALE, BF)
-            grad = grad_ref[rows, out_cols]
-            delta = jnp.sum((grad.astype(F32) * full_ref[rows, out_cols]).T, axis=0, keepdims=True)
-            log_row = log_ref[0, pl.ds(head, 1), rows]
-
-            def add(j, acc, masked):
-                key_rows = rows_of(j, tile)
-                scores = dot_nt(x_ref[key_rows, k_cols], query)
-                probs = jnp.exp(scores - log_row)
+    heads = range(2)
+    cols = lambda head, kind: pl.ds(head * HEAD_COLS + kind * HEAD_DIM, HEAD_DIM)
+
+    def turn(j, carry):
+        for head in heads:
+            key_t[head, j] = x_ref[rows_of(j, tile), cols(head, 1)].T
+        return carry
+
+    steps(tiles, unrolled, turn, 0)
+    key_acc[...] = jnp.zeros_like(key_acc)
+    value_acc[...] = jnp.zeros_like(value_acc)
+
+    def query_tile(i, query_sums):
+        rows = rows_of(i, tile)
+        queries, grads, deltas, logs = [], [], [], []
+        for head in heads:
+            out_cols = pl.ds(head * HEAD_DIM, HEAD_DIM)
+            queries.append(x_ref[rows, cols(head, 0)] * jnp.asarray(SCALE, BF))
+            grads.append(grad_ref[rows, out_cols])
+            product = grads[head].astype(F32) * full_ref[rows, out_cols]
+            deltas.append(jnp.sum(product.T, axis=0, keepdims=True))
+            logs.append(log_ref[0, pl.ds(head, 1), rows])
+
+        def add(j, accs, masked):
+            key_rows = rows_of(j, tile)
+            scores = [dot_nt(x_ref[key_rows, cols(head, 1)], queries[head]) for head in heads]
+            grad_probs = [dot_nt(x_ref[key_rows, cols(head, 2)], grads[head]) for head in heads]
+            found = []
+            for head in heads:
+                probs = jnp.exp(scores[head] - logs[head])
                 if masked:
                     probs = jnp.where(causal(tile), probs, 0.0)
-                grad_probs = dot_nt(x_ref[key_rows, v_cols], grad)
-                grad_scores = (probs * (grad_probs - delta)).astype(BF)
-                value_acc[key_rows, :] += dot_nn(probs.astype(BF), grad)
-                key_acc[key_rows, :] += dot_nn(grad_scores, query)
-                return acc + dot_nn(key_t[j], grad_scores)
-
-            acc = jnp.zeros((HEAD_DIM, tile), F32)
-            acc = steps(i, unrolled, lambda j, s: add(j, s, False), acc)
-            acc = add(i, acc, True)
+                grad_scores = (probs * (grad_probs[head] - deltas[head])).astype(BF)
+                value_acc[head, key_rows, :] += dot_nn(probs.astype(BF), grads[head])
+                key_acc[head, key_rows, :] += dot_nn(grad_scores, queries[head])
+                found.append(accs[head] + dot_nn(key_t[head, j], grad_scores))
+            return tuple(found)
+
+        acc = jnp.zeros((HEAD_DIM, tile), F32)
+        accs = steps(i, unrolled, lambda j, s: add(j, s, False), (acc, acc))
+        sums = []
+        for head, acc in enumerate(add(i, accs, True)):
             result = acc.T * SCALE
-            dx_ref[rows, q_cols] = result.astype(BF)
-            return query_sum + jnp.sum(result, axis=0, keepdims=True)
-
-        query_sum = steps(tiles, unrolled, query_tile, jnp.zeros((1, HEAD_DIM), F32))
-        dx_ref[:, k_cols] = key_acc[...].astype(BF)
-        dx_ref[:, v_cols] = value_acc[...].astype(BF)
-        sum_ref[0, :, q_cols] = query_sum
-        sum_ref[0, :, k_cols] = jnp.sum(key_acc[...], axis=0, keepdims=True)
-        sum_ref[0, :, v_cols] = jnp.sum(value_acc[...], axis=0, keepdims=True)
+            dx_ref[rows, cols(head, 0)] = result.astype(BF)
+            sums.append(query_sums[head] + jnp.sum(result, axis=0, keepdims=True))
+        return tuple(sums)
+
+    query_sums = steps(tiles, unrolled, query_tile, (jnp.zeros((1, HEAD_DIM), F32),) * 2)
+    for head in heads:
+        dx_ref[:, cols(head, 1)] = key_acc[head].astype(BF)
+        dx_ref[:, cols(head, 2)] = value_acc[head].astype(BF)
+        sum_ref[0, :, cols(head, 0)] = query_sums[head]
+        sum_ref[0, :, cols(head, 1)] = jnp.sum(key_acc[head], axis=0, keepdims=True)
+        sum_ref[0, :, cols(head, 2)] = jnp.sum(value_acc[head], axis=0, keepdims=True)
 
 
 def attention_forward(projected, table, heads):
@@ -204,7 +215,7 @@
             pl.BlockSpec((length, narrow), columns),
             pl.BlockSpec((1, 2, length), lambda g, t: (g, 0, 0)),
         ],
-        scratch=[pltpu.VMEM((tiles, HEAD_DIM, tile), BF)],
+        scratch=[pltpu.VMEM((2, tiles, HEAD_DIM, tile), BF)],
         us=15,
         name="attention_forward",
     )
@@ -233,9 +244,9 @@
             pl.BlockSpec((1, 1, wide), lambda g, t: (g, 0, 0)),
         ],
         scratch=[
-            pltpu.VMEM((tiles, HEAD_DIM, tile), BF),
-            pltpu.VMEM((length, HEAD_DIM), F32),
-            pltpu.VMEM((length, HEAD_DIM), F32),
+            pltpu.VMEM((2, tiles, HEAD_DIM, tile), BF),
+            pltpu.VMEM((2, length, HEAD_DIM), F32),
+            pltpu.VMEM((2, length, HEAD_DIM), F32),
         ],
         us=14,
         wait=wait,
@@ -371,42 +382,51 @@
 def mlp_kernel(shards, group, table, fc, bias, out, *refs):
     blocks, cotangents, refs = refs[:shards], refs[shards : 2 * shards], refs[2 * shards :]
     act, low, sums, results = refs[:4]
-    shares, (normed, cots) = refs[4 : 4 + shards], refs[4 + shards :]
-    step = pl.program_id(0)
+    shares, refs = refs[4 : 4 + shards], refs[4 + shards :]
+    fc_in, out_in, normed, cots, act_here, low_here, results_here, shares_here, came, left = refs
     span = blocks[0].shape[0]
+    pairs = [(fc, fc_in), (out, out_in)]
+    for r in range(shards):
+        pairs += [(blocks[r], normed.at[r]), (cotangents[r], cots.at[r])]
+    copies = [pltpu.make_async_copy(a, b, came.at[i]) for i, (a, b) in enumerate(pairs)]
+    for i in [0, *range(2, 2 + 2 * group), 1, *range(2 + 2 * group, len(copies))]:
+        copies[i].start()
+    copies[0].wait()
+    sums[...] = jnp.zeros_like(sums)
+    sent = []
+
+    def send(source, target):
+        copy = pltpu.make_async_copy(source, target, left.at[len(sent)])
+        copy.start()
+        sent.append(copy)
+
     for first in range(0, shards, group):
-
-        @pl.when(step == first // group)
-        def _(first=first):
-            for i in range(group):
-                normed[i * span : (i + 1) * span, :] = blocks[first + i][...]
-                cots[i * span : (i + 1) * span, :] = cotangents[first + i][...]
-
-    hidden = dot_nn(normed[...], fc[...]) + bias[...]
-    activated, slope = gelu_both(hidden)
-    act[...] = activated.astype(BF)
-    grad = dot_nt(cots[...], out[...]) * slope
-    total = jnp.sum(grad, axis=0, keepdims=True)
-
-    @pl.when(step == 0)
-    def _():
-        sums[...] = total
-
-    @pl.when(step > 0)
-    def _():
-        sums[...] += total
-
-    low[...] = grad.astype(BF)
-    share = dot_nt(low[...], fc[...]).astype(BF)
-    result = dot_nn(act[...], out[...]).astype(BF)
-    for i in range(group):
-        results[i] = result[i * span : (i + 1) * span, :]
-    for first in range(0, shards, group):
-
-        @pl.when(step == first // group)
-        def _(first=first):
-            for i in range(group):
-                shares[first + i][...] = share[i * span : (i + 1) * span, :]
+        places = range(first, first + group)
+        rows = pl.ds(first * span, group * span)
+        some = pl.ds(first, group)
+        for r in places:
+            copies[2 + 2 * r].wait()
+            copies[3 + 2 * r].wait()
+        flat = lambda ref: ref[some].reshape(group * span, ref.shape[2])
+        hidden = dot_nn(flat(normed), fc_in[...]) + bias[...]
+        activated, slope = gelu_both(hidden)
+        act_here[rows, :] = activated.astype(BF)
+        if not first:
+            copies[1].wait()
+        grad = dot_nt(flat(cots), out_in[...]) * slope
+        sums[...] += jnp.sum(grad, axis=0, keepdims=True)
+        low_here[rows, :] = grad.astype(BF)
+        share = dot_nt(low_here[rows, :], fc_in[...]).astype(BF)
+        shares_here[some] = share.reshape(group, span, share.shape[1])
+        for r in places:
+            send(shares_here.at[r], shares[r])
+        send(act_here.at[rows, :], act.at[rows, :])
+        send(low_here.at[rows, :], low.at[rows, :])
+        result = dot_nn(act_here[rows, :], out_in[...]).astype(BF)
+        results_here[some] = result.reshape(group, span, result.shape[1])
+        send(results_here.at[some], results.at[some])
+    for copy in sent:
+        copy.wait()
 
 
 def mlp_part(blocks, cotangents, fc, bias, out, table):
@@ -419,28 +439,33 @@
         first, second = halves
         results = jnp.concatenate([first[3], second[3]])
         return first[0] + second[0], first[1] + second[1], first[2] + second[2], results, first[4] + second[4]
-    group = min(shards, max(1, 512 // span))
+    group = min(shards, max(1, 256 // span))
     rows_at = lambda cols: pl.BlockSpec((group * span, cols), lambda g, t: (g, 0))
+    anywhere = pl.BlockSpec(memory_space=pl.ANY)
+    stack = pltpu.VMEM((shards, span, width), BF)
     got = call(
         functools.partial(mlp_kernel, shards, group),
         table,
         [fc, bias, out, *blocks, *cotangents],
         [shape_of((rows, units), BF)] * 2
-        + [
-            shape_of((1, units), F32),
-            shape_of((shards, span, width), BF),
-        ]
+        + [shape_of((1, units), F32), shape_of((shards, span, width), BF)]
         + [shape_of((span, width), BF)] * shards,
-        grid=(shards // group,),
-        out_specs=[
-            rows_at(units),
-            rows_at(units),
-            whole(1, units),
-            pl.BlockSpec((group, span, width), lambda g, t: (g, 0, 0)),
-        ]
-        + [whole(span, width)] * shards,
-        scratch=[pltpu.VMEM((group * span, width), BF)] * 2,
-        us=15,
+        grid=(1,),
+        in_specs=[anywhere, whole(1, units)] + [anywhere] * (1 + 2 * shards),
+        out_specs=[anywhere, anywhere, whole(1, units)] + [anywhere] * (1 + shards),
+        scratch=[
+            pltpu.VMEM(fc.shape, BF),
+            pltpu.VMEM(out.shape, BF),
+            stack,
+            stack,
+            pltpu.VMEM((rows, units), BF),
+            pltpu.VMEM((rows, units), BF),
+            stack,
+            stack,
+            pltpu.SemaphoreType.DMA((2 + 2 * shards,)),
+            pltpu.SemaphoreType.DMA((shards + 3 * (shards // group),)),
+        ],
+        us=18,
         name="mlp",
     )
     return got[:1], got[1:2], got[2], got[3], got[4:]
@@ -1135,11 +1160,11 @@
 
     def vector_gradients():
         sums = jnp.concatenate([total[-1:, : 8 * part], fc_sums], axis=1)
-        bit = 1
-        while bit < batches:
-            (came,) = yield [lax.ppermute(sums, "batch", [(b, b ^ bit) for b in range(batches)])]
-            sums = sums + came
-            bit *= 2
+        came = yield [
+            lax.ppermute(sums, "batch", [(b, b ^ apart) for b in range(batches)])
+            for apart in range(1, batches)
+        ]
+        sums = sums + sum(came)
         held["sums"] = sums[0]
 
     rounds.add(vector_gradients())

time: 556 us -> 549 us (0.987)
  Pallas kernels: 177 us -> 167 us
    pallas_call x20, Pallas kernels: 162 us -> 152 us  [call(): pl.pallas_call(body, grid_spec=pltpu.PrefetchScalarGridSpec(num_scalar_pr...]
    pallas_call x37 -> x36, Pallas kernels: 14.8 us -> 14.8 us  [gate(): pl.pallas_call(functools.partial(gate_kernel, count, total), in_specs=blo...]
  transfers between devices with their start and end apart: 74 -> 75, of which waited for: 35 -> 36; matrix products, arithmetic and copies ran while one was open for 5% -> 5% of each run, Pallas kernels for 25% -> 24%
where the time goes in v4:
time: 549 us; the launch traced here: 540 us
  waiting for transfers between devices  194 us (35%)
  Pallas kernels  167 us (30%)
  starting transfers between devices  100 us (18%)
  local copies, waits for them, and re-layouts  48.3 us (9%)
  other arithmetic  15.5 us (3%)
  between operations  15 us (3%)
    ppermute x62, waiting for transfers between devices, permute(): return lax.ppermute(cut(value), axis, pairs).reshape(value.shape)  155 us
    pallas_call x20, Pallas kernels, call(): pl.pallas_call(body, grid_spec=pltpu.PrefetchScalarGridSpec(num_scalar_pr...  152 us
    ppermute x62, starting transfers between devices, permute(): return lax.ppermute(cut(value), axis, pairs).reshape(value.shape)  63.5 us
    all_to_all x8, waiting for transfers between devices, swap_blocks(): lax.all_to_all(cut(value), axis, 0, 0, tiled=True).reshape(value.shape)  38.6 us
    all_to_all x8, starting transfers between devices, swap_blocks(): lax.all_to_all(cut(value), axis, 0, 0, tiled=True).reshape(value.shape)  34.9 us
    unnamed x194, local copies, waits for them, and re-layouts  30.5 us
    pallas_call x36, Pallas kernels, gate(): pl.pallas_call(functools.partial(gate_kernel, count, total), in_specs=blo...  14.8 us
  transfers between devices with their start and end apart: 75, of which 36 were waited for; matrix products, arithmetic and copies ran while one was open for 5% of the time, Pallas kernels for 24%

profile of v4, /device:TPU:0, one launch (start us, length us, event | category | flops | bytes accessed | tf_op | source)
XLA Modules:
  0.0 540.1 jit_solution(15393557144441981054)
XLA Ops:
  16.7 7.4 %all-to-all-start = ((bf16[8,1,27,8,192]{4,3,2,1,0:T(8,128)(2,1)}), bf16[8,1,27,8,192]{4,3,2,1,0:T(8,128)(2,1)S(1)}, u32[]{:S(2)}, u32[]{:S(2)}) async-start(bf16[8,1,27,8,192]{4,3,2,1,0:T(8,128)(2,1)} %bitcast.238), calls=%async_computation | async-start | bytes 1769472 | tf_op jit(solution)/shard_map/all_to_all | solution.py:781
  27.4 27.6 %collective-permute-done = bf16[1,16,8,1600]{3,2,1,0:T(8,128)(2,1)S(1)} collective-permute-done((bf16[1,16,8,1600]{3,2,1,0:T(8,128)(2,1)S(1)}, bf16[1,16,8,1600]{3,2,1,0:T(8,128)(2,1)S(1)}, u32[]{:S(2)}, u32[]{:S(2)}) %collective-permute-start) | collective-permute-done | bytes 409632 | tf_op jit(solution)/shard_map/ppermute | solution.py:679
  59.4 6.2 %collective-permute-start.2 = (bf16[1,16,8,1600]{3,2,1,0:T(8,128)(2,1)}, bf16[1,16,8,1600]{3,2,1,0:T(8,128)(2,1)S(1)}, u32[]{:S(2)}, u32[]{:S(2)}) collective-permute-start(bf16[1,16,8,1600]{3,2,1,0:T(8,128)(2,1)} %bitcast.268), channel_id=1, source_target_pairs={{0,2},{2,4},{4,6},{6,7},{7,5},{5,3},{3,1},{1,0},{8,10},{10,12},{12... | collective-permute-start | bytes 1228808 | tf_op jit(solution)/shard_map/ppermute | solution.py:679
  69.2 9.7 %collective-permute-done.2 = bf16[1,16,8,1600]{3,2,1,0:T(8,128)(2,1)S(1)} collective-permute-done((bf16[1,16,8,1600]{3,2,1,0:T(8,128)(2,1)}, bf16[1,16,8,1600]{3,2,1,0:T(8,128)(2,1)S(1)}, u32[]{:S(2)}, u32[]{:S(2)}) %collective-permute-start.2) | collective-permute-done | bytes 409632 | tf_op jit(solution)/shard_map/ppermute | solution.py:679
  78.9 6.0 %collective-permute-done.3 = bf16[1,16,8,1600]{3,2,1,0:T(8,128)(2,1)S(1)} collective-permute-done((bf16[1,16,8,1600]{3,2,1,0:T(8,128)(2,1)}, bf16[1,16,8,1600]{3,2,1,0:T(8,128)(2,1)S(1)}, u32[]{:S(2)}, u32[]{:S(2)}) %collective-permute-start.3) | collective-permute-done | bytes 409632 | tf_op jit(solution)/shard_map/ppermute | solution.py:679
  88.0 10.4 %collective-permute-done.5 = bf16[1,16,8,1600]{3,2,1,0:T(8,128)(2,1)S(1)} collective-permute-done((bf16[1,16,8,1600]{3,2,1,0:T(8,128)(2,1)}, bf16[1,16,8,1600]{3,2,1,0:T(8,128)(2,1)S(1)}, u32[]{:S(2)}, u32[]{:S(2)}) %collective-permute-start.5) | collective-permute-done | bytes 409632 | tf_op jit(solution)/shard_map/ppermute | solution.py:679
  126.5 11.7 %project.1 = (bf16[1024,1600]{1,0:T(8,128)(2,1)}, bf16[1024,768]{1,0:T(8,128)(2,1)}, bf16[1024,1600]{1,0:T(8,128)(2,1)}) custom-call(s32[9]{0:T(128)} %pad_add_fusion.refs_0_, f32[1,1600]{1,0:T(1,128)} %reshape.709.refs_1_, f32[1,1600]{1,0:T(1,128)} %reshape.710.refs_2_, f32[1,768]{1,0:T(1,128)} %dynamic-slice_convert_fusion.refs_3_, ...), custom_call_target="tpu_custom_call" | custom-call | flops 1760000000 | bytes 65536 | tf_op jit(solution)/shard_map/project/pallas_call | solution.py:50
  142.4 5.0 collective-permute-start.14
  147.7 9.9 %attention_forward.1 = (bf16[1024,256]{1,0:T(8,128)(2,1)}, f32[1024,256]{1,0:T(8,128)}, f32[2,2,1024]{2,1,0:T(2,128)}) custom-call(s32[9]{0:T(128)} %pad_add_fusion.refs_0_, bf16[1024,768]{1,0:T(8,128)(2,1)} %get-tuple-element.181.refs_1_), custom_call_target="tpu_custom_call" | custom-call | flops 2400000000 | bytes 65536 | tf_op jit(solution)/shard_map/attention_forward/pallas_call | solution.py:50
  169.4 7.2 %assemble.4.refs_1_ = bf16[1600,1600]{1,0:T(8,128)(2,1)} custom-call(s32[9]{0:T(128)} %pad_add_fusion.refs_0_, bf16[4,200,400]{2,1,0:T(8,128)(2,1)} %get-tuple-element.381.refs_1_, bf16[4,200,400]{2,1,0:T(8,128)(2,1)} %get-tuple-element.378.refs_2_, bf16[4,200,400]{2,1,0:T(8,128)(2,1)} %bitcast.274, bf16[4,200,400]{2,1,0:T(8,128)(2,1)} %bitcast.275, ...), custom_call_target="tpu_custom_call" | custom-call | flops 800000000 | bytes 65536 | tf_op jit(solution)/shard_map/assemble/pallas_call | solution.py:50
  176.6 4.9 collective-permute-done.20
  191.0 5.5 %mix.1 = (bf16[128,1600]{1,0:T(8,128)(2,1)}, f32[128,1600]{1,0:T(8,128)}, bf16[128,1600]{1,0:T(8,128)(2,1)}) custom-call(s32[9]{0:T(128)} %pad_add_fusion.refs_0_, bf16[128,1600]{1,0:T(8,128)(2,1)} %bitcast.193, bf16[1600,1600]{1,0:T(8,128)(2,1)} %get-tuple-element.192.refs_2_.refs_6_, f32[1,1600]{1,0:T(1,128)} %reshape.711.refs_3_, ...), custom_call_target="tpu_custom_call" | custom-call | flops 960000000 | bytes 65536 | tf_op jit(solution)/shard_map/mix/pallas_call | solution.py:50
  200.8 6.2 %collective-permute-done.22 = bf16[1,16,8,1600]{3,2,1,0:T(8,128)(2,1)S(1)} collective-permute-done((bf16[1,16,8,1600]{3,2,1,0:T(8,128)(2,1)}, bf16[1,16,8,1600]{3,2,1,0:T(8,128)(2,1)S(1)}, u32[]{:S(2)}, u32[]{:S(2)}) %collective-permute-start.22) | collective-permute-done | bytes 409632 | tf_op jit(solution)/shard_map/ppermute | solution.py:679
  210.7 8.0 %collective-permute-done.24 = bf16[1,16,8,1600]{3,2,1,0:T(8,128)(2,1)S(1)} collective-permute-done((bf16[1,16,8,1600]{3,2,1,0:T(8,128)(2,1)}, bf16[1,16,8,1600]{3,2,1,0:T(8,128)(2,1)S(1)}, u32[]{:S(2)}, u32[]{:S(2)}) %collective-permute-start.24) | collective-permute-done | bytes 409632 | tf_op jit(solution)/shard_map/ppermute | solution.py:679
  223.5 10.4 %collective-permute-done.28 = bf16[1,16,8,1600]{3,2,1,0:T(8,128)(2,1)S(1)} collective-permute-done((bf16[1,16,8,1600]{3,2,1,0:T(8,128)(2,1)}, bf16[1,16,8,1600]{3,2,1,0:T(8,128)(2,1)S(1)}, u32[]{:S(2)}, u32[]{:S(2)}) %collective-permute-start.28) | collective-permute-done | bytes 409632 | tf_op jit(solution)/shard_map/ppermute | solution.py:679
  237.8 5.2 assemble.5.refs_1_
  247.9 22.6 %mlp.1 = (bf16[1024,800]{1,0:T(8,128)(2,1)}, bf16[1024,800]{1,0:T(8,128)(2,1)}, f32[1,800]{1,0:T(1,128)}, bf16[8,128,1600]{2,1,0:T(8,128)(2,1)}, bf16[128,1600]{...) custom-call(s32[9]{0:T(128)} %pad_add_fusion.refs_0_, ...), custom_call_target="tpu_custom_call" | custom-call | flops 2880000000 | bytes 65536 | tf_op jit(solution)/shard_map/mlp/pallas_call | solution.py:50
  274.0 6.9 %collective-permute-done.33 = bf16[1,16,8,1600]{3,2,1,0:T(8,128)(2,1)S(1)} collective-permute-done((bf16[1,16,8,1600]{3,2,1,0:T(8,128)(2,1)}, bf16[1,16,8,1600]{3,2,1,0:T(8,128)(2,1)S(1)}, u32[]{:S(2)}, u32[]{:S(2)}) %collective-permute-start.33) | collective-permute-done | bytes 409632 | tf_op jit(solution)/shard_map/ppermute | solution.py:679
  285.9 6.9 %join.1.refs_4_ = bf16[8,128,1600]{2,1,0:T(8,128)(2,1)} custom-call(s32[9]{0:T(128)} %pad_add_fusion.refs_0_, bf16[8,128,1600]{2,1,0:T(8,128)(2,1)} %get-tuple-element.216.refs_1_, bf16[128,1600]{1,0:T(8,128)(2,1)} %get-tuple-element.213.refs_2_), custom_call_target="tpu_custom_call" | custom-call | flops 640000000 | bytes 65536 | tf_op jit(solution)/shard_map/join/pallas_call | solution.py:50
  299.5 9.7 %fc_grad.1 = (bf16[8,200,200]{2,1,0:T(8,128)(2,1)}, bf16[8,200,200]{2,1,0:T(8,128)(2,1)}, bf16[8,200,200]{2,1,0:T(8,128)(2,1)}, bf16[8,200,200]{2,1,0:T(8,128)(2,1)}) custom-call(s32[9]{0:T(128)} %pad_add_fusion.refs_0_, bf16[128,1600]{1,0:T(8,128)(2,1)} %get-tuple-element.195.refs_4_.refs_1_, bf16[128,1600]{1,0:T(8,128)(2,1)} %get-tuple-element.197.refs_5_.refs_2_, ...), custom_call_target="tpu_custom_call" | custom-call | flops 1440000000 | bytes 65536 | tf_op jit(solution)/shard_map/fc_grad/pallas_call | solution.py:50
  316.2 8.9 %out_grad.1 = (bf16[1,800,400]{2,1,0:T(8,128)(2,1)}, bf16[1,800,400]{2,1,0:T(8,128)(2,1)}, bf16[1,800,400]{2,1,0:T(8,128)(2,1)}, bf16[1,800,400]{2,1,0:T(8,128)(2,1)}) custom-call(s32[9]{0:T(128)} %pad_add_fusion.refs_0_, bf16[1024,800]{1,0:T(8,128)(2,1)} %get-tuple-element.233.refs_1_, bf16[128,1600]{1,0:T(8,128)(2,1)} %bitcast.196, ...), custom_call_target="tpu_custom_call" | custom-call | flops 1440000000 | bytes 65536 | tf_op jit(solution)/shard_map/out_grad/pallas_call | solution.py:50
  328.4 7.2 %unmix.1 = (f32[128,1600]{1,0:T(8,128)}, bf16[128,1600]{1,0:T(8,128)(2,1)}, f32[3,1600]{1,0:T(4,128)}, bf16[8,128,256]{2,1,0:T(8,128)(2,1)}) custom-call(s32[9]{0:T(128)} %pad_add_fusion.refs_0_, bf16[128,1600]{1,0:T(8,128)(2,1)} %get-tuple-element.238.refs_1_, bf16[128,1600]{1,0:T(8,128)(2,1)} %get-tuple-element.239.refs_2_, ...), custom_call_target="tpu_custom_call" | custom-call | flops 1120000000 | bytes 65536 | tf_op jit(solution)/shard_map/unmix/pallas_call | solution.py:50
  342.8 9.4 %collective-permute-done.47 = bf16[1,16,8,1600]{3,2,1,0:T(8,128)(2,1)S(1)} collective-permute-done((bf16[1,16,8,1600]{3,2,1,0:T(8,128)(2,1)}, bf16[1,16,8,1600]{3,2,1,0:T(8,128)(2,1)S(1)}, u32[]{:S(2)}, u32[]{:S(2)}) %collective-permute-start.47) | collective-permute-done | bytes 409632 | tf_op jit(solution)/shard_map/ppermute | solution.py:679
  352.2 15.1 %all-to-all-done.3 = bf16[8,1,16,8,256]{4,3,2,1,0:T(8,128)(2,1)S(1)} async-done(((bf16[8,1,16,8,256]{4,3,2,1,0:T(8,128)(2,1)}), bf16[8,1,16,8,256]{4,3,2,1,0:T(8,128)(2,1)S(1)}, u32[]{:S(2)}, u32[]{:S(2)}) %all-to-all-start.3) | async-done | bytes 524320 | tf_op jit(solution)/shard_map/all_to_all | solution.py:781
  370.1 12.1 %attention_backward.1 = (bf16[1024,768]{1,0:T(8,128)(2,1)}, f32[2,1,384]{2,1,0:T(1,128)}) custom-call(s32[9]{0:T(128)} %pad_add_fusion.refs_0_, bf16[1024,768]{1,0:T(8,128)(2,1)} %get-tuple-element.181.refs_1_, bf16[1024,256]{1,0:T(8,128)(2,1)} %bitcast.212, f32[1024,256]{1,0:T(8,128)} %get-tuple-element.251.refs_3_, f32[2,2,1024]{2,1,0:T(2,128)} %get-tuple-element.252.refs_4_), custom_call_target="tpu_custom_call" | custom-call | flops 2240000000 | bytes 65536 | tf_op jit(solution)/shard_map/attention_backward/pallas_call | solution.py:50
  387.1 8.3 %qkv_grad.1 = (bf16[8,200,192]{2,1,0:T(8,128)(2,1)}, bf16[8,200,192]{2,1,0:T(8,128)(2,1)}, bf16[8,200,192]{2,1,0:T(8,128)(2,1)}, bf16[8,200,192]{2,1,0:T(8,128)(2,1)}) custom-call(s32[9]{0:T(128)} %pad_add_fusion.refs_0_, bf16[1024,1600]{1,0:T(8,128)(2,1)} %get-tuple-element.285.refs_1_, bf16[1024,768]{1,0:T(8,128)(2,1)} %get-tuple-element.258.refs_1_.refs_2_), custom_call_target="tpu_custom_call" | custom-call | flops 1440000000 | bytes 65536 | tf_op jit(solution)/shard_map/qkv_grad/pallas_call | solution.py:50
  406.0 5.2 proj_grad.1
  411.3 10.5 %unproject.1 = (bf16[184,1600]{1,0:T(8,128)(2,1)}, bf16[184,1600]{1,0:T(8,128)(2,1)}, bf16[184,1600]{1,0:T(8,128)(2,1)}, bf16[184,1600]{1,0:T(8,128)(2,1)}, bf16...) custom-call(s32[9]{0:T(128)} %pad_add_fusion.refs_0_, ...), custom_call_target="tpu_custom_call" | custom-call | flops 1440000000 | bytes 65536 | tf_op jit(solution)/shard_map/unproject/pallas_call | solution.py:50
  421.8 10.0 %all-to-all-done.4 = bf16[8,1,25,8,200]{4,3,2,1,0:T(8,128)(2,1)S(1)} async-done(((bf16[8,1,25,8,200]{4,3,2,1,0:T(8,128)(2,1)}), bf16[8,1,25,8,200]{4,3,2,1,0:T(8,128)(2,1)S(1)}, u32[]{:S(2)}, u32[]{:S(2)}) %all-to-all-start.4) | async-done | bytes 640032 | tf_op jit(solution)/shard_map/all_to_all | solution.py:781
  445.0 6.4 %collective-permute-done.54 = bf16[1,23,8,1600]{3,2,1,0:T(8,128)(2,1)} collective-permute-done((bf16[1,23,8,1600]{3,2,1,0:T(8,128)(2,1)}, bf16[1,23,8,1600]{3,2,1,0:T(8,128)(2,1)}, u32[]{:S(2)}, u32[]{:S(2)}) %collective-permute-start.54) | collective-permute-done | bytes 588832 | tf_op jit(solution)/shard_map/ppermute | solution.py:679
  453.8 15.4 %collective-permute-done.56 = bf16[1,23,8,1600]{3,2,1,0:T(8,128)(2,1)S(1)} collective-permute-done((bf16[1,23,8,1600]{3,2,1,0:T(8,128)(2,1)S(1)}, bf16[1,23,8,1600]{3,2,1,0:T(8,128)(2,1)S(1)}, u32[]{:S(2)}, u32[]{:S(2)}) %collective-permute-start.56) | collective-permute-done | bytes 588832 | tf_op jit(solution)/shard_map/ppermute | solution.py:679
  487.2 9.3 %all-to-all-done.6 = bf16[4,1,25,8,384]{4,3,2,1,0:T(8,128)(2,1)S(1)} async-done(((bf16[4,1,25,8,384]{4,3,2,1,0:T(8,128)(2,1)}), bf16[4,1,25,8,384]{4,3,2,1,0:T(8,128)(2,1)S(1)}, u32[]{:S(2)}, u32[]{:S(2)}) %all-to-all-start.6) | async-done | bytes 614432 | tf_op jit(solution)/shard_map/all_to_all | solution.py:781
  (429 shorter events, 219.7 us)
Async XLA Ops:
  16.7 40.1 %all-to-all-start = ((bf16[8,1,27,8,192]{4,3,2,1,0:T(8,128)(2,1)}), bf16[8,1,27,8,192]{4,3,2,1,0:T(8,128)(2,1)S(1)}, u32[]{:S(2)}, u32[]{:S(2)}) async-start(bf16[8,1,27,8,192]{4,3,2,1,0:T(8,128)(2,1)} %bitcast.238), calls=%async_computation | async-start | bytes 1769472 | tf_op jit(solution)/shard_map/all_to_all | solution.py:781
  24.1 92.5 %all-gather.2.cloned.1.call-start = ((), (), s32[]{:S(2)}) async-start(), calls=%async_computation.9 | async-start | bytes 1843200 | tf_op jit(solution)/shard_map/all_gather | solution.py:894
  25.3 29.7 %collective-permute-start = (bf16[1,16,8,1600]{3,2,1,0:T(8,128)(2,1)S(1)}, bf16[1,16,8,1600]{3,2,1,0:T(8,128)(2,1)S(1)}, u32[]{:S(2)}, u32[]{:S(2)}) collective-permute-start(bf16[1,16,8,1600]{3,2,1,0:T(8,128)(2,1)S(1)} %bitcast.190), channel_id=1, source_target_pairs={{0,2},{2,4},{4,6},{6,7},{7,5},{5,3},{3,1},{1,0},{8,10},{10,12},{12... | collective-permute-start | bytes 1228808 | tf_op jit(solution)/shard_map/ppermute | solution.py:679
  27.3 29.5 %collective-permute-start.1 = (bf16[1,16,8,1600]{3,2,1,0:T(8,128)(2,1)S(1)}, bf16[1,16,8,1600]{3,2,1,0:T(8,128)(2,1)S(1)}, u32[]{:S(2)}, u32[]{:S(2)}) collective-permute-start(bf16[1,16,8,1600]{3,2,1,0:T(8,128)(2,1)S(1)} %bitcast.191), channel_id=1, source_target_pairs={{0,1},{2,0},{4,2},{6,4},{7,6},{5,7},{3,5},{1,3},{8,9},{10,8},{12,1... | collective-permute-start | bytes 1228808 | tf_op jit(solution)/shard_map/ppermute | solution.py:679
  57.9 27.1 %collective-permute-start.4 = (bf16[8,1,27,8,192]{4,3,2,0,1:T(8,128)(2,1)}, bf16[8,1,27,8,192]{4,3,2,0,1:T(8,128)(2,1)S(1)}, u32[]{:S(2)}, u32[]{:S(2)}) collective-permute-start(bf16[8,1,27,8,192]{4,3,2,0,1:T(8,128)(2,1)} %bitcast.205), channel_id=1, source_target_pairs={{0,16},{8,24},{16,0},{24,8},{1,17},{9,25},{17,1},{25,9},{2,18},{10... | collective-permute-start | bytes 1990664 | tf_op jit(solution)/shard_map/ppermute | solution.py:679
  59.4 19.5 %collective-permute-start.2 = (bf16[1,16,8,1600]{3,2,1,0:T(8,128)(2,1)}, bf16[1,16,8,1600]{3,2,1,0:T(8,128)(2,1)S(1)}, u32[]{:S(2)}, u32[]{:S(2)}) collective-permute-start(bf16[1,16,8,1600]{3,2,1,0:T(8,128)(2,1)} %bitcast.268), channel_id=1, source_target_pairs={{0,2},{2,4},{4,6},{6,7},{7,5},{5,3},{3,1},{1,0},{8,10},{10,12},{12... | collective-permute-start | bytes 1228808 | tf_op jit(solution)/shard_map/ppermute | solution.py:679
  65.6 19.4 %collective-permute-start.3 = (bf16[1,16,8,1600]{3,2,1,0:T(8,128)(2,1)}, bf16[1,16,8,1600]{3,2,1,0:T(8,128)(2,1)S(1)}, u32[]{:S(2)}, u32[]{:S(2)}) collective-permute-start(bf16[1,16,8,1600]{3,2,1,0:T(8,128)(2,1)} %bitcast.315), channel_id=1, source_target_pairs={{0,1},{2,0},{4,2},{6,4},{7,6},{5,7},{3,5},{1,3},{8,9},{10,8},{12,1... | collective-permute-start | bytes 1228808 | tf_op jit(solution)/shard_map/ppermute | solution.py:679
  65.6 22.4 %collective-permute-start.7 = (bf16[8,1,27,8,192]{4,3,2,0,1:T(8,128)(2,1)}, bf16[8,1,27,8,192]{4,3,2,0,1:T(8,128)(2,1)S(1)}, u32[]{:S(2)}, u32[]{:S(2)}) collective-permute-start(bf16[8,1,27,8,192]{4,3,2,0,1:T(8,128)(2,1)} %bitcast.206), channel_id=1, source_target_pairs={{0,8},{8,0},{16,24},{24,16},{1,9},{9,1},{17,25},{25,17},{2,10},{10... | collective-permute-start | bytes 1990664 | tf_op jit(solution)/shard_map/ppermute | solution.py:679
  112.5 28.8 %all-to-all-start.1 = ((bf16[8,1,25,8,200]{4,3,2,1,0:T(8,128)(2,1)}), bf16[8,1,25,8,200]{4,3,2,1,0:T(8,128)(2,1)S(1)}, u32[]{:S(2)}, u32[]{:S(2)}) async-start(bf16[8,1,25,8,200]{4,3,2,1,0:T(8,128)(2,1)} %bitcast.200), calls=%async_computation.1 | async-start | bytes 1638400 | tf_op jit(solution)/shard_map/all_to_all | solution.py:781
  119.9 21.4 %collective-permute-start.10 = (bf16[4,1,25,8,400]{4,3,2,0,1:T(8,128)(2,1)}, bf16[4,1,25,8,400]{4,3,2,0,1:T(8,128)(2,1)S(1)}, u32[]{:S(2)}, u32[]{:S(2)}) collective-permute-start(bf16[4,1,25,8,400]{4,3,2,0,1:T(8,128)(2,1)} %get-tuple-element.379), channel_id=1, source_target_pairs={{0,16},{8,24},{16,0},{24,8},{1,17},{9,25},{17,1},{25,9},{2,18},{10... | collective-permute-start | bytes 1920008 | tf_op jit(solution)/shard_map/ppermute | solution.py:679
  121.6 16.6 %collective-permute-start.11 = (bf16[1,16,8,1600]{3,2,1,0:T(8,128)(2,1)}, bf16[1,16,8,1600]{3,2,1,0:T(8,128)(2,1)S(1)}, u32[]{:S(2)}, u32[]{:S(2)}) collective-permute-start(bf16[1,16,8,1600]{3,2,1,0:T(8,128)(2,1)} %bitcast.265), channel_id=1, source_target_pairs={{0,2},{2,4},{4,6},{6,7},{7,5},{5,3},{3,1},{1,0},{8,10},{10,12},{12... | collective-permute-start | bytes 1228808 | tf_op jit(solution)/shard_map/ppermute | solution.py:679
  123.7 16.8 %collective-permute-start.12 = (bf16[1,16,8,1600]{3,2,1,0:T(8,128)(2,1)}, bf16[1,16,8,1600]{3,2,1,0:T(8,128)(2,1)S(1)}, u32[]{:S(2)}, u32[]{:S(2)}) collective-permute-start(bf16[1,16,8,1600]{3,2,1,0:T(8,128)(2,1)} %bitcast.266), channel_id=1, source_target_pairs={{0,1},{2,0},{4,2},{6,4},{7,6},{5,7},{3,5},{1,3},{8,9},{10,8},{12,1... | collective-permute-start | bytes 1228808 | tf_op jit(solution)/shard_map/ppermute | solution.py:679
  125.3 32.3 %collective-permute-start.13 = (bf16[4,1,25,8,400]{4,3,2,0,1:T(8,128)(2,1)}, bf16[4,1,25,8,400]{4,3,2,0,1:T(8,128)(2,1)S(1)}, u32[]{:S(2)}, u32[]{:S(2)}) collective-permute-start(bf16[4,1,25,8,400]{4,3,2,0,1:T(8,128)(2,1)} %get-tuple-element.380), channel_id=1, source_target_pairs={{0,16},{8,24},{16,0},{24,8},{1,17},{9,25},{17,1},{25,9},{2,18},{10... | collective-permute-start | bytes 1920008 | tf_op jit(solution)/shard_map/ppermute | solution.py:679
  147.7 18.5 %collective-permute-start.16 = (bf16[4,1,25,8,400]{4,3,2,0,1:T(8,128)(2,1)}, bf16[4,1,25,8,400]{4,3,2,0,1:T(8,128)(2,1)S(1)}, u32[]{:S(2)}, u32[]{:S(2)}) collective-permute-start(bf16[4,1,25,8,400]{4,3,2,0,1:T(8,128)(2,1)} %get-tuple-element.379), channel_id=1, source_target_pairs={{0,8},{8,0},{16,24},{24,16},{1,9},{9,1},{17,25},{25,17},{2,10},{10... | collective-permute-start | bytes 1920008 | tf_op jit(solution)/shard_map/ppermute | solution.py:679
  158.9 24.8 %all-to-all-start.2 = ((bf16[8,1,16,8,256]{4,3,2,1,0:T(8,128)(2,1)}), bf16[8,1,16,8,256]{4,3,2,1,0:T(8,128)(2,1)S(1)}, u32[]{:S(2)}, u32[]{:S(2)}) async-start(bf16[8,1,16,8,256]{4,3,2,1,0:T(8,128)(2,1)} %bitcast.263), calls=%async_computation.2 | async-start | bytes 1048576 | tf_op jit(solution)/shard_map/all_to_all | solution.py:781
  163.6 287.8 %reduce-scatter.2.cloned.1.call-start = ((), (), s32[]{:S(2)}) async-start(), calls=%async_computation.10 | async-start | bytes 3833856 | tf_op jit(solution)/shard_map/reduce_scatter | solution.py:1046
  164.3 17.3 %collective-permute-start.20 = (bf16[1,16,8,1600]{3,2,1,0:T(8,128)(2,1)}, bf16[1,16,8,1600]{3,2,1,0:T(8,128)(2,1)S(1)}, u32[]{:S(2)}, u32[]{:S(2)}) collective-permute-start(bf16[1,16,8,1600]{3,2,1,0:T(8,128)(2,1)} %bitcast.219), channel_id=1, source_target_pairs={{0,2},{2,4},{4,6},{6,7},{7,5},{5,3},{3,1},{1,0},{8,10},{10,12},{12... | collective-permute-start | bytes 1228808 | tf_op jit(solution)/shard_map/ppermute | solution.py:679
  167.1 16.6 %collective-permute-start.21 = (bf16[1,16,8,1600]{3,2,1,0:T(8,128)(2,1)}, bf16[1,16,8,1600]{3,2,1,0:T(8,128)(2,1)S(1)}, u32[]{:S(2)}, u32[]{:S(2)}) collective-permute-start(bf16[1,16,8,1600]{3,2,1,0:T(8,128)(2,1)} %bitcast.221), channel_id=1, source_target_pairs={{0,1},{2,0},{4,2},{6,4},{7,6},{5,7},{3,5},{1,3},{8,9},{10,8},{12,1... | collective-permute-start | bytes 1228808 | tf_op jit(solution)/shard_map/ppermute | solution.py:679
  199.3 21.1 %collective-permute-start.27 = (bf16[8,1,25,8,200]{4,3,2,0,1:T(8,128)(2,1)}, bf16[8,1,25,8,200]{4,3,2,0,1:T(8,128)(2,1)S(1)}, u32[]{:S(2)}, u32[]{:S(2)}) collective-permute-start(bf16[8,1,25,8,200]{4,3,2,0,1:T(8,128)(2,1)} %bitcast.202), channel_id=1, source_target_pairs={{0,16},{8,24},{16,0},{24,8},{1,17},{9,25},{17,1},{25,9},{2,18},{10... | collective-permute-start | bytes 1920008 | tf_op jit(solution)/shard_map/ppermute | solution.py:679
  273.4 19.4 %collective-permute-start.37 = (bf16[1,16,8,1600]{3,2,1,0:T(8,128)(2,1)}, bf16[1,16,8,1600]{3,2,1,0:T(8,128)(2,1)S(1)}, u32[]{:S(2)}, u32[]{:S(2)}) collective-permute-start(bf16[1,16,8,1600]{3,2,1,0:T(8,128)(2,1)} %bitcast.308), channel_id=1, source_target_pairs={{0,8},{8,0},{16,24},{24,16},{1,9},{9,1},{17,25},{25,17},{2,10},{10... | collective-permute-start | bytes 1228808 | tf_op jit(solution)/shard_map/ppermute | solution.py:679
  273.4 19.4 %collective-permute-start.36 = (bf16[1,16,8,1600]{3,2,1,0:T(8,128)(2,1)}, bf16[1,16,8,1600]{3,2,1,0:T(8,128)(2,1)S(1)}, u32[]{:S(2)}, u32[]{:S(2)}) collective-permute-start(bf16[1,16,8,1600]{3,2,1,0:T(8,128)(2,1)} %bitcast.328), channel_id=1, source_target_pairs={{0,1},{2,0},{4,2},{6,4},{7,6},{5,7},{3,5},{1,3},{8,9},{10,8},{12,1... | collective-permute-start | bytes 1228808 | tf_op jit(solution)/shard_map/ppermute | solution.py:679
  335.5 31.7 %all-to-all-start.3 = ((bf16[8,1,16,8,256]{4,3,2,1,0:T(8,128)(2,1)}), bf16[8,1,16,8,256]{4,3,2,1,0:T(8,128)(2,1)S(1)}, u32[]{:S(2)}, u32[]{:S(2)}) async-start(bf16[8,1,16,8,256]{4,3,2,1,0:T(8,128)(2,1)} %bitcast.264), calls=%async_computation.4 | async-start | bytes 1048576 | tf_op jit(solution)/shard_map/all_to_all | solution.py:781
  368.1 18.1 %collective-permute-start.48 = (bf16[8,1,25,8,200]{4,3,2,0,1:T(8,128)(2,1)}, bf16[8,1,25,8,200]{4,3,2,0,1:T(8,128)(2,1)S(1)}, u32[]{:S(2)}, u32[]{:S(2)}) collective-permute-start(bf16[8,1,25,8,200]{4,3,2,0,1:T(8,128)(2,1)} %bitcast.251), channel_id=1, source_target_pairs={{0,16},{8,24},{16,0},{24,8},{1,17},{9,25},{17,1},{25,9},{2,18},{10... | collective-permute-start | bytes 1920008 | tf_op jit(solution)/shard_map/ppermute | solution.py:679
  397.1 34.6 %all-to-all-start.4 = ((bf16[8,1,25,8,200]{4,3,2,1,0:T(8,128)(2,1)}), bf16[8,1,25,8,200]{4,3,2,1,0:T(8,128)(2,1)S(1)}, u32[]{:S(2)}, u32[]{:S(2)}) async-start(bf16[8,1,25,8,200]{4,3,2,1,0:T(8,128)(2,1)} %fusion.11), calls=%async_computation.5 | async-start | bytes 1638400 | tf_op jit(solution)/shard_map/all_to_all | solution.py:781
  403.8 27.9 %collective-permute-start.53 = (bf16[8,1,25,8,192]{4,3,2,0,1:T(8,128)(2,1)S(1)}, bf16[8,1,25,8,192]{4,3,2,0,1:T(8,128)(2,1)S(1)}, u32[]{:S(2)}, u32[]{:S(2)}) collective-permute-start(bf16[8,1,25,8,192]{4,3,2,0,1:T(8,128)(2,1)S(1)} %fusion.12), channel_id=1, source_target_pairs={{0,16},{8,24},{16,0},{24,8},{1,17},{9,25},{17,1},{25,9},{2,18},{10... | collective-permute-start | bytes 1843208 | tf_op jit(solution)/shard_map/ppermute | solution.py:679
  432.9 18.5 %collective-permute-start.54 = (bf16[1,23,8,1600]{3,2,1,0:T(8,128)(2,1)}, bf16[1,23,8,1600]{3,2,1,0:T(8,128)(2,1)}, u32[]{:S(2)}, u32[]{:S(2)}) collective-permute-start(bf16[1,23,8,1600]{3,2,1,0:T(8,128)(2,1)} %bitcast.282), channel_id=1, source_target_pairs={{0,2},{2,4},{4,6},{6,7},{7,5},{5,3},{3,1},{1,0},{8,10},{10,12},{12... | collective-permute-start | bytes 1766408 | tf_op jit(solution)/shard_map/ppermute | solution.py:679
  436.7 32.6 %all-to-all-start.5 = ((bf16[8,1,25,8,192]{4,3,2,1,0:T(8,128)(2,1)}), bf16[8,1,25,8,192]{4,3,2,1,0:T(8,128)(2,1)S(1)}, u32[]{:S(2)}, u32[]{:S(2)}) async-start(bf16[8,1,25,8,192]{4,3,2,1,0:T(8,128)(2,1)} %fusion.13), calls=%async_computation.6 | async-start | bytes 1638400 | tf_op jit(solution)/shard_map/all_to_all | solution.py:781
  441.5 27.7 %collective-permute-start.57 = (bf16[1,4,25,8,400]{4,3,2,1,0:T(8,128)(2,1)}, bf16[1,4,25,8,400]{4,3,2,1,0:T(8,128)(2,1)S(1)}, u32[]{:S(2)}, u32[]{:S(2)}) collective-permute-start(bf16[1,4,25,8,400]{4,3,2,1,0:T(8,128)(2,1)} %bitcast.249), channel_id=1, source_target_pairs={{0,16},{8,24},{16,0},{24,8},{1,17},{9,25},{17,1},{25,9},{2,18},{10... | collective-permute-start | bytes 1920008 | tf_op jit(solution)/shard_map/ppermute | solution.py:679
  443.0 26.3 %collective-permute-start.56 = (bf16[1,23,8,1600]{3,2,1,0:T(8,128)(2,1)S(1)}, bf16[1,23,8,1600]{3,2,1,0:T(8,128)(2,1)S(1)}, u32[]{:S(2)}, u32[]{:S(2)}) collective-permute-start(bf16[1,23,8,1600]{3,2,1,0:T(8,128)(2,1)S(1)} %bitcast.283), channel_id=1, source_target_pairs={{0,1},{2,0},{4,2},{6,4},{7,6},{5,7},{3,5},{1,3},{8,9},{10,8},{12,1... | collective-permute-start | bytes 1766408 | tf_op jit(solution)/shard_map/ppermute | solution.py:679
  453.7 19.3 %collective-permute-start.55 = (bf16[1,23,8,1600]{3,2,1,0:T(8,128)(2,1)}, bf16[1,23,8,1600]{3,2,1,0:T(8,128)(2,1)}, u32[]{:S(2)}, u32[]{:S(2)}) collective-permute-start(bf16[1,23,8,1600]{3,2,1,0:T(8,128)(2,1)} %bitcast.288), channel_id=1, source_target_pairs={{0,2},{2,4},{4,6},{6,7},{7,5},{5,3},{3,1},{1,0},{8,10},{10,12},{12... | collective-permute-start | bytes 1766408 | tf_op jit(solution)/shard_map/ppermute | solution.py:679
  475.8 20.6 %collective-permute-start.58 = (bf16[1,23,8,1600]{3,2,1,0:T(8,128)(2,1)}, bf16[1,23,8,1600]{3,2,1,0:T(8,128)(2,1)S(1)}, u32[]{:S(2)}, u32[]{:S(2)}) collective-permute-start(bf16[1,23,8,1600]{3,2,1,0:T(8,128)(2,1)} %bitcast.327), channel_id=1, source_target_pairs={{0,2},{2,4},{4,6},{6,7},{7,5},{5,3},{3,1},{1,0},{8,10},{10,12},{12... | collective-permute-start | bytes 1766408 | tf_op jit(solution)/shard_map/ppermute | solution.py:679
  500.5 18.1 %collective-permute-start.60 = (bf16[1,23,8,1600]{3,2,1,0:T(8,128)(2,1)}, bf16[1,23,8,1600]{3,2,1,0:T(8,128)(2,1)}, u32[]{:S(2)}, u32[]{:S(2)}) collective-permute-start(bf16[1,23,8,1600]{3,2,1,0:T(8,128)(2,1)} %bitcast.284), channel_id=1, source_target_pairs={{0,2},{2,4},{4,6},{6,7},{7,5},{5,3},{3,1},{1,0},{8,10},{10,12},{12... | collective-permute-start | bytes 1766408 | tf_op jit(solution)/shard_map/ppermute | solution.py:679
  (137 other events, 818.6 us)
Sparse Core Ops, SparseCore 0:
  27.7 56.3 all-gather.1
  328.5 95.5 reduce-scatter.1

commit v5 on v4

--- a/solution.py
+++ b/solution.py
@@ -439,7 +439,7 @@
         first, second = halves
         results = jnp.concatenate([first[3], second[3]])
         return first[0] + second[0], first[1] + second[1], first[2] + second[2], results, first[4] + second[4]
-    group = min(shards, max(1, 256 // span))
+    group = min(shards, max(1, 512 // span))
     rows_at = lambda cols: pl.BlockSpec((group * span, cols), lambda g, t: (g, 0))
     anywhere = pl.BlockSpec(memory_space=pl.ANY)
     stack = pltpu.VMEM((shards, span, width), BF)

time: 549 us -> 549 us (level)
  no operation moved by 1% of the time
where the time goes in v5:
time: 549 us; the launch traced here: 540 us
  waiting for transfers between devices  194 us (35%)
  Pallas kernels  167 us (30%)
  starting transfers between devices  100 us (18%)
  local copies, waits for them, and re-layouts  48.3 us (9%)
  other arithmetic  15.5 us (3%)
  between operations  15 us (3%)
    ppermute x62, waiting for transfers between devices, permute(): return lax.ppermute(cut(value), axis, pairs).reshape(value.shape)  155 us
    pallas_call x20, Pallas kernels, call(): pl.pallas_call(body, grid_spec=pltpu.PrefetchScalarGridSpec(num_scalar_pr...  152 us
    ppermute x62, starting transfers between devices, permute(): return lax.ppermute(cut(value), axis, pairs).reshape(value.shape)  63.5 us
    all_to_all x8, waiting for transfers between devices, swap_blocks(): lax.all_to_all(cut(value), axis, 0, 0, tiled=True).reshape(value.shape)  38.5 us
    all_to_all x8, starting transfers between devices, swap_blocks(): lax.all_to_all(cut(value), axis, 0, 0, tiled=True).reshape(value.shape)  34.9 us
    unnamed x194, local copies, waits for them, and re-layouts  30.5 us
    pallas_call x36, Pallas kernels, gate(): pl.pallas_call(functools.partial(gate_kernel, count, total), in_specs=blo...  14.8 us
  transfers between devices with their start and end apart: 75, of which 36 were waited for; matrix products, arithmetic and copies ran while one was open for 5% of the time, Pallas kernels for 24%

profile of v5, /device:TPU:0, one launch (start us, length us, event | category | flops | bytes accessed | tf_op | source)
XLA Modules:
  0.0 539.8 jit_solution(6051114019969768574)
XLA Ops:
  16.7 7.4 %all-to-all-start = ((bf16[8,1,27,8,192]{4,3,2,1,0:T(8,128)(2,1)}), bf16[8,1,27,8,192]{4,3,2,1,0:T(8,128)(2,1)S(1)}, u32[]{:S(2)}, u32[]{:S(2)}) async-start(bf16[8,1,27,8,192]{4,3,2,1,0:T(8,128)(2,1)} %bitcast.238), calls=%async_computation | async-start | bytes 1769472 | tf_op jit(solution)/shard_map/all_to_all | solution.py:781
  27.4 27.6 %collective-permute-done = bf16[1,16,8,1600]{3,2,1,0:T(8,128)(2,1)S(1)} collective-permute-done((bf16[1,16,8,1600]{3,2,1,0:T(8,128)(2,1)S(1)}, bf16[1,16,8,1600]{3,2,1,0:T(8,128)(2,1)S(1)}, u32[]{:S(2)}, u32[]{:S(2)}) %collective-permute-start) | collective-permute-done | bytes 409632 | tf_op jit(solution)/shard_map/ppermute | solution.py:679
  59.4 6.2 %collective-permute-start.2 = (bf16[1,16,8,1600]{3,2,1,0:T(8,128)(2,1)}, bf16[1,16,8,1600]{3,2,1,0:T(8,128)(2,1)S(1)}, u32[]{:S(2)}, u32[]{:S(2)}) collective-permute-start(bf16[1,16,8,1600]{3,2,1,0:T(8,128)(2,1)} %bitcast.268), channel_id=1, source_target_pairs={{0,2},{2,4},{4,6},{6,7},{7,5},{5,3},{3,1},{1,0},{8,10},{10,12},{12... | collective-permute-start | bytes 1228808 | tf_op jit(solution)/shard_map/ppermute | solution.py:679
  69.2 9.7 %collective-permute-done.2 = bf16[1,16,8,1600]{3,2,1,0:T(8,128)(2,1)S(1)} collective-permute-done((bf16[1,16,8,1600]{3,2,1,0:T(8,128)(2,1)}, bf16[1,16,8,1600]{3,2,1,0:T(8,128)(2,1)S(1)}, u32[]{:S(2)}, u32[]{:S(2)}) %collective-permute-start.2) | collective-permute-done | bytes 409632 | tf_op jit(solution)/shard_map/ppermute | solution.py:679
  78.9 6.0 %collective-permute-done.3 = bf16[1,16,8,1600]{3,2,1,0:T(8,128)(2,1)S(1)} collective-permute-done((bf16[1,16,8,1600]{3,2,1,0:T(8,128)(2,1)}, bf16[1,16,8,1600]{3,2,1,0:T(8,128)(2,1)S(1)}, u32[]{:S(2)}, u32[]{:S(2)}) %collective-permute-start.3) | collective-permute-done | bytes 409632 | tf_op jit(solution)/shard_map/ppermute | solution.py:679
  88.0 10.4 %collective-permute-done.5 = bf16[1,16,8,1600]{3,2,1,0:T(8,128)(2,1)S(1)} collective-permute-done((bf16[1,16,8,1600]{3,2,1,0:T(8,128)(2,1)}, bf16[1,16,8,1600]{3,2,1,0:T(8,128)(2,1)S(1)}, u32[]{:S(2)}, u32[]{:S(2)}) %collective-permute-start.5) | collective-permute-done | bytes 409632 | tf_op jit(solution)/shard_map/ppermute | solution.py:679
  126.5 11.7 %project.1 = (bf16[1024,1600]{1,0:T(8,128)(2,1)}, bf16[1024,768]{1,0:T(8,128)(2,1)}, bf16[1024,1600]{1,0:T(8,128)(2,1)}) custom-call(s32[9]{0:T(128)} %pad_add_fusion.refs_0_, f32[1,1600]{1,0:T(1,128)} %reshape.709.refs_1_, f32[1,1600]{1,0:T(1,128)} %reshape.710.refs_2_, f32[1,768]{1,0:T(1,128)} %dynamic-slice_convert_fusion.refs_3_, ...), custom_call_target="tpu_custom_call" | custom-call | flops 1760000000 | bytes 65536 | tf_op jit(solution)/shard_map/project/pallas_call | solution.py:50
  142.4 5.0 collective-permute-start.14
  147.7 9.9 %attention_forward.1 = (bf16[1024,256]{1,0:T(8,128)(2,1)}, f32[1024,256]{1,0:T(8,128)}, f32[2,2,1024]{2,1,0:T(2,128)}) custom-call(s32[9]{0:T(128)} %pad_add_fusion.refs_0_, bf16[1024,768]{1,0:T(8,128)(2,1)} %get-tuple-element.181.refs_1_), custom_call_target="tpu_custom_call" | custom-call | flops 2400000000 | bytes 65536 | tf_op jit(solution)/shard_map/attention_forward/pallas_call | solution.py:50
  169.4 7.2 %assemble.4.refs_1_ = bf16[1600,1600]{1,0:T(8,128)(2,1)} custom-call(s32[9]{0:T(128)} %pad_add_fusion.refs_0_, bf16[4,200,400]{2,1,0:T(8,128)(2,1)} %get-tuple-element.381.refs_1_, bf16[4,200,400]{2,1,0:T(8,128)(2,1)} %get-tuple-element.378.refs_2_, bf16[4,200,400]{2,1,0:T(8,128)(2,1)} %bitcast.274, bf16[4,200,400]{2,1,0:T(8,128)(2,1)} %bitcast.275, ...), custom_call_target="tpu_custom_call" | custom-call | flops 800000000 | bytes 65536 | tf_op jit(solution)/shard_map/assemble/pallas_call | solution.py:50
  176.6 4.9 collective-permute-done.20
  191.0 5.5 %mix.1 = (bf16[128,1600]{1,0:T(8,128)(2,1)}, f32[128,1600]{1,0:T(8,128)}, bf16[128,1600]{1,0:T(8,128)(2,1)}) custom-call(s32[9]{0:T(128)} %pad_add_fusion.refs_0_, bf16[128,1600]{1,0:T(8,128)(2,1)} %bitcast.193, bf16[1600,1600]{1,0:T(8,128)(2,1)} %get-tuple-element.192.refs_2_.refs_6_, f32[1,1600]{1,0:T(1,128)} %reshape.711.refs_3_, ...), custom_call_target="tpu_custom_call" | custom-call | flops 960000000 | bytes 65536 | tf_op jit(solution)/shard_map/mix/pallas_call | solution.py:50
  200.8 6.2 %collective-permute-done.22 = bf16[1,16,8,1600]{3,2,1,0:T(8,128)(2,1)S(1)} collective-permute-done((bf16[1,16,8,1600]{3,2,1,0:T(8,128)(2,1)}, bf16[1,16,8,1600]{3,2,1,0:T(8,128)(2,1)S(1)}, u32[]{:S(2)}, u32[]{:S(2)}) %collective-permute-start.22) | collective-permute-done | bytes 409632 | tf_op jit(solution)/shard_map/ppermute | solution.py:679
  210.7 8.0 %collective-permute-done.24 = bf16[1,16,8,1600]{3,2,1,0:T(8,128)(2,1)S(1)} collective-permute-done((bf16[1,16,8,1600]{3,2,1,0:T(8,128)(2,1)}, bf16[1,16,8,1600]{3,2,1,0:T(8,128)(2,1)S(1)}, u32[]{:S(2)}, u32[]{:S(2)}) %collective-permute-start.24) | collective-permute-done | bytes 409632 | tf_op jit(solution)/shard_map/ppermute | solution.py:679
  223.5 10.4 %collective-permute-done.28 = bf16[1,16,8,1600]{3,2,1,0:T(8,128)(2,1)S(1)} collective-permute-done((bf16[1,16,8,1600]{3,2,1,0:T(8,128)(2,1)}, bf16[1,16,8,1600]{3,2,1,0:T(8,128)(2,1)S(1)}, u32[]{:S(2)}, u32[]{:S(2)}) %collective-permute-start.28) | collective-permute-done | bytes 409632 | tf_op jit(solution)/shard_map/ppermute | solution.py:679
  237.8 5.2 assemble.5.refs_1_
  247.9 22.6 %mlp.1 = (bf16[1024,800]{1,0:T(8,128)(2,1)}, bf16[1024,800]{1,0:T(8,128)(2,1)}, f32[1,800]{1,0:T(1,128)}, bf16[8,128,1600]{2,1,0:T(8,128)(2,1)}, bf16[128,1600]{...) custom-call(s32[9]{0:T(128)} %pad_add_fusion.refs_0_, ...), custom_call_target="tpu_custom_call" | custom-call | flops 2880000000 | bytes 65536 | tf_op jit(solution)/shard_map/mlp/pallas_call | solution.py:50
  274.2 6.9 %collective-permute-done.33 = bf16[1,16,8,1600]{3,2,1,0:T(8,128)(2,1)S(1)} collective-permute-done((bf16[1,16,8,1600]{3,2,1,0:T(8,128)(2,1)}, bf16[1,16,8,1600]{3,2,1,0:T(8,128)(2,1)S(1)}, u32[]{:S(2)}, u32[]{:S(2)}) %collective-permute-start.33) | collective-permute-done | bytes 409632 | tf_op jit(solution)/shard_map/ppermute | solution.py:679
  286.1 6.9 %join.1.refs_4_ = bf16[8,128,1600]{2,1,0:T(8,128)(2,1)} custom-call(s32[9]{0:T(128)} %pad_add_fusion.refs_0_, bf16[8,128,1600]{2,1,0:T(8,128)(2,1)} %get-tuple-element.216.refs_1_, bf16[128,1600]{1,0:T(8,128)(2,1)} %get-tuple-element.213.refs_2_), custom_call_target="tpu_custom_call" | custom-call | flops 640000000 | bytes 65536 | tf_op jit(solution)/shard_map/join/pallas_call | solution.py:50
  299.7 9.7 %fc_grad.1 = (bf16[8,200,200]{2,1,0:T(8,128)(2,1)}, bf16[8,200,200]{2,1,0:T(8,128)(2,1)}, bf16[8,200,200]{2,1,0:T(8,128)(2,1)}, bf16[8,200,200]{2,1,0:T(8,128)(2,1)}) custom-call(s32[9]{0:T(128)} %pad_add_fusion.refs_0_, bf16[128,1600]{1,0:T(8,128)(2,1)} %get-tuple-element.195.refs_4_.refs_1_, bf16[128,1600]{1,0:T(8,128)(2,1)} %get-tuple-element.197.refs_5_.refs_2_, ...), custom_call_target="tpu_custom_call" | custom-call | flops 1440000000 | bytes 65536 | tf_op jit(solution)/shard_map/fc_grad/pallas_call | solution.py:50
  316.2 8.9 %out_grad.1 = (bf16[1,800,400]{2,1,0:T(8,128)(2,1)}, bf16[1,800,400]{2,1,0:T(8,128)(2,1)}, bf16[1,800,400]{2,1,0:T(8,128)(2,1)}, bf16[1,800,400]{2,1,0:T(8,128)(2,1)}) custom-call(s32[9]{0:T(128)} %pad_add_fusion.refs_0_, bf16[1024,800]{1,0:T(8,128)(2,1)} %get-tuple-element.233.refs_1_, bf16[128,1600]{1,0:T(8,128)(2,1)} %bitcast.196, ...), custom_call_target="tpu_custom_call" | custom-call | flops 1440000000 | bytes 65536 | tf_op jit(solution)/shard_map/out_grad/pallas_call | solution.py:50
  328.3 7.2 %unmix.1 = (f32[128,1600]{1,0:T(8,128)}, bf16[128,1600]{1,0:T(8,128)(2,1)}, f32[3,1600]{1,0:T(4,128)}, bf16[8,128,256]{2,1,0:T(8,128)(2,1)}) custom-call(s32[9]{0:T(128)} %pad_add_fusion.refs_0_, bf16[128,1600]{1,0:T(8,128)(2,1)} %get-tuple-element.238.refs_1_, bf16[128,1600]{1,0:T(8,128)(2,1)} %get-tuple-element.239.refs_2_, ...), custom_call_target="tpu_custom_call" | custom-call | flops 1120000000 | bytes 65536 | tf_op jit(solution)/shard_map/unmix/pallas_call | solution.py:50
  342.8 9.4 %collective-permute-done.47 = bf16[1,16,8,1600]{3,2,1,0:T(8,128)(2,1)S(1)} collective-permute-done((bf16[1,16,8,1600]{3,2,1,0:T(8,128)(2,1)}, bf16[1,16,8,1600]{3,2,1,0:T(8,128)(2,1)S(1)}, u32[]{:S(2)}, u32[]{:S(2)}) %collective-permute-start.47) | collective-permute-done | bytes 409632 | tf_op jit(solution)/shard_map/ppermute | solution.py:679
  352.2 15.1 %all-to-all-done.3 = bf16[8,1,16,8,256]{4,3,2,1,0:T(8,128)(2,1)S(1)} async-done(((bf16[8,1,16,8,256]{4,3,2,1,0:T(8,128)(2,1)}), bf16[8,1,16,8,256]{4,3,2,1,0:T(8,128)(2,1)S(1)}, u32[]{:S(2)}, u32[]{:S(2)}) %all-to-all-start.3) | async-done | bytes 524320 | tf_op jit(solution)/shard_map/all_to_all | solution.py:781
  370.0 12.1 %attention_backward.1 = (bf16[1024,768]{1,0:T(8,128)(2,1)}, f32[2,1,384]{2,1,0:T(1,128)}) custom-call(s32[9]{0:T(128)} %pad_add_fusion.refs_0_, bf16[1024,768]{1,0:T(8,128)(2,1)} %get-tuple-element.181.refs_1_, bf16[1024,256]{1,0:T(8,128)(2,1)} %bitcast.212, f32[1024,256]{1,0:T(8,128)} %get-tuple-element.251.refs_3_, f32[2,2,1024]{2,1,0:T(2,128)} %get-tuple-element.252.refs_4_), custom_call_target="tpu_custom_call" | custom-call | flops 2240000000 | bytes 65536 | tf_op jit(solution)/shard_map/attention_backward/pallas_call | solution.py:50
  387.0 8.4 %qkv_grad.1 = (bf16[8,200,192]{2,1,0:T(8,128)(2,1)}, bf16[8,200,192]{2,1,0:T(8,128)(2,1)}, bf16[8,200,192]{2,1,0:T(8,128)(2,1)}, bf16[8,200,192]{2,1,0:T(8,128)(2,1)}) custom-call(s32[9]{0:T(128)} %pad_add_fusion.refs_0_, bf16[1024,1600]{1,0:T(8,128)(2,1)} %get-tuple-element.285.refs_1_, bf16[1024,768]{1,0:T(8,128)(2,1)} %get-tuple-element.258.refs_1_.refs_2_), custom_call_target="tpu_custom_call" | custom-call | flops 1440000000 | bytes 65536 | tf_op jit(solution)/shard_map/qkv_grad/pallas_call | solution.py:50
  406.0 5.2 proj_grad.1
  411.2 10.5 %unproject.1 = (bf16[184,1600]{1,0:T(8,128)(2,1)}, bf16[184,1600]{1,0:T(8,128)(2,1)}, bf16[184,1600]{1,0:T(8,128)(2,1)}, bf16[184,1600]{1,0:T(8,128)(2,1)}, bf16...) custom-call(s32[9]{0:T(128)} %pad_add_fusion.refs_0_, ...), custom_call_target="tpu_custom_call" | custom-call | flops 1440000000 | bytes 65536 | tf_op jit(solution)/shard_map/unproject/pallas_call | solution.py:50
  421.7 9.8 %all-to-all-done.4 = bf16[8,1,25,8,200]{4,3,2,1,0:T(8,128)(2,1)S(1)} async-done(((bf16[8,1,25,8,200]{4,3,2,1,0:T(8,128)(2,1)}), bf16[8,1,25,8,200]{4,3,2,1,0:T(8,128)(2,1)S(1)}, u32[]{:S(2)}, u32[]{:S(2)}) %all-to-all-start.4) | async-done | bytes 640032 | tf_op jit(solution)/shard_map/all_to_all | solution.py:781
  444.8 6.4 %collective-permute-done.54 = bf16[1,23,8,1600]{3,2,1,0:T(8,128)(2,1)} collective-permute-done((bf16[1,23,8,1600]{3,2,1,0:T(8,128)(2,1)}, bf16[1,23,8,1600]{3,2,1,0:T(8,128)(2,1)}, u32[]{:S(2)}, u32[]{:S(2)}) %collective-permute-start.54) | collective-permute-done | bytes 588832 | tf_op jit(solution)/shard_map/ppermute | solution.py:679
  453.6 15.4 %collective-permute-done.56 = bf16[1,23,8,1600]{3,2,1,0:T(8,128)(2,1)S(1)} collective-permute-done((bf16[1,23,8,1600]{3,2,1,0:T(8,128)(2,1)S(1)}, bf16[1,23,8,1600]{3,2,1,0:T(8,128)(2,1)S(1)}, u32[]{:S(2)}, u32[]{:S(2)}) %collective-permute-start.56) | collective-permute-done | bytes 588832 | tf_op jit(solution)/shard_map/ppermute | solution.py:679
  486.9 9.3 %all-to-all-done.6 = bf16[4,1,25,8,384]{4,3,2,1,0:T(8,128)(2,1)S(1)} async-done(((bf16[4,1,25,8,384]{4,3,2,1,0:T(8,128)(2,1)}), bf16[4,1,25,8,384]{4,3,2,1,0:T(8,128)(2,1)S(1)}, u32[]{:S(2)}, u32[]{:S(2)}) %all-to-all-start.6) | async-done | bytes 614432 | tf_op jit(solution)/shard_map/all_to_all | solution.py:781
  (429 shorter events, 219.6 us)
Async XLA Ops:
  16.7 40.1 %all-to-all-start = ((bf16[8,1,27,8,192]{4,3,2,1,0:T(8,128)(2,1)}), bf16[8,1,27,8,192]{4,3,2,1,0:T(8,128)(2,1)S(1)}, u32[]{:S(2)}, u32[]{:S(2)}) async-start(bf16[8,1,27,8,192]{4,3,2,1,0:T(8,128)(2,1)} %bitcast.238), calls=%async_computation | async-start | bytes 1769472 | tf_op jit(solution)/shard_map/all_to_all | solution.py:781
  24.1 92.5 %all-gather.2.cloned.1.call-start = ((), (), s32[]{:S(2)}) async-start(), calls=%async_computation.9 | async-start | bytes 1843200 | tf_op jit(solution)/shard_map/all_gather | solution.py:894
  25.3 29.7 %collective-permute-start = (bf16[1,16,8,1600]{3,2,1,0:T(8,128)(2,1)S(1)}, bf16[1,16,8,1600]{3,2,1,0:T(8,128)(2,1)S(1)}, u32[]{:S(2)}, u32[]{:S(2)}) collective-permute-start(bf16[1,16,8,1600]{3,2,1,0:T(8,128)(2,1)S(1)} %bitcast.190), channel_id=1, source_target_pairs={{0,2},{2,4},{4,6},{6,7},{7,5},{5,3},{3,1},{1,0},{8,10},{10,12},{12... | collective-permute-start | bytes 1228808 | tf_op jit(solution)/shard_map/ppermute | solution.py:679
  27.3 29.5 %collective-permute-start.1 = (bf16[1,16,8,1600]{3,2,1,0:T(8,128)(2,1)S(1)}, bf16[1,16,8,1600]{3,2,1,0:T(8,128)(2,1)S(1)}, u32[]{:S(2)}, u32[]{:S(2)}) collective-permute-start(bf16[1,16,8,1600]{3,2,1,0:T(8,128)(2,1)S(1)} %bitcast.191), channel_id=1, source_target_pairs={{0,1},{2,0},{4,2},{6,4},{7,6},{5,7},{3,5},{1,3},{8,9},{10,8},{12,1... | collective-permute-start | bytes 1228808 | tf_op jit(solution)/shard_map/ppermute | solution.py:679
  57.9 27.1 %collective-permute-start.4 = (bf16[8,1,27,8,192]{4,3,2,0,1:T(8,128)(2,1)}, bf16[8,1,27,8,192]{4,3,2,0,1:T(8,128)(2,1)S(1)}, u32[]{:S(2)}, u32[]{:S(2)}) collective-permute-start(bf16[8,1,27,8,192]{4,3,2,0,1:T(8,128)(2,1)} %bitcast.205), channel_id=1, source_target_pairs={{0,16},{8,24},{16,0},{24,8},{1,17},{9,25},{17,1},{25,9},{2,18},{10... | collective-permute-start | bytes 1990664 | tf_op jit(solution)/shard_map/ppermute | solution.py:679
  59.4 19.5 %collective-permute-start.2 = (bf16[1,16,8,1600]{3,2,1,0:T(8,128)(2,1)}, bf16[1,16,8,1600]{3,2,1,0:T(8,128)(2,1)S(1)}, u32[]{:S(2)}, u32[]{:S(2)}) collective-permute-start(bf16[1,16,8,1600]{3,2,1,0:T(8,128)(2,1)} %bitcast.268), channel_id=1, source_target_pairs={{0,2},{2,4},{4,6},{6,7},{7,5},{5,3},{3,1},{1,0},{8,10},{10,12},{12... | collective-permute-start | bytes 1228808 | tf_op jit(solution)/shard_map/ppermute | solution.py:679
  65.6 19.4 %collective-permute-start.3 = (bf16[1,16,8,1600]{3,2,1,0:T(8,128)(2,1)}, bf16[1,16,8,1600]{3,2,1,0:T(8,128)(2,1)S(1)}, u32[]{:S(2)}, u32[]{:S(2)}) collective-permute-start(bf16[1,16,8,1600]{3,2,1,0:T(8,128)(2,1)} %bitcast.315), channel_id=1, source_target_pairs={{0,1},{2,0},{4,2},{6,4},{7,6},{5,7},{3,5},{1,3},{8,9},{10,8},{12,1... | collective-permute-start | bytes 1228808 | tf_op jit(solution)/shard_map/ppermute | solution.py:679
  65.6 22.4 %collective-permute-start.7 = (bf16[8,1,27,8,192]{4,3,2,0,1:T(8,128)(2,1)}, bf16[8,1,27,8,192]{4,3,2,0,1:T(8,128)(2,1)S(1)}, u32[]{:S(2)}, u32[]{:S(2)}) collective-permute-start(bf16[8,1,27,8,192]{4,3,2,0,1:T(8,128)(2,1)} %bitcast.206), channel_id=1, source_target_pairs={{0,8},{8,0},{16,24},{24,16},{1,9},{9,1},{17,25},{25,17},{2,10},{10... | collective-permute-start | bytes 1990664 | tf_op jit(solution)/shard_map/ppermute | solution.py:679
  112.5 28.8 %all-to-all-start.1 = ((bf16[8,1,25,8,200]{4,3,2,1,0:T(8,128)(2,1)}), bf16[8,1,25,8,200]{4,3,2,1,0:T(8,128)(2,1)S(1)}, u32[]{:S(2)}, u32[]{:S(2)}) async-start(bf16[8,1,25,8,200]{4,3,2,1,0:T(8,128)(2,1)} %bitcast.200), calls=%async_computation.1 | async-start | bytes 1638400 | tf_op jit(solution)/shard_map/all_to_all | solution.py:781
  119.9 21.4 %collective-permute-start.10 = (bf16[4,1,25,8,400]{4,3,2,0,1:T(8,128)(2,1)}, bf16[4,1,25,8,400]{4,3,2,0,1:T(8,128)(2,1)S(1)}, u32[]{:S(2)}, u32[]{:S(2)}) collective-permute-start(bf16[4,1,25,8,400]{4,3,2,0,1:T(8,128)(2,1)} %get-tuple-element.379), channel_id=1, source_target_pairs={{0,16},{8,24},{16,0},{24,8},{1,17},{9,25},{17,1},{25,9},{2,18},{10... | collective-permute-start | bytes 1920008 | tf_op jit(solution)/shard_map/ppermute | solution.py:679
  121.6 16.6 %collective-permute-start.11 = (bf16[1,16,8,1600]{3,2,1,0:T(8,128)(2,1)}, bf16[1,16,8,1600]{3,2,1,0:T(8,128)(2,1)S(1)}, u32[]{:S(2)}, u32[]{:S(2)}) collective-permute-start(bf16[1,16,8,1600]{3,2,1,0:T(8,128)(2,1)} %bitcast.265), channel_id=1, source_target_pairs={{0,2},{2,4},{4,6},{6,7},{7,5},{5,3},{3,1},{1,0},{8,10},{10,12},{12... | collective-permute-start | bytes 1228808 | tf_op jit(solution)/shard_map/ppermute | solution.py:679
  123.7 16.8 %collective-permute-start.12 = (bf16[1,16,8,1600]{3,2,1,0:T(8,128)(2,1)}, bf16[1,16,8,1600]{3,2,1,0:T(8,128)(2,1)S(1)}, u32[]{:S(2)}, u32[]{:S(2)}) collective-permute-start(bf16[1,16,8,1600]{3,2,1,0:T(8,128)(2,1)} %bitcast.266), channel_id=1, source_target_pairs={{0,1},{2,0},{4,2},{6,4},{7,6},{5,7},{3,5},{1,3},{8,9},{10,8},{12,1... | collective-permute-start | bytes 1228808 | tf_op jit(solution)/shard_map/ppermute | solution.py:679
  125.3 32.3 %collective-permute-start.13 = (bf16[4,1,25,8,400]{4,3,2,0,1:T(8,128)(2,1)}, bf16[4,1,25,8,400]{4,3,2,0,1:T(8,128)(2,1)S(1)}, u32[]{:S(2)}, u32[]{:S(2)}) collective-permute-start(bf16[4,1,25,8,400]{4,3,2,0,1:T(8,128)(2,1)} %get-tuple-element.380), channel_id=1, source_target_pairs={{0,16},{8,24},{16,0},{24,8},{1,17},{9,25},{17,1},{25,9},{2,18},{10... | collective-permute-start | bytes 1920008 | tf_op jit(solution)/shard_map/ppermute | solution.py:679
  147.7 18.5 %collective-permute-start.16 = (bf16[4,1,25,8,400]{4,3,2,0,1:T(8,128)(2,1)}, bf16[4,1,25,8,400]{4,3,2,0,1:T(8,128)(2,1)S(1)}, u32[]{:S(2)}, u32[]{:S(2)}) collective-permute-start(bf16[4,1,25,8,400]{4,3,2,0,1:T(8,128)(2,1)} %get-tuple-element.379), channel_id=1, source_target_pairs={{0,8},{8,0},{16,24},{24,16},{1,9},{9,1},{17,25},{25,17},{2,10},{10... | collective-permute-start | bytes 1920008 | tf_op jit(solution)/shard_map/ppermute | solution.py:679
  158.9 24.8 %all-to-all-start.2 = ((bf16[8,1,16,8,256]{4,3,2,1,0:T(8,128)(2,1)}), bf16[8,1,16,8,256]{4,3,2,1,0:T(8,128)(2,1)S(1)}, u32[]{:S(2)}, u32[]{:S(2)}) async-start(bf16[8,1,16,8,256]{4,3,2,1,0:T(8,128)(2,1)} %bitcast.263), calls=%async_computation.2 | async-start | bytes 1048576 | tf_op jit(solution)/shard_map/all_to_all | solution.py:781
  163.6 287.6 %reduce-scatter.2.cloned.1.call-start = ((), (), s32[]{:S(2)}) async-start(), calls=%async_computation.10 | async-start | bytes 3833856 | tf_op jit(solution)/shard_map/reduce_scatter | solution.py:1046
  164.3 17.3 %collective-permute-start.20 = (bf16[1,16,8,1600]{3,2,1,0:T(8,128)(2,1)}, bf16[1,16,8,1600]{3,2,1,0:T(8,128)(2,1)S(1)}, u32[]{:S(2)}, u32[]{:S(2)}) collective-permute-start(bf16[1,16,8,1600]{3,2,1,0:T(8,128)(2,1)} %bitcast.219), channel_id=1, source_target_pairs={{0,2},{2,4},{4,6},{6,7},{7,5},{5,3},{3,1},{1,0},{8,10},{10,12},{12... | collective-permute-start | bytes 1228808 | tf_op jit(solution)/shard_map/ppermute | solution.py:679
  167.1 16.6 %collective-permute-start.21 = (bf16[1,16,8,1600]{3,2,1,0:T(8,128)(2,1)}, bf16[1,16,8,1600]{3,2,1,0:T(8,128)(2,1)S(1)}, u32[]{:S(2)}, u32[]{:S(2)}) collective-permute-start(bf16[1,16,8,1600]{3,2,1,0:T(8,128)(2,1)} %bitcast.221), channel_id=1, source_target_pairs={{0,1},{2,0},{4,2},{6,4},{7,6},{5,7},{3,5},{1,3},{8,9},{10,8},{12,1... | collective-permute-start | bytes 1228808 | tf_op jit(solution)/shard_map/ppermute | solution.py:679
  199.3 21.1 %collective-permute-start.27 = (bf16[8,1,25,8,200]{4,3,2,0,1:T(8,128)(2,1)}, bf16[8,1,25,8,200]{4,3,2,0,1:T(8,128)(2,1)S(1)}, u32[]{:S(2)}, u32[]{:S(2)}) collective-permute-start(bf16[8,1,25,8,200]{4,3,2,0,1:T(8,128)(2,1)} %bitcast.202), channel_id=1, source_target_pairs={{0,16},{8,24},{16,0},{24,8},{1,17},{9,25},{17,1},{25,9},{2,18},{10... | collective-permute-start | bytes 1920008 | tf_op jit(solution)/shard_map/ppermute | solution.py:679
  273.6 19.4 %collective-permute-start.37 = (bf16[1,16,8,1600]{3,2,1,0:T(8,128)(2,1)}, bf16[1,16,8,1600]{3,2,1,0:T(8,128)(2,1)S(1)}, u32[]{:S(2)}, u32[]{:S(2)}) collective-permute-start(bf16[1,16,8,1600]{3,2,1,0:T(8,128)(2,1)} %bitcast.308), channel_id=1, source_target_pairs={{0,8},{8,0},{16,24},{24,16},{1,9},{9,1},{17,25},{25,17},{2,10},{10... | collective-permute-start | bytes 1228808 | tf_op jit(solution)/shard_map/ppermute | solution.py:679
  273.6 19.4 %collective-permute-start.36 = (bf16[1,16,8,1600]{3,2,1,0:T(8,128)(2,1)}, bf16[1,16,8,1600]{3,2,1,0:T(8,128)(2,1)S(1)}, u32[]{:S(2)}, u32[]{:S(2)}) collective-permute-start(bf16[1,16,8,1600]{3,2,1,0:T(8,128)(2,1)} %bitcast.328), channel_id=1, source_target_pairs={{0,1},{2,0},{4,2},{6,4},{7,6},{5,7},{3,5},{1,3},{8,9},{10,8},{12,1... | collective-permute-start | bytes 1228808 | tf_op jit(solution)/shard_map/ppermute | solution.py:679
  335.5 31.7 %all-to-all-start.3 = ((bf16[8,1,16,8,256]{4,3,2,1,0:T(8,128)(2,1)}), bf16[8,1,16,8,256]{4,3,2,1,0:T(8,128)(2,1)S(1)}, u32[]{:S(2)}, u32[]{:S(2)}) async-start(bf16[8,1,16,8,256]{4,3,2,1,0:T(8,128)(2,1)} %bitcast.264), calls=%async_computation.4 | async-start | bytes 1048576 | tf_op jit(solution)/shard_map/all_to_all | solution.py:781
  368.1 18.1 %collective-permute-start.48 = (bf16[8,1,25,8,200]{4,3,2,0,1:T(8,128)(2,1)}, bf16[8,1,25,8,200]{4,3,2,0,1:T(8,128)(2,1)S(1)}, u32[]{:S(2)}, u32[]{:S(2)}) collective-permute-start(bf16[8,1,25,8,200]{4,3,2,0,1:T(8,128)(2,1)} %bitcast.251), channel_id=1, source_target_pairs={{0,16},{8,24},{16,0},{24,8},{1,17},{9,25},{17,1},{25,9},{2,18},{10... | collective-permute-start | bytes 1920008 | tf_op jit(solution)/shard_map/ppermute | solution.py:679
  397.1 34.4 %all-to-all-start.4 = ((bf16[8,1,25,8,200]{4,3,2,1,0:T(8,128)(2,1)}), bf16[8,1,25,8,200]{4,3,2,1,0:T(8,128)(2,1)S(1)}, u32[]{:S(2)}, u32[]{:S(2)}) async-start(bf16[8,1,25,8,200]{4,3,2,1,0:T(8,128)(2,1)} %fusion.11), calls=%async_computation.5 | async-start | bytes 1638400 | tf_op jit(solution)/shard_map/all_to_all | solution.py:781
  403.8 27.7 %collective-permute-start.53 = (bf16[8,1,25,8,192]{4,3,2,0,1:T(8,128)(2,1)S(1)}, bf16[8,1,25,8,192]{4,3,2,0,1:T(8,128)(2,1)S(1)}, u32[]{:S(2)}, u32[]{:S(2)}) collective-permute-start(bf16[8,1,25,8,192]{4,3,2,0,1:T(8,128)(2,1)S(1)} %fusion.12), channel_id=1, source_target_pairs={{0,16},{8,24},{16,0},{24,8},{1,17},{9,25},{17,1},{25,9},{2,18},{10... | collective-permute-start | bytes 1843208 | tf_op jit(solution)/shard_map/ppermute | solution.py:679
  432.7 18.5 %collective-permute-start.54 = (bf16[1,23,8,1600]{3,2,1,0:T(8,128)(2,1)}, bf16[1,23,8,1600]{3,2,1,0:T(8,128)(2,1)}, u32[]{:S(2)}, u32[]{:S(2)}) collective-permute-start(bf16[1,23,8,1600]{3,2,1,0:T(8,128)(2,1)} %bitcast.282), channel_id=1, source_target_pairs={{0,2},{2,4},{4,6},{6,7},{7,5},{5,3},{3,1},{1,0},{8,10},{10,12},{12... | collective-permute-start | bytes 1766408 | tf_op jit(solution)/shard_map/ppermute | solution.py:679
  436.5 32.6 %all-to-all-start.5 = ((bf16[8,1,25,8,192]{4,3,2,1,0:T(8,128)(2,1)}), bf16[8,1,25,8,192]{4,3,2,1,0:T(8,128)(2,1)S(1)}, u32[]{:S(2)}, u32[]{:S(2)}) async-start(bf16[8,1,25,8,192]{4,3,2,1,0:T(8,128)(2,1)} %fusion.13), calls=%async_computation.6 | async-start | bytes 1638400 | tf_op jit(solution)/shard_map/all_to_all | solution.py:781
  441.3 27.7 %collective-permute-start.57 = (bf16[1,4,25,8,400]{4,3,2,1,0:T(8,128)(2,1)}, bf16[1,4,25,8,400]{4,3,2,1,0:T(8,128)(2,1)S(1)}, u32[]{:S(2)}, u32[]{:S(2)}) collective-permute-start(bf16[1,4,25,8,400]{4,3,2,1,0:T(8,128)(2,1)} %bitcast.249), channel_id=1, source_target_pairs={{0,16},{8,24},{16,0},{24,8},{1,17},{9,25},{17,1},{25,9},{2,18},{10... | collective-permute-start | bytes 1920008 | tf_op jit(solution)/shard_map/ppermute | solution.py:679
  442.8 26.2 %collective-permute-start.56 = (bf16[1,23,8,1600]{3,2,1,0:T(8,128)(2,1)S(1)}, bf16[1,23,8,1600]{3,2,1,0:T(8,128)(2,1)S(1)}, u32[]{:S(2)}, u32[]{:S(2)}) collective-permute-start(bf16[1,23,8,1600]{3,2,1,0:T(8,128)(2,1)S(1)} %bitcast.283), channel_id=1, source_target_pairs={{0,1},{2,0},{4,2},{6,4},{7,6},{5,7},{3,5},{1,3},{8,9},{10,8},{12,1... | collective-permute-start | bytes 1766408 | tf_op jit(solution)/shard_map/ppermute | solution.py:679
  453.5 19.3 %collective-permute-start.55 = (bf16[1,23,8,1600]{3,2,1,0:T(8,128)(2,1)}, bf16[1,23,8,1600]{3,2,1,0:T(8,128)(2,1)}, u32[]{:S(2)}, u32[]{:S(2)}) collective-permute-start(bf16[1,23,8,1600]{3,2,1,0:T(8,128)(2,1)} %bitcast.288), channel_id=1, source_target_pairs={{0,2},{2,4},{4,6},{6,7},{7,5},{5,3},{3,1},{1,0},{8,10},{10,12},{12... | collective-permute-start | bytes 1766408 | tf_op jit(solution)/shard_map/ppermute | solution.py:679
  475.6 20.6 %collective-permute-start.58 = (bf16[1,23,8,1600]{3,2,1,0:T(8,128)(2,1)}, bf16[1,23,8,1600]{3,2,1,0:T(8,128)(2,1)S(1)}, u32[]{:S(2)}, u32[]{:S(2)}) collective-permute-start(bf16[1,23,8,1600]{3,2,1,0:T(8,128)(2,1)} %bitcast.327), channel_id=1, source_target_pairs={{0,2},{2,4},{4,6},{6,7},{7,5},{5,3},{3,1},{1,0},{8,10},{10,12},{12... | collective-permute-start | bytes 1766408 | tf_op jit(solution)/shard_map/ppermute | solution.py:679
  500.3 18.2 %collective-permute-start.60 = (bf16[1,23,8,1600]{3,2,1,0:T(8,128)(2,1)}, bf16[1,23,8,1600]{3,2,1,0:T(8,128)(2,1)}, u32[]{:S(2)}, u32[]{:S(2)}) collective-permute-start(bf16[1,23,8,1600]{3,2,1,0:T(8,128)(2,1)} %bitcast.284), channel_id=1, source_target_pairs={{0,2},{2,4},{4,6},{6,7},{7,5},{5,3},{3,1},{1,0},{8,10},{10,12},{12... | collective-permute-start | bytes 1766408 | tf_op jit(solution)/shard_map/ppermute | solution.py:679
  (137 other events, 818.0 us)
Sparse Core Ops, SparseCore 0:
  27.7 56.3 all-gather.1
  328.5 94.6 reduce-scatter.1
